TPU v7x, 32 devices: a whole 2x2x4 slice. The times are simulated.
32 devices in a mesh: groups: 2 (over y), expert: 4 (over z), dp: 4 (over x, core).
Axes of the slice: x: 2, y: 2, z: 4, core: 2. Of those that a mesh axis runs over, the one named last changes fastest.
Arguments:
- tokens: bfloat16 [384, 6144], P(('groups', 'expert'), 'dp'), parts along dimension 0, may hold values from -6 to 6
- expert_ids: int32 [384, 2], P(('groups', 'expert')), parts along dimension 0, may hold values from 0 to 7, as said below
- route_weights: float32 [384, 2], P(('groups', 'expert')), parts along dimension 0, may hold values from 0.1 to 0.9
- gate_weight: bfloat16 [6144, 16384], P('dp', 'expert'), may hold values from -0.078125 to 0.078125
- up_weight: bfloat16 [6144, 16384], P('dp', 'expert'), may hold values from -0.078125 to 0.078125
- down_weight: bfloat16 [16384, 6144], P('expert', 'dp'), may hold values from -0.0625 to 0.0625
- gate_probe: bfloat16 [6144, 16384], P('dp', 'expert'), may hold values from -1 to 1, as said below
- up_probe: bfloat16 [6144, 16384], P('dp', 'expert'), may hold values from -1 to 1, as said below
Outputs:
- gate_hvp: bfloat16 [12288, 16384], P(('groups', 'dp'), 'expert'), parts along dimension 0
- up_hvp: bfloat16 [12288, 16384], P(('groups', 'dp'), 'expert'), parts along dimension 0
There are 2 independent parts, one for each index of `groups`. A program takes and returns all parts, laid end to end along the dimension named above; an argument that names none is the same for every part. Nothing has to cross between parts.
Inputs may be any that keep to these rules, and one draw needn't show every extreme that they name: `expert_ids`: A row never names one expert twice. Among the 48 rows of one index of expert, each window expert below 2 is named by at most 24 rows, and one of them is named by exactly 24 rows in every such block. `gate_probe`: every entry is +1 or -1. `up_probe`: every entry is +1 or -1.
All inputs are finite; a program needn't handle non-finite values.
Results may differ from a plain program's by a relative error of at most 0.025.
Values may be sent and summed in bfloat16 or wider, within the bound.
No kernel may reach another device: no remote copies, remote signals or barrier semaphores. Data moves between devices by JAX's collectives and lax.ppermute only.
A program may use at most 192 MiB of HBM per device.

v0:
```python
import jax
import jax.numpy as jnp
from jax import lax
from jax.sharding import PartitionSpec as P

EXPERTS = 2


def sigmoid_terms(gate_value):
    sigmoid_value = jax.nn.sigmoid(gate_value)
    active = gate_value * sigmoid_value
    slope_value = sigmoid_value + gate_value * sigmoid_value * (1.0 - sigmoid_value)
    bend_value = (
        sigmoid_value * (1.0 - sigmoid_value) * (2.0 + gate_value * (1.0 - 2.0 * sigmoid_value))
    )
    return (active, slope_value, bend_value)


def forward_hidden(gate_value, up_value, gate_tangent, up_tangent):
    active, slope_value, bend_value = sigmoid_terms(gate_value)
    hidden = (active * up_value).astype(jnp.bfloat16)
    hidden_tangent = (slope_value * gate_tangent * up_value + active * up_tangent).astype(
        jnp.bfloat16
    )
    return (hidden, hidden_tangent)


def backward_terms(gate_value, up_value, gate_tangent, up_tangent, back_value, back_tangent):
    active, slope_value, bend_value = sigmoid_terms(gate_value)
    gate_term = (
        back_tangent * up_value * slope_value
        + back_value * up_tangent * slope_value
        + back_value * up_value * bend_value * gate_tangent
    ).astype(jnp.bfloat16)
    up_term = (back_tangent * active + back_value * slope_value * gate_tangent).astype(jnp.bfloat16)
    return (gate_term, up_term)


def routing_tables(expert_ids, route_weights, capacity):
    expert_list = jnp.arange(EXPERTS, dtype=jnp.int32)
    matches = expert_ids[None, :, :] == expert_list[:, None, None]
    chosen = jnp.any(matches, axis=2)
    route_share = jnp.sum(jnp.where(matches, route_weights[None, :, :], jnp.float32(0.0)), axis=2)
    place = jnp.cumsum(chosen.astype(jnp.int32), axis=1) - 1
    slot_ids = jnp.arange(capacity, dtype=jnp.int32)
    route_table = chosen[:, None, :] & (place[:, None, :] == slot_ids[None, :, None])
    return (route_table, route_share)


def per_device(
    tokens, expert_ids, route_weights, gate_weight, up_weight, down_weight, gate_probe, up_probe
):
    tok_rows, width_dev = tokens.shape
    capacity = tok_rows // 2
    expert_ranks = lax.axis_size("expert")
    per_expert = expert_ranks // EXPERTS
    token_total = expert_ranks * tok_rows
    route_table, route_share = routing_tables(expert_ids, route_weights, capacity)
    spread = route_table.astype(jnp.float32) * route_share[:, None, :]
    token_slots = jnp.einsum(
        "ect,tf->ecf", route_table.astype(jnp.bfloat16), tokens, preferred_element_type=jnp.float32
    ).astype(jnp.bfloat16)
    received = lax.all_to_all(
        jnp.repeat(token_slots, per_expert, axis=0),
        "expert",
        split_axis=0,
        concat_axis=0,
        tiled=True,
    )
    slot_rows = received.reshape(expert_ranks * capacity, width_dev)
    gate_part = jnp.dot(slot_rows, gate_weight, preferred_element_type=jnp.float32)
    up_part = jnp.dot(slot_rows, up_weight, preferred_element_type=jnp.float32)
    gate_probe_part = jnp.dot(slot_rows, gate_probe, preferred_element_type=jnp.float32)
    up_probe_part = jnp.dot(slot_rows, up_probe, preferred_element_type=jnp.float32)
    gate_value, up_value, gate_tangent, up_tangent = (
        lax.psum(gate_part.astype(jnp.bfloat16), "dp").astype(jnp.float32),
        lax.psum(up_part.astype(jnp.bfloat16), "dp").astype(jnp.float32),
        lax.psum(gate_probe_part.astype(jnp.bfloat16), "dp").astype(jnp.float32),
        lax.psum(up_probe_part.astype(jnp.bfloat16), "dp").astype(jnp.float32),
    )
    hidden, hidden_tangent = forward_hidden(gate_value, up_value, gate_tangent, up_tangent)
    out_part = jnp.dot(hidden, down_weight, preferred_element_type=jnp.float32).astype(jnp.bfloat16)
    out_tangent = jnp.dot(hidden_tangent, down_weight, preferred_element_type=jnp.float32).astype(
        jnp.bfloat16
    )
    out_part = out_part.reshape(expert_ranks, capacity, width_dev)
    out_tangent = out_tangent.reshape(expert_ranks, capacity, width_dev)
    back_part, back_part_tangent = (
        lax.all_to_all(out_part, "expert", split_axis=0, concat_axis=0, tiled=True),
        lax.all_to_all(out_tangent, "expert", split_axis=0, concat_axis=0, tiled=True),
    )
    summed = (
        back_part.astype(jnp.float32).reshape(EXPERTS, per_expert, capacity, width_dev).sum(axis=1)
    )
    summed_tangent = (
        back_part_tangent.astype(jnp.float32)
        .reshape(EXPERTS, per_expert, capacity, width_dev)
        .sum(axis=1)
    )
    mixed = jnp.einsum("ect,ecf->tf", spread, summed, precision=lax.Precision.HIGHEST)
    mixed_tangent = jnp.einsum(
        "ect,ecf->tf", spread, summed_tangent, precision=lax.Precision.HIGHEST
    )
    cotangent = jnp.einsum(
        "ect,tf->ecf", spread, mixed / token_total, precision=lax.Precision.HIGHEST
    ).astype(jnp.bfloat16)
    cot_tangent = jnp.einsum(
        "ect,tf->ecf", spread, mixed_tangent / token_total, precision=lax.Precision.HIGHEST
    ).astype(jnp.bfloat16)
    cot_rows, cot_tangent_rows = (
        lax.all_to_all(
            jnp.repeat(cotangent, per_expert, axis=0),
            "expert",
            split_axis=0,
            concat_axis=0,
            tiled=True,
        ),
        lax.all_to_all(
            jnp.repeat(cot_tangent, per_expert, axis=0),
            "expert",
            split_axis=0,
            concat_axis=0,
            tiled=True,
        ),
    )
    cot_rows = cot_rows.reshape(expert_ranks * capacity, width_dev)
    cot_tangent_rows = cot_tangent_rows.reshape(expert_ranks * capacity, width_dev)
    contract_features = (((1,), (1,)), ((), ()))
    back_part_value = lax.dot_general(
        cot_rows, down_weight, contract_features, preferred_element_type=jnp.float32
    )
    back_part_tangent = lax.dot_general(
        cot_tangent_rows, down_weight, contract_features, preferred_element_type=jnp.float32
    )
    back_value, back_tangent = (
        lax.psum(back_part_value.astype(jnp.bfloat16), "dp").astype(jnp.float32),
        lax.psum(back_part_tangent.astype(jnp.bfloat16), "dp").astype(jnp.float32),
    )
    gate_term, up_term = backward_terms(
        gate_value, up_value, gate_tangent, up_tangent, back_value, back_tangent
    )
    contract_slots = (((0,), (0,)), ((), ()))
    gate_hvp = lax.dot_general(
        slot_rows, gate_term, contract_slots, preferred_element_type=jnp.float32
    )
    up_hvp = lax.dot_general(slot_rows, up_term, contract_slots, preferred_element_type=jnp.float32)
    return (gate_hvp.astype(jnp.bfloat16), up_hvp.astype(jnp.bfloat16))


def solution(mesh):
    return jax.shard_map(
        per_device,
        mesh=mesh,
        in_specs=(
            P(("groups", "expert"), "dp"),
            P(("groups", "expert"), None),
            P(("groups", "expert"), None),
            P("dp", "expert"),
            P("dp", "expert"),
            P("expert", "dp"),
            P("dp", "expert"),
            P("dp", "expert"),
        ),
        out_specs=(P(("groups", "dp"), "expert"), P(("groups", "dp"), "expert")),
        check_vma=False,
    )
```

profile of v0, /device:TPU:0, one launch (start us, length us, event | category | flops | bytes accessed | tf_op | source)
XLA Modules:
  0.0 247.7 jit_solution(7369054929712135758)
XLA Ops:
  8.4 15.7 %all_to_all.25 = bf16[4,24,1536]{2,1,0:T(8,128)(2,1)S(1)} all-to-all(bf16[4,24,1536]{2,1,0:T(8,128)(2,1)S(1)} %bitcast.63), channel_id=1, replica_groups=mesh['groups'=2,'expert'=4,'dp'=4] {'expert'}, dimensions={0} | all-to-all | bytes 589824 | tf_op jit(solution)/shard_map/all_to_all | solution.py:63
  24.1 7.7 %convolution_convert_fusion.4 = bf16[96,4096]{1,0:T(8,128)(2,1)} fusion(bf16[96,1536]{1,0:T(8,128)(2,1)S(1)} %bitcast.57, bf16[1536,4096]{1,0:T(8,128)(2,1)} %param.15), kind=kOutput, calls=%fused_computation.4 | convolution fusion | flops 1208352768 | bytes 13664256 | tf_op jit(solution)/shard_map/dot_general | solution.py:74
  32.5 3.0 %convolution_convert_fusion.5 = bf16[96,4096]{1,0:T(8,128)(2,1)} fusion(bf16[96,1536]{1,0:T(8,128)(2,1)S(1)} %bitcast.58, bf16[1536,4096]{1,0:T(8,128)(2,1)S(1)} %copy-done.2), kind=kOutput, calls=%fused_computation.5 | convolution fusion | flops 1208352768 | bytes 13664256 | tf_op jit(solution)/shard_map/dot_general | solution.py:72
  35.5 1.1 slice-done.2
  36.7 3.0 %convolution_convert_fusion.6 = bf16[96,4096]{1,0:T(8,128)(2,1)} fusion(bf16[96,1536]{1,0:T(8,128)(2,1)S(1)} %bitcast.59, bf16[1536,4096]{1,0:T(8,128)(2,1)S(1)} %bitcast.54), kind=kOutput, calls=%fused_computation.6 | convolution fusion | flops 1208352768 | bytes 13664256 | tf_op jit(solution)/shard_map/dot_general | solution.py:73
  39.7 0.8 slice-done.5
  40.5 3.0 %convolution_convert_fusion.7 = bf16[96,4096]{1,0:T(8,128)(2,1)} fusion(bf16[96,1536]{1,0:T(8,128)(2,1)S(1)} %bitcast.60, bf16[1536,4096]{1,0:T(8,128)(2,1)S(1)} %bitcast.56), kind=kOutput, calls=%fused_computation.7 | convolution fusion | flops 1208352768 | bytes 13664256 | tf_op jit(solution)/shard_map/dot_general | solution.py:71
  44.2 67.6 %all-reduce.7.cloned.1.call-done = (bf16[96,4096]{1,0:T(8,128)(2,1)}, bf16[96,4096]{1,0:T(8,128)(2,1)}, bf16[96,4096]{1,0:T(8,128)(2,1)}, bf16[96,4096]{1,0:T(8,128)(2,1)}) async-done(((bf16[96,4096]{1,0:T(8,128)(2,1)}, bf16[96,4096]{1,0:T(8,128)(2,1)}, bf16[96,4096]{1,0:T(8,128)(2,1)}, bf16[96,4096]{1,0:T(8,128)(2,1)}), (bf16[96,4096]{1,0:T(8,128)(2,1)}, bf16[96,4096]{1,0:T(8,128)(2,1)}, ...) | async-done | bytes 3145744 | tf_op jit(solution)/shard_map/psum | solution.py:78
  111.8 8.1 %convolution_convert_fusion.8 = bf16[96,1536]{1,0:T(8,128)(2,1)} fusion(bf16[4096,1536]{1,0:T(8,128)(2,1)} %param.13, bf16[96,4096]{1,0:T(8,128)(2,1)} %get-tuple-element.7, bf16[96,4096]{1,0:T(8,128)(2,1)} %get-tuple-element.5), kind=kOutput, calls=%fused_computation.20 | convolution fusion | flops 1211252736 | bytes 14450688 | tf_op jit(solution)/shard_map/dot_general | solution.py:82
  119.9 4.6 %all-to-all-start.3 = ((bf16[4,24,1536]{2,1,0:T(8,128)(2,1)}), bf16[4,24,1536]{2,1,0:T(8,128)(2,1)S(1)}, u32[]{:S(2)}, u32[]{:S(2)}) async-start(bf16[4,24,1536]{2,1,0:T(8,128)(2,1)} %bitcast.9), calls=%async_computation.3 | async-start | bytes 589824 | tf_op jit(solution)/shard_map/all_to_all | solution.py:89
  124.5 8.0 %convolution_convert_fusion.9 = bf16[96,1536]{1,0:T(8,128)(2,1)} fusion(bf16[4096,1536]{1,0:T(8,128)(2,1)} %param.13, bf16[96,4096]{1,0:T(8,128)(2,1)S(1)} %copy-done.7, bf16[96,4096]{1,0:T(8,128)(2,1)} %get-tuple-element.7, bf16[96,4096]{1,0:T(8,128)(2,1)S(1)} %copy-done.3, bf16[96,4096]{1,0:T(8,128)(2,1)S(1)} %copy-done.4), kind=kOutput, calls=%fused_computation.21 | convolution fusion | flops 1214398464 | bytes 16023552 | tf_op jit(solution)/shard_map/dot_general | solution.py:83
  132.5 1.5 all-to-all-done.3
  134.0 3.6 %all-to-all-start.1 = ((bf16[4,24,1536]{2,1,0:T(8,128)(2,1)}), bf16[4,24,1536]{2,1,0:T(8,128)(2,1)S(1)}, u32[]{:S(2)}, u32[]{:S(2)}) async-start(bf16[4,24,1536]{2,1,0:T(8,128)(2,1)} %bitcast.66), calls=%async_computation.1 | async-start | bytes 589824 | tf_op jit(solution)/shard_map/all_to_all | solution.py:90
  138.5 8.0 %all-to-all-done.1 = bf16[4,24,1536]{2,1,0:T(8,128)(2,1)S(1)} async-done(((bf16[4,24,1536]{2,1,0:T(8,128)(2,1)}), bf16[4,24,1536]{2,1,0:T(8,128)(2,1)S(1)}, u32[]{:S(2)}, u32[]{:S(2)}) %all-to-all-start.1) | async-done | bytes 294944 | tf_op jit(solution)/shard_map/all_to_all | solution.py:90
  146.5 0.7 broadcast_in_dim.32
  147.2 3.6 %all-to-all-start.4 = ((bf16[4,24,1536]{2,1,0:T(8,128)(2,1)}), bf16[4,24,1536]{2,1,0:T(8,128)(2,1)S(1)}, u32[]{:S(2)}, u32[]{:S(2)}) async-start(bf16[4,24,1536]{2,1,0:T(8,128)(2,1)} %bitcast.13), calls=%async_computation.4 | async-start | bytes 589824 | tf_op jit(solution)/shard_map/all_to_all | solution.py:111
  151.8 7.0 %all-to-all-done.4 = bf16[4,24,1536]{2,1,0:T(8,128)(2,1)S(1)} async-done(((bf16[4,24,1536]{2,1,0:T(8,128)(2,1)}), bf16[4,24,1536]{2,1,0:T(8,128)(2,1)S(1)}, u32[]{:S(2)}, u32[]{:S(2)}) %all-to-all-start.4) | async-done | bytes 294944 | tf_op jit(solution)/shard_map/all_to_all | solution.py:111
  158.8 0.7 broadcast_in_dim.31
  159.5 3.5 %all-to-all-start.2 = ((bf16[4,24,1536]{2,1,0:T(8,128)(2,1)}), bf16[4,24,1536]{2,1,0:T(8,128)(2,1)S(1)}, u32[]{:S(2)}, u32[]{:S(2)}) async-start(bf16[4,24,1536]{2,1,0:T(8,128)(2,1)} %bitcast.7), calls=%async_computation.2 | async-start | bytes 589824 | tf_op jit(solution)/shard_map/all_to_all | solution.py:118
  163.0 9.3 %convolution_convert_fusion.2 = bf16[96,4096]{1,0:T(8,128)(2,1)} fusion(bf16[96,1536]{1,0:T(8,128)(2,1)S(1)} %bitcast.64, bf16[4096,1536]{1,0:T(8,128)(2,1)} %param.13), kind=kOutput, calls=%fused_computation.2 | convolution fusion | flops 1208352768 | bytes 13664256 | tf_op jit(solution)/shard_map/dot_general | solution.py:129
  172.4 9.3 %convolution_convert_fusion.3 = bf16[96,4096]{1,0:T(8,128)(2,1)} fusion(bf16[96,1536]{1,0:T(8,128)(2,1)S(1)} %bitcast.65, bf16[4096,1536]{1,0:T(8,128)(2,1)} %param.13), kind=kOutput, calls=%fused_computation.3 | convolution fusion | flops 1208352768 | bytes 13664256 | tf_op jit(solution)/shard_map/dot_general | solution.py:132
  181.7 43.9 %all-reduce.5.cloned.1.call-done = (bf16[96,4096]{1,0:T(8,128)(2,1)}, bf16[96,4096]{1,0:T(8,128)(2,1)}) async-done(((bf16[96,4096]{1,0:T(8,128)(2,1)}, bf16[96,4096]{1,0:T(8,128)(2,1)}), (bf16[96,4096]{1,0:T(8,128)(2,1)}, bf16[96,4096]{1,0:T(8,128)(2,1)})) %all-reduce.5.cloned.1.call-update) | async-done | bytes 1572880 | tf_op jit(solution)/shard_map/psum | solution.py:136
  225.7 8.5 %convolution_convert_fusion.1 = bf16[1536,4096]{1,0:T(8,128)(2,1)} fusion(bf16[96,1536]{1,0:T(8,128)(2,1)S(1)} %bitcast.61, bf16[96,4096]{1,0:T(8,128)(2,1)S(1)} %copy-done.3, bf16[96,4096]{1,0:T(8,128)(2,1)S(1)} %copy-done.4, bf16[96,4096]{1,0:T(8,128)(2,1)S(1)} %copy-done.7, bf16[96,4096]{1,0:T(8,128)(2,1)} %get-tuple-element.2, ...), kind=kOutput, calls=%fused_computation.1 | convolution fusion | flops 1225261056 | bytes 17596416 | tf_op jit(solution)/shard_map/dot_general | solution.py:143
  234.2 6.7 %convolution_convert_fusion = bf16[1536,4096]{1,0:T(8,128)(2,1)} fusion(bf16[96,1536]{1,0:T(8,128)(2,1)S(1)} %bitcast.62, bf16[96,4096]{1,0:T(8,128)(2,1)S(1)} %copy-done.6, bf16[96,4096]{1,0:T(8,128)(2,1)S(1)} %copy-done.3, bf16[96,4096]{1,0:T(8,128)(2,1)S(1)} %copy-done.5, bf16[96,4096]{1,0:T(8,128)(2,1)S(1)} %copy-done.4), kind=kOutput, calls=%fused_computation | convolution fusion | flops 1220542464 | bytes 16023552 | tf_op jit(solution)/shard_map/dot_general | solution.py:146
  (50 shorter events, 4.5 us)
Async XLA Ops:
  7.2 1.0 copy-start
  7.2 104.6 %all-reduce.7.cloned.1.call-start = ((), (), s32[]{:S(2)}) async-start(), calls=%async_computation.6 | async-start | bytes 6291456 | tf_op jit(solution)/shard_map/psum | solution.py:78
  24.1 8.4 %copy-start.2 = (bf16[1536,4096]{1,0:T(8,128)(2,1)S(1)}, bf16[1536,4096]{1,0:T(8,128)(2,1)}, u32[]{:S(2)}) copy-start(bf16[1536,4096]{1,0:T(8,128)(2,1)} %param.12) | copy-start | bytes 37748740
  24.1 11.4 %slice-start = ((s8[12582912]{0:T(1024)(128)(4,1)}), s8[4194304]{0:T(1024)(128)(4,1)S(1)}, s32[]{:S(2)}) async-start(s8[12582912]{0:T(1024)(128)(4,1)} %bitcast.53), calls=%async_computation.7 | async-start | bytes 8388608
  24.1 11.4 %slice-start.1 = ((s8[12582912]{0:T(1024)(128)(4,1)}), s8[4194304]{0:T(1024)(128)(4,1)S(1)}, s32[]{:S(2)}) async-start(s8[12582912]{0:T(1024)(128)(4,1)} %bitcast.53), calls=%async_computation.8 | async-start | bytes 8388608
  32.5 4.1 %slice-start.2 = ((s8[12582912]{0:T(1024)(128)(4,1)}), s8[4194304]{0:T(1024)(128)(4,1)S(1)}, s32[]{:S(2)}) async-start(s8[12582912]{0:T(1024)(128)(4,1)} %bitcast.53), calls=%async_computation.9 | async-start | bytes 8388608
  32.5 7.1 %slice-start.3 = ((s8[12582912]{0:T(1024)(128)(4,1)}), s8[4194304]{0:T(1024)(128)(4,1)S(1)}, s32[]{:S(2)}) async-start(s8[12582912]{0:T(1024)(128)(4,1)} %bitcast.55), calls=%async_computation.10 | async-start | bytes 8388608
  32.5 7.1 %slice-start.4 = ((s8[12582912]{0:T(1024)(128)(4,1)}), s8[4194304]{0:T(1024)(128)(4,1)S(1)}, s32[]{:S(2)}) async-start(s8[12582912]{0:T(1024)(128)(4,1)} %bitcast.55), calls=%async_computation.11 | async-start | bytes 8388608
  36.6 3.9 %slice-start.5 = ((s8[12582912]{0:T(1024)(128)(4,1)}), s8[4194304]{0:T(1024)(128)(4,1)S(1)}, s32[]{:S(2)}) async-start(s8[12582912]{0:T(1024)(128)(4,1)} %bitcast.55), calls=%async_computation.12 | async-start | bytes 8388608
  43.5 0.7 copy-start.8
  43.5 0.7 copy-start.9
  111.8 12.7 %copy-start.3 = (bf16[96,4096]{1,0:T(8,128)(2,1)S(1)}, bf16[96,4096]{1,0:T(8,128)(2,1)}, u32[]{:S(2)}) copy-start(bf16[96,4096]{1,0:T(8,128)(2,1)} %get-tuple-element.4) | copy-start | bytes 2359300
  111.8 12.7 %copy-start.4 = (bf16[96,4096]{1,0:T(8,128)(2,1)S(1)}, bf16[96,4096]{1,0:T(8,128)(2,1)}, u32[]{:S(2)}) copy-start(bf16[96,4096]{1,0:T(8,128)(2,1)} %get-tuple-element.5) | copy-start | bytes 2359300
  111.8 12.7 %copy-start.7 = (bf16[96,4096]{1,0:T(8,128)(2,1)S(1)}, bf16[96,4096]{1,0:T(8,128)(2,1)}, u32[]{:S(2)}) copy-start(bf16[96,4096]{1,0:T(8,128)(2,1)} %get-tuple-element.6) | copy-start | bytes 2359300
  119.9 14.1 %all-to-all-start.3 = ((bf16[4,24,1536]{2,1,0:T(8,128)(2,1)}), bf16[4,24,1536]{2,1,0:T(8,128)(2,1)S(1)}, u32[]{:S(2)}, u32[]{:S(2)}) async-start(bf16[4,24,1536]{2,1,0:T(8,128)(2,1)} %bitcast.9), calls=%async_computation.3 | async-start | bytes 589824 | tf_op jit(solution)/shard_map/all_to_all | solution.py:89
  134.0 12.5 %all-to-all-start.1 = ((bf16[4,24,1536]{2,1,0:T(8,128)(2,1)}), bf16[4,24,1536]{2,1,0:T(8,128)(2,1)S(1)}, u32[]{:S(2)}, u32[]{:S(2)}) async-start(bf16[4,24,1536]{2,1,0:T(8,128)(2,1)} %bitcast.66), calls=%async_computation.1 | async-start | bytes 589824 | tf_op jit(solution)/shard_map/all_to_all | solution.py:90
  147.2 11.5 %all-to-all-start.4 = ((bf16[4,24,1536]{2,1,0:T(8,128)(2,1)}), bf16[4,24,1536]{2,1,0:T(8,128)(2,1)S(1)}, u32[]{:S(2)}, u32[]{:S(2)}) async-start(bf16[4,24,1536]{2,1,0:T(8,128)(2,1)} %bitcast.13), calls=%async_computation.4 | async-start | bytes 589824 | tf_op jit(solution)/shard_map/all_to_all | solution.py:111
  159.5 12.9 %all-to-all-start.2 = ((bf16[4,24,1536]{2,1,0:T(8,128)(2,1)}), bf16[4,24,1536]{2,1,0:T(8,128)(2,1)S(1)}, u32[]{:S(2)}, u32[]{:S(2)}) async-start(bf16[4,24,1536]{2,1,0:T(8,128)(2,1)} %bitcast.7), calls=%async_computation.2 | async-start | bytes 589824 | tf_op jit(solution)/shard_map/all_to_all | solution.py:118
  163.0 62.7 %all-reduce.5.cloned.1.call-start = ((), (), s32[]{:S(2)}) async-start(), calls=%async_computation.5 | async-start | bytes 3145728 | tf_op jit(solution)/shard_map/psum | solution.py:136
  225.7 8.5 %copy-start.5 = (bf16[96,4096]{1,0:T(8,128)(2,1)S(1)}, bf16[96,4096]{1,0:T(8,128)(2,1)}, u32[]{:S(2)}) copy-start(bf16[96,4096]{1,0:T(8,128)(2,1)} %get-tuple-element.2) | copy-start | bytes 2359300
  225.7 8.5 %copy-start.6 = (bf16[96,4096]{1,0:T(8,128)(2,1)S(1)}, bf16[96,4096]{1,0:T(8,128)(2,1)}, u32[]{:S(2)}) copy-start(bf16[96,4096]{1,0:T(8,128)(2,1)} %get-tuple-element.3) | copy-start | bytes 2359300
  234.2 6.7 %copy-start.1 = (bf16[48,1536]{1,0:T(8,128)(2,1)S(1)}, bf16[48,1536]{1,0:T(8,128)(2,1)}, u32[]{:S(2)}) copy-start(bf16[48,1536]{1,0:T(8,128)(2,1)} %param.8) | copy-start | bytes 442372
Sparse Core Ops, SparseCore 0:
  43.7 68.0 all-reduce.6
  181.8 43.7 all-reduce.4
where the time goes:
time: 248 us
  waiting for transfers between devices  128 us (52%)
  matrix products  68.6 us (28%)
  blocking collectives  15.7 us (6%)
  starting transfers between devices  15.3 us (6%)
  between operations  14.1 us (6%)
  local copies, waits for them, and re-layouts  4.85 us (2%)
    psum x1, waiting for transfers between devices, per_device(): lax.psum(gate_probe_part.astype(jnp.bfloat16), 'dp').astype(jnp.float32)  67.6 us
    psum x1, waiting for transfers between devices, per_device(): lax.psum(back_part_value.astype(jnp.bfloat16), 'dp').astype(jnp.float32)  43.9 us
    all_to_all x1, blocking collectives, per_device(): lax.all_to_all(jnp.repeat(token_slots, per_expert, axis=0), 'expert', spl...  15.7 us
    dot_general x1, matrix products, per_device(): lax.dot_general(cot_rows, down_weight, contract_features, preferred_eleme...  9.34 us
    dot_general x1, matrix products, per_device(): lax.dot_general(cot_tangent_rows, down_weight, contract_features, preferr...  9.34 us
    dot_general x1, matrix products, per_device(): lax.dot_general(slot_rows, gate_term, contract_slots, preferred_element_t...  8.49 us
    dot_general x1, matrix products, per_device(): jnp.dot(hidden, down_weight, preferred_element_type=jnp.float32)  8.1 us
    all_to_all x1, waiting for transfers between devices, per_device(): lax.all_to_all(out_tangent, 'expert', split_axis=0, concat_axis=0, tiled=...  8.02 us
  transfers between devices with their start and end apart: 6, of which 5 were waited for; matrix products, arithmetic and copies ran while one was open for 8% of the time, Pallas kernels for 0%

commit v1 on v0

v1 whole, which is shorter than its diff:
```python
import functools

import jax
import jax.numpy as jnp
from jax import lax
from jax.experimental import pallas as pl
from jax.experimental.pallas import tpu as pltpu
from jax.sharding import PartitionSpec as P

EXPERTS = 2
BF16 = jnp.bfloat16
F32 = jnp.float32
KIB = 1024
MIB = 1024 * KIB
IN_VMEM = pl.BlockSpec(memory_space=pltpu.VMEM)
IN_SMEM = pl.BlockSpec(memory_space=pltpu.SMEM)
IN_HBM = pl.BlockSpec(memory_space=pltpu.HBM)
ANYWHERE = pl.BlockSpec(memory_space=pl.ANY)
SLOTS = 4


def swap(value, axis, mask):
    size = lax.axis_size(axis)
    return lax.ppermute(value, axis, [(i, i ^ mask) for i in range(size)])


def sub_width(width):
    return 512 if width % 512 == 0 else width


def params(limit):
    return pltpu.CompilerParams(vmem_limit_bytes=limit)


def cost(flops, size):
    return pl.CostEstimate(flops=flops, bytes_accessed=size, transcendentals=0)


def stream_kernel(count, offsets, me_ref, rows_ref, *refs):
    weights, outs, (slots_ref, sems) = refs[:count], refs[-4:-2], refs[-2:]
    quarter = outs[0].shape[2]
    slots, unused, sub = slots_ref.shape
    copies, targets = [], []
    for k in range(count):
        for out_ref, offset in zip(outs, offsets):
            base = (me_ref[0] ^ offset) * quarter
            for c in range(0, quarter, sub):
                columns = pl.ds(pl.multiple_of(base + c, sub), sub)
                slot = len(copies) % slots
                copies.append(
                    pltpu.make_async_copy(
                        weights[k].at[:, columns], slots_ref.at[slot], sems.at[slot]
                    )
                )
                targets.append(out_ref.at[k, :, c : c + sub])
    for copy in copies[:slots]:
        copy.start()
    for i, target_ref in enumerate(targets):
        copies[i].wait()
        target_ref[...] = jnp.dot(
            rows_ref[...], slots_ref[i % slots], preferred_element_type=F32
        ).astype(BF16)
        if i + slots < len(copies):
            copies[i + slots].start()


def quarter_products(me, rows, weights, offsets, after=()):
    count, (height, depth) = len(weights), rows.shape
    quarter = weights[0].shape[1] // 4
    sub = sub_width(quarter)
    slots = min(4, 2 * count * (quarter // sub))
    result = jax.ShapeDtypeStruct((count, height, quarter), BF16)
    return pl.pallas_call(
        functools.partial(stream_kernel, count, offsets),
        in_specs=[IN_SMEM, IN_VMEM] + [IN_HBM] * count + [ANYWHERE] * len(after),
        out_specs=[IN_VMEM] * 2,
        out_shape=[result] * 2,
        scratch_shapes=[pltpu.VMEM((slots, depth, sub), BF16), pltpu.SemaphoreType.DMA((slots,))],
        compiler_params=params(12 * MIB),
        cost_estimate=cost(1, 1),
    )(me, rows, *weights, *after)


def back_kernel(me_ref, rows_ref, weight_ref, *refs):
    outs, turned_ref = refs[-3:-1], refs[-1]
    quarter = outs[0].shape[2]
    sub = sub_width(quarter)
    turned_ref[...] = rows_ref[...].astype(F32).T.astype(BF16)
    for out_ref, offset in zip(outs, ((3, 1), (2, 0))):
        for k in range(2):
            base = (me_ref[0] ^ offset[k]) * quarter
            for c in range(0, quarter, sub):
                piece = weight_ref[pl.ds(pl.multiple_of(base + c, sub), sub), :]
                product = jnp.dot(piece, turned_ref[...], preferred_element_type=F32)
                out_ref[k, :, c : c + sub] = product.T.astype(BF16)


def back_products(me, rows, weight):
    height, depth = rows.shape
    quarter = weight.shape[0] // 4
    result = jax.ShapeDtypeStruct((2, height, quarter), BF16)
    return pl.pallas_call(
        back_kernel,
        in_specs=[IN_SMEM] + [IN_VMEM] * 2,
        out_specs=[IN_VMEM] * 2,
        out_shape=[result] * 2,
        scratch_shapes=[pltpu.VMEM((depth, height), BF16)],
        compiler_params=params(8 * MIB),
        cost_estimate=cost(1, 1),
    )(me, rows, weight)


def down_kernel(offsets, has_start, me_ref, first_ref, second_ref, weight_ref, *rest):
    out_ref = rest[-1]
    quarter = first_ref.shape[1]
    width = weight_ref.shape[1]
    sub = sub_width(width)
    for c in range(0, width, sub):
        total = rest[0][:, c : c + sub] if has_start else 0.0
        for rows_ref, offset in zip((first_ref, second_ref), offsets):
            base = pl.multiple_of((me_ref[0] ^ offset) * quarter, quarter)
            piece = weight_ref[pl.ds(base, quarter), c : c + sub]
            total += jnp.dot(rows_ref[...], piece, preferred_element_type=F32)
        out_ref[:, c : c + sub] = total.astype(out_ref.dtype)


def down_products(me, first, second, weight, offsets, start, out_type):
    height, quarter = first.shape
    width = weight.shape[1]
    operands = [first, second, weight] + ([] if start is None else [start])
    return pl.pallas_call(
        functools.partial(down_kernel, offsets, start is not None),
        in_specs=[IN_SMEM] + [IN_VMEM] * len(operands),
        out_specs=IN_VMEM,
        out_shape=jax.ShapeDtypeStruct((height, width), out_type),
        compiler_params=params(4 * MIB),
        cost_estimate=cost(1, 1),
    )(me, *operands)


def outer_kernel(offsets, counts, me_ref, tokens_ref, *refs):
    terms = refs[: len(offsets)]
    outs, (slots_ref, sems) = refs[-2 - counts : -2], refs[-2:]
    quarter = terms[0].shape[2]
    sub = slots_ref.shape[2]
    copies = []
    for term_ref, offset in zip(terms, offsets):
        base = (me_ref[0] ^ offset) * quarter
        for k in range(counts):
            for c in range(0, quarter, sub):
                slot = len(copies) % SLOTS
                if len(copies) >= SLOTS:
                    copies[-SLOTS].wait()
                slots_ref[slot] = jnp.dot(
                    tokens_ref[...], term_ref[k, :, c : c + sub], preferred_element_type=F32
                ).astype(BF16)
                columns = pl.ds(pl.multiple_of(base + c, sub), sub)
                copy = pltpu.make_async_copy(
                    slots_ref.at[slot], outs[k].at[:, columns], sems.at[slot]
                )
                copy.start()
                copies.append(copy)
    for copy in copies[-SLOTS:]:
        copy.wait()


def outer_products(me, tokens, terms, offsets, outputs):
    width, height = tokens.shape
    counts, unused, quarter = terms[0].shape
    sub = sub_width(quarter)
    given = [] if outputs is None else list(outputs)
    operands = [tokens, *terms]
    whole = jax.ShapeDtypeStruct((width, 4 * quarter), BF16)
    return pl.pallas_call(
        functools.partial(outer_kernel, offsets, counts),
        in_specs=[IN_SMEM] + [IN_VMEM] * len(operands) + [ANYWHERE] * len(given),
        out_specs=[ANYWHERE] * counts,
        out_shape=[whole] * counts,
        input_output_aliases={1 + len(operands) + k: k for k in range(len(given))},
        scratch_shapes=[
            pltpu.VMEM((SLOTS, width, sub), BF16),
            pltpu.SemaphoreType.DMA((SLOTS,)),
        ],
        compiler_params=params(14 * MIB),
        cost_estimate=cost(
            2 * counts * len(terms) * height * width * quarter,
            2 * counts * len(terms) * width * quarter,
        ),
    )(me, *operands, *given)


def turn_kernel(rows_ref, out_ref):
    out_ref[...] = rows_ref[...].astype(F32).T.astype(BF16)


def turn(rows):
    return pl.pallas_call(
        turn_kernel,
        in_specs=[IN_VMEM],
        out_specs=IN_VMEM,
        out_shape=jax.ShapeDtypeStruct(rows.shape[::-1], rows.dtype),
        cost_estimate=cost(1, 1),
    )(rows)


def fence_kernel(value_ref, *refs):
    refs[-1][...] = value_ref[...]


def fence(value, *after):
    return pl.pallas_call(
        fence_kernel,
        in_specs=[IN_VMEM] + [ANYWHERE] * len(after),
        out_specs=IN_VMEM,
        out_shape=jax.ShapeDtypeStruct(value.shape, value.dtype),
        cost_estimate=cost(1, 1),
    )(value, *after)


def near_sum(keep, got):
    return keep.astype(F32) + got.astype(F32)


def exchange(pieces):
    ranks = lax.axis_size("expert")
    if ranks <= 4:
        return [pieces[0]] + [swap(pieces[i], "expert", i) for i in range(1, ranks)]
    order = lax.axis_index("expert") ^ jnp.arange(ranks)
    stacked = jnp.take(jnp.stack(pieces), order, axis=0)
    moved = lax.all_to_all(stacked, "expert", split_axis=0, concat_axis=0, tiled=True)
    moved = jnp.take(moved, order, axis=0)
    return [moved[i] for i in range(ranks)]


def routing_tables(expert_ids, route_weights, expert_list, capacity):
    matches = expert_ids[None, :, :] == expert_list[:, None, None]
    chosen = jnp.any(matches, axis=2)
    route_share = jnp.sum(jnp.where(matches, route_weights[None, :, :], F32(0.0)), axis=2)
    place = jnp.cumsum(chosen.astype(jnp.int32), axis=1) - 1
    slot_ids = jnp.arange(capacity, dtype=jnp.int32)
    route_table = chosen[:, None, :] & (place[:, None, :] == slot_ids[None, :, None])
    return route_table, route_share


def per_device(
    tokens, expert_ids, route_weights, gate_weight, up_weight, down_weight, gate_probe, up_probe
):
    tok_rows, width_dev = tokens.shape
    capacity = tok_rows // 2
    ranks = lax.axis_size("expert")
    per_expert = ranks // EXPERTS
    token_total = ranks * tok_rows
    me = lax.axis_index("dp").astype(jnp.int32).reshape(1)
    mine = lax.axis_index("expert") // per_expert
    expert_list = jnp.stack([mine, 1 - mine]).astype(expert_ids.dtype)

    route_table, route_share = routing_tables(expert_ids, route_weights, expert_list, capacity)
    spread = route_table.astype(F32) * route_share[:, None, :]
    slots = jnp.einsum(
        "ect,tf->ecf", route_table.astype(BF16), tokens, preferred_element_type=F32
    ).astype(BF16)
    slot_rows = jnp.concatenate(exchange([slots[i // per_expert] for i in range(ranks)]), axis=0)

    def far_half(weight, after):
        send, keep = quarter_products(me, slot_rows, [weight], (3, 2), after)
        far = near_sum(keep[0], swap(send, "dp", 1)[0]).astype(BF16)
        return far, swap(far, "dp", 2)

    def near_half(weights, after):
        send, keep = quarter_products(me, slot_rows, weights, (1, 0), after)
        half = send.shape[1] // 2
        got = [swap(send[:, :half], "dp", 1), swap(send[:, half:], "dp", 1)]
        return near_sum(keep, jnp.concatenate(got, axis=1))

    far_gate, gate_across = far_half(gate_weight, ())
    far_up, up_across = far_half(up_weight, ())
    far_gate_tangent, gate_tangent_across = far_half(gate_probe, [far_gate])
    far_up_tangent, up_tangent_across = far_half(up_probe, [far_up])
    near = near_half([gate_weight, up_weight], [far_gate_tangent, gate_across])
    near_tangent = near_half([gate_probe, up_probe], [far_up_tangent, up_across])
    gate_value = near[0] + gate_across.astype(F32)
    up_value = near[1] + up_across.astype(F32)
    gate_tangent = near_tangent[0] + gate_tangent_across.astype(F32)
    up_tangent = near_tangent[1] + up_tangent_across.astype(F32)

    s = jax.nn.sigmoid(gate_value)
    active = gate_value * s
    slope = s + gate_value * s * (1.0 - s)
    bend = s * (1.0 - s) * (2.0 + gate_value * (1.0 - 2.0 * s))

    def through_down(own):
        beside = swap(own, "dp", 1)
        across = swap(own, "dp", 2)
        half = down_products(me, own, beside, down_weight, (0, 1), None, F32)
        return down_products(
            me, across, swap(across, "dp", 1), down_weight, (2, 3), half, BF16
        )

    def back(rows):
        send, keep = back_products(me, rows, down_weight)
        got = swap(send, "dp", 1)
        far = near_sum(keep[0], got[0]).astype(BF16)
        return near_sum(keep[1], got[1]) + swap(far, "dp", 2).astype(F32)

    def mix(out):
        came = exchange(list(out.reshape(ranks, capacity, width_dev)))
        sums = jnp.stack(
            [
                sum(piece.astype(F32) for piece in came[e * per_expert : (e + 1) * per_expert])
                for e in range(EXPERTS)
            ]
        )
        mixed = jnp.einsum("ect,ecf->tf", spread, sums, precision=lax.Precision.HIGHEST)
        cot = jnp.einsum(
            "ect,tf->ecf", spread, mixed / token_total, precision=lax.Precision.HIGHEST
        ).astype(BF16)
        return jnp.concatenate(exchange([cot[i // per_expert] for i in range(ranks)]), axis=0)

    hidden = (active * up_value).astype(BF16)
    cot_rows = mix(through_down(hidden))
    back_value = back(cot_rows)

    hidden_tangent = (slope * gate_tangent * up_value + active * up_tangent).astype(BF16)
    cot_tangent_rows = mix(through_down(hidden_tangent))
    back_tangent = back(cot_tangent_rows)

    gate_term = (
        back_tangent * up_value * slope
        + back_value * up_tangent * slope
        + back_value * up_value * bend * gate_tangent
    ).astype(BF16)
    up_term = (back_tangent * active + back_value * slope * gate_tangent).astype(BF16)

    turned = turn(slot_rows)
    terms = jnp.stack([gate_term, up_term])
    across = swap(terms, "dp", 2)
    outputs = outer_products(me, turned, [terms, swap(terms, "dp", 1)], (0, 1), None)
    across = fence(across, *outputs)
    beyond = swap(across, "dp", 1)
    outputs = outer_products(me, turned, [across], (2,), outputs)
    outputs = outer_products(me, turned, [beyond], (3,), outputs)
    return tuple(outputs)


def solution(mesh):
    return jax.shard_map(
        per_device,
        mesh=mesh,
        in_specs=(
            P(("groups", "expert"), "dp"),
            P(("groups", "expert"), None),
            P(("groups", "expert"), None),
            P("dp", "expert"),
            P("dp", "expert"),
            P("expert", "dp"),
            P("dp", "expert"),
            P("dp", "expert"),
        ),
        out_specs=(P(("groups", "dp"), "expert"), P(("groups", "dp"), "expert")),
        check_vma=False,
    )
```

time: 248 us -> 142 us (0.57)
  waiting for transfers between devices: 128 us -> 43.3 us
  matrix products: 68.6 us -> 1.84 us
  Pallas kernels: 0 us -> 47.2 us
  starting transfers between devices: 15.3 us -> 34.3 us
  blocking collectives: 15.7 us -> 0 us
  between operations: 14.1 us -> 1.48 us
  local copies, waits for them, and re-layouts: 4.85 us -> 9.7 us
    psum x2 -> x0, waiting for transfers between devices: 112 us -> none  [the longest x1 67.6 us: per_device(): lax.psum(gate_probe_part.astype(jnp.bfloat16), 'dp').astype(jnp.float32)]
    dot_general x15 -> x5, matrix products: 68.6 us -> 1.84 us  [the longest x2 0.89 us: mix(): jnp.einsum('ect,ecf->tf', spread, sums, precision=lax.Precision.HIGHEST)]
    pallas_call x0 -> x17, Pallas kernels: none -> 47.2 us  [the longest x6 19.8 us: quarter_products(): pl.pallas_call(functools.partial(stream_kernel, count, offsets), in_specs...]
    ppermute x0 -> x40, waiting for transfers between devices: none -> 43.3 us  [swap(): return lax.ppermute(value, axis, [(i, i ^ mask) for i in range(size)])]
    ppermute x0 -> x40, starting transfers between devices: none -> 34.3 us  [swap(): return lax.ppermute(value, axis, [(i, i ^ mask) for i in range(size)])]
    all_to_all x4 -> x0, waiting for transfers between devices: 16.5 us -> none  [the longest x1 8.02 us: per_device(): lax.all_to_all(out_tangent, 'expert', split_axis=0, concat_axis=0, tiled=...]
    all_to_all x1 -> x0, blocking collectives: 15.7 us -> none  [per_device(): lax.all_to_all(jnp.repeat(token_slots, per_expert, axis=0), 'expert', spl...]
    all_to_all x4 -> x0, starting transfers between devices: 15.3 us -> none  [the longest x1 4.59 us: per_device(): lax.all_to_all(out_part, 'expert', split_axis=0, concat_axis=0, tiled=True)]
  transfers between devices with their start and end apart: 6 -> 40, of which waited for: 5 -> 15; matrix products, arithmetic and copies ran while one was open for 8% -> 2% of each run, Pallas kernels for 0% -> 28%
where the time goes in v1:
time: 142 us; the launch traced here: 141 us
  Pallas kernels  47.2 us (33%)
  waiting for transfers between devices  43.3 us (30%)
  starting transfers between devices  34.3 us (24%)
  local copies, waits for them, and re-layouts  9.7 us (7%)
  other arithmetic  3.42 us (2%)
  matrix products  1.84 us (1%)
  between operations  1.48 us (1%)
    ppermute x40, waiting for transfers between devices, swap(): return lax.ppermute(value, axis, [(i, i ^ mask) for i in range(size)])  43.3 us
    ppermute x40, starting transfers between devices, swap(): return lax.ppermute(value, axis, [(i, i ^ mask) for i in range(size)])  34.3 us
    pallas_call x6, Pallas kernels, quarter_products(): pl.pallas_call(functools.partial(stream_kernel, count, offsets), in_specs...  19.8 us
    pallas_call x3, Pallas kernels, outer_products(): pl.pallas_call(functools.partial(outer_kernel, offsets, counts), in_specs...  11.8 us
    unnamed x46, local copies, waits for them, and re-layouts  9.58 us
    pallas_call x2, Pallas kernels, back_products(): pl.pallas_call(back_kernel, in_specs=[IN_SMEM] + [IN_VMEM] * 2, out_specs...  7.33 us
    pallas_call x4, Pallas kernels, down_products(): pl.pallas_call(functools.partial(down_kernel, offsets, start is not None)...  4.58 us
  transfers between devices with their start and end apart: 40, of which 15 were waited for; matrix products, arithmetic and copies ran while one was open for 2% of the time, Pallas kernels for 28%

profile of v1, /device:TPU:0, one launch (start us, length us, event | category | flops | bytes accessed | tf_op | source)
XLA Modules:
  0.0 141.2 jit_solution(12377228584708851614)
XLA Ops:
  1.9 3.1 %collective-permute-start = (bf16[24,1536]{1,0:T(8,128)(2,1)S(1)}, bf16[24,1536]{1,0:T(8,128)(2,1)S(1)}, u32[]{:S(2)}, u32[]{:S(2)}) collective-permute-start(bf16[24,1536]{1,0:T(8,128)(2,1)S(1)} %get-tuple-element.58), channel_id=1, source_target_pairs={{0,4},{4,0},{8,12},{12,8},{1,5},{5,1},{9,13},{13,9},{2,6},{6,2},{1... | collective-permute-start | bytes 221192 | tf_op jit(solution)/shard_map/ppermute | solution.py:24
  5.0 2.5 %collective-permute-start.2 = (bf16[24,1536]{1,0:T(8,128)(2,1)S(1)}, bf16[24,1536]{1,0:T(8,128)(2,1)S(1)}, u32[]{:S(2)}, u32[]{:S(2)}) collective-permute-start(bf16[24,1536]{1,0:T(8,128)(2,1)S(1)} %get-tuple-element.59), channel_id=1, source_target_pairs={{0,12},{4,8},{8,4},{12,0},{1,13},{5,9},{9,5},{13,1},{2,14},{6,10},... | collective-permute-start | bytes 221192 | tf_op jit(solution)/shard_map/ppermute | solution.py:24
  7.6 4.6 %collective-permute-done.2 = bf16[24,1536]{1,0:T(8,128)(2,1)S(1)} collective-permute-done((bf16[24,1536]{1,0:T(8,128)(2,1)S(1)}, bf16[24,1536]{1,0:T(8,128)(2,1)S(1)}, u32[]{:S(2)}, u32[]{:S(2)}) %collective-permute-start.2) | collective-permute-done | bytes 73760 | tf_op jit(solution)/shard_map/ppermute | solution.py:24
  14.6 4.7 %copy-done.2 = bf16[1536,4096]{1,0:T(8,128)(2,1)S(1)} copy-done((bf16[1536,4096]{1,0:T(8,128)(2,1)S(1)}, bf16[1536,4096]{1,0:T(8,128)(2,1)}, u32[]{:S(2)}) %copy-start.2) | copy-done | bytes 12582936
  19.3 2.4 %shard_map.99 = (bf16[1,96,1024]{2,1,0:T(8,128)(2,1)S(1)}, bf16[1,96,1024]{2,1,0:T(8,128)(2,1)S(1)}) custom-call(s32[1]{0:T(128)} %bitcast.me_ref, bf16[96,1536]{1,0:T(8,128)(2,1)S(1)} %pad_maximum_fusion.1.rows_ref, bf16[1536,4096]{1,0:T(8,128)(2,1)S(1)} %copy-done.2), custom_call_target="tpu_custom_call" | custom-call | flops 1 | bytes 1 | tf_op jit(solution)/shard_map/pallas_call | solution.py:73
  23.9 2.5 %shard_map.96 = (bf16[1,96,1024]{2,1,0:T(8,128)(2,1)S(1)}, bf16[1,96,1024]{2,1,0:T(8,128)(2,1)S(1)}) custom-call(s32[1]{0:T(128)} %bitcast.me_ref, bf16[96,1536]{1,0:T(8,128)(2,1)S(1)} %pad_maximum_fusion.1.rows_ref, bf16[1536,4096]{1,0:T(8,128)(2,1)S(1)} %copy-done.3), custom_call_target="tpu_custom_call" | custom-call | flops 1 | bytes 1 | tf_op jit(solution)/shard_map/pallas_call | solution.py:73
  28.1 2.5 %shard_map.100 = (bf16[1,96,1024]{2,1,0:T(8,128)(2,1)S(1)}, bf16[1,96,1024]{2,1,0:T(8,128)(2,1)S(1)}) custom-call(s32[1]{0:T(128)} %bitcast.me_ref, bf16[96,1536]{1,0:T(8,128)(2,1)S(1)} %pad_maximum_fusion.1.rows_ref, bf16[1536,4096]{1,0:T(8,128)(2,1)S(1)} %copy-done.4, bf16[96,1024]{1,0:T(8,128)(2,1)S(1)} %fusion.22.refs_1_), custom_call_target="tpu_custom_call" | custom-call | flops 1 | bytes 1 | tf_op jit(solution)/shard_map/pallas_call | solution.py:73
  31.6 2.5 %shard_map.97 = (bf16[1,96,1024]{2,1,0:T(8,128)(2,1)S(1)}, bf16[1,96,1024]{2,1,0:T(8,128)(2,1)S(1)}) custom-call(s32[1]{0:T(128)} %bitcast.me_ref, bf16[96,1536]{1,0:T(8,128)(2,1)S(1)} %pad_maximum_fusion.1.rows_ref, bf16[1536,4096]{1,0:T(8,128)(2,1)S(1)} %copy-done.5, bf16[96,1024]{1,0:T(8,128)(2,1)S(1)} %fusion.20.refs_1_), custom_call_target="tpu_custom_call" | custom-call | flops 1 | bytes 1 | tf_op jit(solution)/shard_map/pallas_call | solution.py:73
  38.7 4.9 %shard_map.98 = (bf16[2,96,1024]{2,1,0:T(8,128)(2,1)S(1)}, bf16[2,96,1024]{2,1,0:T(8,128)(2,1)S(1)}) custom-call(s32[1]{0:T(128)} %bitcast.me_ref, bf16[96,1536]{1,0:T(8,128)(2,1)S(1)} %pad_maximum_fusion.1.rows_ref, bf16[1536,4096]{1,0:T(8,128)(2,1)S(1)} %copy-done.3, bf16[1536,4096]{1,0:T(8,128)(2,1)S(1)} %bitcast.139, ...), custom_call_target="tpu_custom_call" | custom-call | flops 1 | bytes 1 | tf_op jit(solution)/shard_map/pallas_call | solution.py:73
  44.3 5.1 %shard_map.101 = (bf16[2,96,1024]{2,1,0:T(8,128)(2,1)S(1)}, bf16[2,96,1024]{2,1,0:T(8,128)(2,1)S(1)}) custom-call(s32[1]{0:T(128)} %bitcast.me_ref, bf16[96,1536]{1,0:T(8,128)(2,1)S(1)} %pad_maximum_fusion.1.rows_ref, bf16[1536,4096]{1,0:T(8,128)(2,1)S(1)} %copy-done.6, bf16[1536,4096]{1,0:T(8,128)(2,1)S(1)} %bitcast.141, ...), custom_call_target="tpu_custom_call" | custom-call | flops 1 | bytes 1 | tf_op jit(solution)/shard_map/pallas_call | solution.py:73
  54.3 5.2 %collective-permute-done.15.first_ref = bf16[96,1024]{1,0:T(8,128)(2,1)S(1)} collective-permute-done((bf16[96,1024]{1,0:T(8,128)(2,1)S(1)}, bf16[96,1024]{1,0:T(8,128)(2,1)S(1)}, u32[]{:S(2)}, u32[]{:S(2)}) %collective-permute-start.15) | collective-permute-done | bytes 196640 | tf_op jit(solution)/shard_map/ppermute | solution.py:24
  59.6 3.4 %collective-permute-done.26.first_ref = bf16[96,1024]{1,0:T(8,128)(2,1)S(1)} collective-permute-done((bf16[96,1024]{1,0:T(8,128)(2,1)S(1)}, bf16[96,1024]{1,0:T(8,128)(2,1)S(1)}, u32[]{:S(2)}, u32[]{:S(2)}) %collective-permute-start.26) | collective-permute-done | bytes 196640 | tf_op jit(solution)/shard_map/ppermute | solution.py:24
  69.9 2.4 %collective-permute-start.31 = (bf16[24,1536]{1,0:T(8,128)(2,1)S(1)}, bf16[24,1536]{1,0:T(8,128)(2,1)S(1)}, u32[]{:S(2)}, u32[]{:S(2)}) collective-permute-start(bf16[24,1536]{1,0:T(8,128)(2,1)S(1)} %get-tuple-element.52), channel_id=1, source_target_pairs={{0,12},{4,8},{8,4},{12,0},{1,13},{5,9},{9,5},{13,1},{2,14},{6,10},... | collective-permute-start | bytes 221192 | tf_op jit(solution)/shard_map/ppermute | solution.py:24
  75.8 4.3 %collective-permute-done.20 = bf16[24,1536]{1,0:T(8,128)(2,1)S(1)} collective-permute-done((bf16[24,1536]{1,0:T(8,128)(2,1)S(1)}, bf16[24,1536]{1,0:T(8,128)(2,1)S(1)}, u32[]{:S(2)}, u32[]{:S(2)}) %collective-permute-start.20) | collective-permute-done | bytes 73760 | tf_op jit(solution)/shard_map/ppermute | solution.py:24
  80.1 5.6 %collective-permute-done.19 = bf16[24,1536]{1,0:T(8,128)(2,1)S(1)} collective-permute-done((bf16[24,1536]{1,0:T(8,128)(2,1)S(1)}, bf16[24,1536]{1,0:T(8,128)(2,1)S(1)}, u32[]{:S(2)}, u32[]{:S(2)}) %collective-permute-start.19) | collective-permute-done | bytes 73760 | tf_op jit(solution)/shard_map/ppermute | solution.py:24
  89.6 2.5 %collective-permute-start.21 = (bf16[24,1536]{1,0:T(8,128)(2,1)S(1)}, bf16[24,1536]{1,0:T(8,128)(2,1)S(1)}, u32[]{:S(2)}, u32[]{:S(2)}) collective-permute-start(bf16[24,1536]{1,0:T(8,128)(2,1)S(1)} %get-tuple-element.54), channel_id=1, source_target_pairs={{0,4},{4,0},{8,12},{12,8},{1,5},{5,1},{9,13},{13,9},{2,6},{6,2},{1... | collective-permute-start | bytes 221192 | tf_op jit(solution)/shard_map/ppermute | solution.py:24
  94.1 2.4 %collective-permute-done.21 = bf16[24,1536]{1,0:T(8,128)(2,1)S(1)} collective-permute-done((bf16[24,1536]{1,0:T(8,128)(2,1)S(1)}, bf16[24,1536]{1,0:T(8,128)(2,1)S(1)}, u32[]{:S(2)}, u32[]{:S(2)}) %collective-permute-start.21) | collective-permute-done | bytes 73760 | tf_op jit(solution)/shard_map/ppermute | solution.py:24
  97.0 3.7 %shard_map.104 = (bf16[2,96,1024]{2,1,0:T(8,128)(2,1)S(1)}, bf16[2,96,1024]{2,1,0:T(8,128)(2,1)S(1)}) custom-call(s32[1]{0:T(128)} %bitcast.me_ref, bf16[96,1536]{1,0:T(8,128)(2,1)S(1)} %pad_maximum_fusion.2.rows_ref, bf16[4096,1536]{1,0:T(8,128)(2,1)S(1)} %bitcast.137), custom_call_target="tpu_custom_call" | custom-call | flops 1 | bytes 1 | tf_op jit(solution)/shard_map/pallas_call | solution.py:102
  102.5 3.7 %shard_map.107 = (bf16[2,96,1024]{2,1,0:T(8,128)(2,1)S(1)}, bf16[2,96,1024]{2,1,0:T(8,128)(2,1)S(1)}) custom-call(s32[1]{0:T(128)} %bitcast.me_ref, bf16[96,1536]{1,0:T(8,128)(2,1)S(1)} %pad_maximum_fusion.3.rows_ref, bf16[4096,1536]{1,0:T(8,128)(2,1)S(1)} %bitcast.137), custom_call_target="tpu_custom_call" | custom-call | flops 1 | bytes 1 | tf_op jit(solution)/shard_map/pallas_call | solution.py:102
  109.4 4.7 %collective-permute-done.25 = bf16[96,1024]{1,0:T(8,128)(2,1)S(1)} collective-permute-done((bf16[96,1024]{1,0:T(8,128)(2,1)S(1)}, bf16[96,1024]{1,0:T(8,128)(2,1)S(1)}, u32[]{:S(2)}, u32[]{:S(2)}) %collective-permute-start.25) | collective-permute-done | bytes 196640 | tf_op jit(solution)/shard_map/ppermute | solution.py:24
  114.1 3.8 %collective-permute-done.36 = bf16[96,1024]{1,0:T(8,128)(2,1)S(1)} collective-permute-done((bf16[96,1024]{1,0:T(8,128)(2,1)S(1)}, bf16[96,1024]{1,0:T(8,128)(2,1)S(1)}, u32[]{:S(2)}, u32[]{:S(2)}) %collective-permute-start.36) | collective-permute-done | bytes 196640 | tf_op jit(solution)/shard_map/ppermute | solution.py:24
  123.5 5.2 %shard_map.108 = (bf16[1536,4096]{1,0:T(8,128)(2,1)}, bf16[1536,4096]{1,0:T(8,128)(2,1)}) custom-call(s32[1]{0:T(128)} %bitcast.me_ref, bf16[1536,96]{1,0:T(8,128)(2,1)S(1)} %copy-done.8, bf16[2,96,1024]{2,1,0:T(8,128)(2,1)S(1)} %pad_maximum_fusion.refs_0_, bf16[2,96,1024]{2,1,0:T(8,128)(2,1)S(1)} %collective-permute-done.38.refs_1_), custom_call_target="tpu_custom_call" | custom-call | flops 1207959552 | bytes 12582912 | tf_op jit(solution)/shard_map/pallas_call | solution.py:174
  134.4 3.3 %shard_map.110 = (bf16[1536,4096]{1,0:T(8,128)(2,1)}, bf16[1536,4096]{1,0:T(8,128)(2,1)}) custom-call(s32[1]{0:T(128)} %bitcast.me_ref, bf16[1536,96]{1,0:T(8,128)(2,1)S(1)} %copy-done.9, bf16[2,96,1024]{2,1,0:T(8,128)(2,1)S(1)} %copy-done.10, bf16[1536,4096]{1,0:T(8,128)(2,1)} %get-tuple-element.38.refs_0_.refs_1_, ...), custom_call_target="tpu_custom_call", output_to_operand_aliasing={{0}: (3, {}), {1}: (4, {})} | custom-call | flops 603979776 | bytes 6291456 | tf_op jit(solution)/shard_map/pallas_call | solution.py:174
  137.7 3.3 %shard_map.111 = (bf16[1536,4096]{1,0:T(8,128)(2,1)}, bf16[1536,4096]{1,0:T(8,128)(2,1)}) custom-call(s32[1]{0:T(128)} %bitcast.me_ref, bf16[1536,96]{1,0:T(8,128)(2,1)S(1)} %copy-done.9, bf16[2,96,1024]{2,1,0:T(8,128)(2,1)S(1)} %collective-permute-done.39.refs_0_, ...), custom_call_target="tpu_custom_call", output_to_operand_aliasing={{0}: (3, {}), {1}: (4, {})} | custom-call | flops 603979776 | bytes 6291456 | tf_op jit(solution)/shard_map/pallas_call | solution.py:174
  (159 shorter events, 51.5 us)
Async XLA Ops:
  5.0 7.2 %collective-permute-start.2 = (bf16[24,1536]{1,0:T(8,128)(2,1)S(1)}, bf16[24,1536]{1,0:T(8,128)(2,1)S(1)}, u32[]{:S(2)}, u32[]{:S(2)}) collective-permute-start(bf16[24,1536]{1,0:T(8,128)(2,1)S(1)} %get-tuple-element.59), channel_id=1, source_target_pairs={{0,12},{4,8},{8,4},{12,0},{1,13},{5,9},{9,5},{13,1},{2,14},{6,10},... | collective-permute-start | bytes 221192 | tf_op jit(solution)/shard_map/ppermute | solution.py:24
  7.5 7.1 %collective-permute-start.1 = (bf16[24,1536]{1,0:T(8,128)(2,1)S(1)}, bf16[24,1536]{1,0:T(8,128)(2,1)S(1)}, u32[]{:S(2)}, u32[]{:S(2)}) collective-permute-start(bf16[24,1536]{1,0:T(8,128)(2,1)S(1)} %get-tuple-element.59), channel_id=1, source_target_pairs={{0,8},{4,12},{8,0},{12,4},{1,9},{5,13},{9,1},{13,5},{2,10},{6,14},... | collective-permute-start | bytes 221192 | tf_op jit(solution)/shard_map/ppermute | solution.py:24
  26.5 17.8 %collective-permute-start.10 = (bf16[96,1024]{1,0:T(8,128)(2,1)S(1)}, bf16[96,1024]{1,0:T(8,128)(2,1)S(1)}, u32[]{:S(2)}, u32[]{:S(2)}) collective-permute-start(bf16[96,1024]{1,0:T(8,128)(2,1)S(1)} %fusion.22.refs_1_), channel_id=1, source_target_pairs={{0,2},{1,3},{2,0},{3,1},{4,6},{5,7},{6,4},{7,5},{8,10},{9,11},{10,... | collective-permute-start | bytes 589832 | tf_op jit(solution)/shard_map/ppermute | solution.py:24
  30.9 7.8 %collective-permute-start.5 = (bf16[96,1024]{1,0:T(8,128)(2,1)S(1)}, bf16[96,1024]{1,0:T(8,128)(2,1)S(1)}, u32[]{:S(2)}, u32[]{:S(2)}) collective-permute-start(bf16[96,1024]{1,0:T(8,128)(2,1)S(1)} %fusion.20.refs_1_), channel_id=1, source_target_pairs={{0,2},{1,3},{2,0},{3,1},{4,6},{5,7},{6,4},{7,5},{8,10},{9,11},{10,... | collective-permute-start | bytes 589832 | tf_op jit(solution)/shard_map/ppermute | solution.py:24
  34.4 16.9 %collective-permute-start.14 = (bf16[96,1024]{1,0:T(8,128)(2,1)S(1)}, bf16[96,1024]{1,0:T(8,128)(2,1)S(1)}, u32[]{:S(2)}, u32[]{:S(2)}) collective-permute-start(bf16[96,1024]{1,0:T(8,128)(2,1)S(1)} %fusion.23.refs_2_), channel_id=1, source_target_pairs={{0,2},{1,3},{2,0},{3,1},{4,6},{5,7},{6,4},{7,5},{8,10},{9,11},{10,... | collective-permute-start | bytes 589832 | tf_op jit(solution)/shard_map/ppermute | solution.py:24
  35.8 15.6 %collective-permute-start.13 = (bf16[96,1024]{1,0:T(8,128)(2,1)S(1)}, bf16[96,1024]{1,0:T(8,128)(2,1)S(1)}, u32[]{:S(2)}, u32[]{:S(2)}) collective-permute-start(bf16[96,1024]{1,0:T(8,128)(2,1)S(1)} %fusion.21.refs_2_), channel_id=1, source_target_pairs={{0,2},{1,3},{2,0},{3,1},{4,6},{5,7},{6,4},{7,5},{8,10},{9,11},{10,... | collective-permute-start | bytes 589832 | tf_op jit(solution)/shard_map/ppermute | solution.py:24
  51.7 7.8 %collective-permute-start.15 = (bf16[96,1024]{1,0:T(8,128)(2,1)S(1)}, bf16[96,1024]{1,0:T(8,128)(2,1)S(1)}, u32[]{:S(2)}, u32[]{:S(2)}) collective-permute-start(bf16[96,1024]{1,0:T(8,128)(2,1)S(1)} %get-tuple-element.42.first_ref), channel_id=1, source_target_pairs={{0,2},{1,3},{2,0},{3,1},{4,6},{5,7},{6,4},{7,5},{8,10},{9,11},{10,... | collective-permute-start | bytes 589832 | tf_op jit(solution)/shard_map/ppermute | solution.py:24
  53.1 9.9 %collective-permute-start.26 = (bf16[96,1024]{1,0:T(8,128)(2,1)S(1)}, bf16[96,1024]{1,0:T(8,128)(2,1)S(1)}, u32[]{:S(2)}, u32[]{:S(2)}) collective-permute-start(bf16[96,1024]{1,0:T(8,128)(2,1)S(1)} %get-tuple-element.43.first_ref), channel_id=1, source_target_pairs={{0,2},{1,3},{2,0},{3,1},{4,6},{5,7},{6,4},{7,5},{8,10},{9,11},{10,... | collective-permute-start | bytes 589832 | tf_op jit(solution)/shard_map/ppermute | solution.py:24
  53.8 9.2 %collective-permute-start.28 = (bf16[96,1024]{1,0:T(8,128)(2,1)S(1)}, bf16[96,1024]{1,0:T(8,128)(2,1)S(1)}, u32[]{:S(2)}, u32[]{:S(2)}) collective-permute-start(bf16[96,1024]{1,0:T(8,128)(2,1)S(1)} %get-tuple-element.43.first_ref), channel_id=1, source_target_pairs={{0,1},{1,0},{2,3},{3,2},{4,5},{5,4},{6,7},{7,6},{8,9},{9,8},{10,11... | collective-permute-start | bytes 589832 | tf_op jit(solution)/shard_map/ppermute | solution.py:24
  53.8 10.4 %collective-permute-start.17 = (bf16[96,1024]{1,0:T(8,128)(2,1)S(1)}, bf16[96,1024]{1,0:T(8,128)(2,1)S(1)}, u32[]{:S(2)}, u32[]{:S(2)}) collective-permute-start(bf16[96,1024]{1,0:T(8,128)(2,1)S(1)} %get-tuple-element.42.first_ref), channel_id=1, source_target_pairs={{0,1},{1,0},{2,3},{3,2},{4,5},{5,4},{6,7},{7,6},{8,9},{9,8},{10,11... | collective-permute-start | bytes 589832 | tf_op jit(solution)/shard_map/ppermute | solution.py:24
  66.6 7.3 %collective-permute-start.18 = (bf16[24,1536]{1,0:T(8,128)(2,1)S(1)}, bf16[24,1536]{1,0:T(8,128)(2,1)S(1)}, u32[]{:S(2)}, u32[]{:S(2)}) collective-permute-start(bf16[24,1536]{1,0:T(8,128)(2,1)S(1)} %get-tuple-element.48), channel_id=1, source_target_pairs={{0,4},{4,0},{8,12},{12,8},{1,5},{5,1},{9,13},{13,9},{2,6},{6,2},{1... | collective-permute-start | bytes 221192 | tf_op jit(solution)/shard_map/ppermute | solution.py:24
  67.8 20.8 %collective-permute-start.29 = (bf16[24,1536]{1,0:T(8,128)(2,1)S(1)}, bf16[24,1536]{1,0:T(8,128)(2,1)S(1)}, u32[]{:S(2)}, u32[]{:S(2)}) collective-permute-start(bf16[24,1536]{1,0:T(8,128)(2,1)S(1)} %get-tuple-element.51), channel_id=1, source_target_pairs={{0,4},{4,0},{8,12},{12,8},{1,5},{5,1},{9,13},{13,9},{2,6},{6,2},{1... | collective-permute-start | bytes 221192 | tf_op jit(solution)/shard_map/ppermute | solution.py:24
  69.9 18.8 %collective-permute-start.31 = (bf16[24,1536]{1,0:T(8,128)(2,1)S(1)}, bf16[24,1536]{1,0:T(8,128)(2,1)S(1)}, u32[]{:S(2)}, u32[]{:S(2)}) collective-permute-start(bf16[24,1536]{1,0:T(8,128)(2,1)S(1)} %get-tuple-element.52), channel_id=1, source_target_pairs={{0,12},{4,8},{8,4},{12,0},{1,13},{5,9},{9,5},{13,1},{2,14},{6,10},... | collective-permute-start | bytes 221192 | tf_op jit(solution)/shard_map/ppermute | solution.py:24
  72.3 16.4 %collective-permute-start.30 = (bf16[24,1536]{1,0:T(8,128)(2,1)S(1)}, bf16[24,1536]{1,0:T(8,128)(2,1)S(1)}, u32[]{:S(2)}, u32[]{:S(2)}) collective-permute-start(bf16[24,1536]{1,0:T(8,128)(2,1)S(1)} %get-tuple-element.53), channel_id=1, source_target_pairs={{0,8},{4,12},{8,0},{12,4},{1,9},{5,13},{9,1},{13,5},{2,10},{6,14},... | collective-permute-start | bytes 221192 | tf_op jit(solution)/shard_map/ppermute | solution.py:24
  72.3 7.8 %collective-permute-start.20 = (bf16[24,1536]{1,0:T(8,128)(2,1)S(1)}, bf16[24,1536]{1,0:T(8,128)(2,1)S(1)}, u32[]{:S(2)}, u32[]{:S(2)}) collective-permute-start(bf16[24,1536]{1,0:T(8,128)(2,1)S(1)} %get-tuple-element.49), channel_id=1, source_target_pairs={{0,12},{4,8},{8,4},{12,0},{1,13},{5,9},{9,5},{13,1},{2,14},{6,10},... | collective-permute-start | bytes 221192 | tf_op jit(solution)/shard_map/ppermute | solution.py:24
  73.9 11.9 %collective-permute-start.19 = (bf16[24,1536]{1,0:T(8,128)(2,1)S(1)}, bf16[24,1536]{1,0:T(8,128)(2,1)S(1)}, u32[]{:S(2)}, u32[]{:S(2)}) collective-permute-start(bf16[24,1536]{1,0:T(8,128)(2,1)S(1)} %get-tuple-element.50), channel_id=1, source_target_pairs={{0,8},{4,12},{8,0},{12,4},{1,9},{5,13},{9,1},{13,5},{2,10},{6,14},... | collective-permute-start | bytes 221192 | tf_op jit(solution)/shard_map/ppermute | solution.py:24
  86.6 10.3 %collective-permute-start.23 = (bf16[24,1536]{1,0:T(8,128)(2,1)S(1)}, bf16[24,1536]{1,0:T(8,128)(2,1)S(1)}, u32[]{:S(2)}, u32[]{:S(2)}) collective-permute-start(bf16[24,1536]{1,0:T(8,128)(2,1)S(1)} %get-tuple-element.55), channel_id=1, source_target_pairs={{0,12},{4,8},{8,4},{12,0},{1,13},{5,9},{9,5},{13,1},{2,14},{6,10},... | collective-permute-start | bytes 221192 | tf_op jit(solution)/shard_map/ppermute | solution.py:24
  88.7 8.3 %collective-permute-start.22 = (bf16[24,1536]{1,0:T(8,128)(2,1)S(1)}, bf16[24,1536]{1,0:T(8,128)(2,1)S(1)}, u32[]{:S(2)}, u32[]{:S(2)}) collective-permute-start(bf16[24,1536]{1,0:T(8,128)(2,1)S(1)} %get-tuple-element.55), channel_id=1, source_target_pairs={{0,8},{4,12},{8,0},{12,4},{1,9},{5,13},{9,1},{13,5},{2,10},{6,14},... | collective-permute-start | bytes 221192 | tf_op jit(solution)/shard_map/ppermute | solution.py:24
  89.6 7.0 %collective-permute-start.21 = (bf16[24,1536]{1,0:T(8,128)(2,1)S(1)}, bf16[24,1536]{1,0:T(8,128)(2,1)S(1)}, u32[]{:S(2)}, u32[]{:S(2)}) collective-permute-start(bf16[24,1536]{1,0:T(8,128)(2,1)S(1)} %get-tuple-element.54), channel_id=1, source_target_pairs={{0,4},{4,0},{8,12},{12,8},{1,5},{5,1},{9,13},{13,9},{2,6},{6,2},{1... | collective-permute-start | bytes 221192 | tf_op jit(solution)/shard_map/ppermute | solution.py:24
  92.1 10.4 %collective-permute-start.34 = (bf16[24,1536]{1,0:T(8,128)(2,1)S(1)}, bf16[24,1536]{1,0:T(8,128)(2,1)S(1)}, u32[]{:S(2)}, u32[]{:S(2)}) collective-permute-start(bf16[24,1536]{1,0:T(8,128)(2,1)S(1)} %get-tuple-element.57), channel_id=1, source_target_pairs={{0,12},{4,8},{8,4},{12,0},{1,13},{5,9},{9,5},{13,1},{2,14},{6,10},... | collective-permute-start | bytes 221192 | tf_op jit(solution)/shard_map/ppermute | solution.py:24
  94.1 8.4 %collective-permute-start.33 = (bf16[24,1536]{1,0:T(8,128)(2,1)S(1)}, bf16[24,1536]{1,0:T(8,128)(2,1)S(1)}, u32[]{:S(2)}, u32[]{:S(2)}) collective-permute-start(bf16[24,1536]{1,0:T(8,128)(2,1)S(1)} %get-tuple-element.57), channel_id=1, source_target_pairs={{0,8},{4,12},{8,0},{12,4},{1,9},{5,13},{9,1},{13,5},{2,10},{6,14},... | collective-permute-start | bytes 221192 | tf_op jit(solution)/shard_map/ppermute | solution.py:24
  106.3 7.8 %collective-permute-start.25 = (bf16[96,1024]{1,0:T(8,128)(2,1)S(1)}, bf16[96,1024]{1,0:T(8,128)(2,1)S(1)}, u32[]{:S(2)}, u32[]{:S(2)}) collective-permute-start(bf16[96,1024]{1,0:T(8,128)(2,1)S(1)} %fusion.24), channel_id=1, source_target_pairs={{0,2},{1,3},{2,0},{3,1},{4,6},{5,7},{6,4},{7,5},{8,10},{9,11},{10,... | collective-permute-start | bytes 589832 | tf_op jit(solution)/shard_map/ppermute | solution.py:24
  108.0 9.9 %collective-permute-start.36 = (bf16[96,1024]{1,0:T(8,128)(2,1)S(1)}, bf16[96,1024]{1,0:T(8,128)(2,1)S(1)}, u32[]{:S(2)}, u32[]{:S(2)}) collective-permute-start(bf16[96,1024]{1,0:T(8,128)(2,1)S(1)} %fusion.25), channel_id=1, source_target_pairs={{0,2},{1,3},{2,0},{3,1},{4,6},{5,7},{6,4},{7,5},{8,10},{9,11},{10,... | collective-permute-start | bytes 589832 | tf_op jit(solution)/shard_map/ppermute | solution.py:24
  119.3 11.5 %collective-permute-start.37 = (bf16[2,96,1024]{2,1,0:T(8,128)(2,1)S(1)}, bf16[2,96,1024]{2,1,0:T(8,128)(2,1)S(1)}, u32[]{:S(2)}, u32[]{:S(2)}) collective-permute-start(bf16[2,96,1024]{2,1,0:T(8,128)(2,1)S(1)} %pad_maximum_fusion.refs_0_), channel_id=1, source_target_pairs={{0,2},{1,3},{2,0},{3,1},{4,6},{5,7},{6,4},{7,5},{8,10},{9,11},{10,... | collective-permute-start | bytes 1179656 | tf_op jit(solution)/shard_map/ppermute | solution.py:24
  (39 other events, 288.8 us)

commit v2 on v1

v2 whole, which is shorter than its diff:
```python
import functools

import jax
import jax.numpy as jnp
from jax import lax
from jax.experimental import pallas as pl
from jax.experimental.pallas import tpu as pltpu
from jax.sharding import PartitionSpec as P

EXPERTS = 2
BF16 = jnp.bfloat16
F32 = jnp.float32
KIB = 1024
MIB = 1024 * KIB
IN_VMEM = pl.BlockSpec(memory_space=pltpu.VMEM)
IN_SMEM = pl.BlockSpec(memory_space=pltpu.SMEM)
IN_HBM = pl.BlockSpec(memory_space=pltpu.HBM)
ANYWHERE = pl.BlockSpec(memory_space=pl.ANY)
PARTS = 2
ROWS = 16


def swap(value, axis, mask):
    size = lax.axis_size(axis)
    return lax.ppermute(value, axis, [(i, i ^ mask) for i in range(size)])


def sub_width(width):
    return 512 if width % 512 == 0 else width


def params(limit):
    return pltpu.CompilerParams(vmem_limit_bytes=limit)


def cost(flops, size):
    return pl.CostEstimate(flops=flops, bytes_accessed=size, transcendentals=0)


def prefetch_kernel(offsets, me_ref, *refs):
    weights, halves, sems = refs[: (len(refs) - 1) // 2], refs[(len(refs) - 1) // 2 : -1], refs[-1]
    quarter = halves[0].shape[2]
    copies = []
    for k, (weight_ref, half_ref) in enumerate(zip(weights, halves)):
        for p, offset in enumerate(offsets):
            base = pl.multiple_of((me_ref[0] ^ offset) * quarter, quarter)
            copies.append(
                pltpu.make_async_copy(
                    weight_ref.at[:, pl.ds(base, quarter)], half_ref.at[p], sems.at[k, p]
                )
            )
    for copy in copies:
        copy.start()
    for copy in copies:
        copy.wait()


def prefetch(me, weights, offsets):
    count, (depth, width) = len(weights), weights[0].shape
    half = (len(offsets), depth, width // 4)
    return pl.pallas_call(
        functools.partial(prefetch_kernel, offsets),
        in_specs=[IN_SMEM] + [IN_HBM] * count,
        out_specs=[IN_VMEM] * count,
        out_shape=[pltpu.VMEM(half, BF16)] * count,
        scratch_shapes=[pltpu.SemaphoreType.DMA((count, len(offsets)))],
        compiler_params=params(36 * MIB),
        cost_estimate=cost(1, 2 * count * depth * width),
    )(me, *weights)


def put(parts, rows, value):
    for i, part in enumerate(parts):
        part[...] = value[i * rows : (i + 1) * rows].astype(BF16)


def resident_kernel(rows_ref, half_ref, *refs):
    sends, keep_ref = refs[-1 - PARTS : -1], refs[-1]
    quarter = keep_ref.shape[2]
    sub = sub_width(quarter)
    for p in range(2):
        for c in range(0, quarter, sub):
            product = jnp.dot(
                rows_ref[...], half_ref[p, :, c : c + sub], preferred_element_type=F32
            )
            if p == 0:
                put([ref.at[:, c : c + sub] for ref in sends], sends[0].shape[0], product)
            else:
                keep_ref[0, :, c : c + sub] = product.astype(BF16)


def result_shapes(count, height, quarter):
    part = jax.ShapeDtypeStruct((height // PARTS, quarter), BF16)
    return [part] * (PARTS * count) + [jax.ShapeDtypeStruct((count, height, quarter), BF16)]


def resident_products(rows, half, after):
    shapes = result_shapes(1, rows.shape[0], half.shape[2])
    *send, keep = pl.pallas_call(
        resident_kernel,
        in_specs=[IN_VMEM] * 2 + [ANYWHERE] * len(after),
        out_specs=[IN_VMEM] * len(shapes),
        out_shape=shapes,
        compiler_params=params(4 * MIB),
        cost_estimate=cost(1, 1),
    )(rows, half, *after)
    return send, keep


def stream_kernel(count, offsets, me_ref, rows_ref, *refs):
    weights, (keep_ref, slots_ref, sems) = refs[:count], refs[-3:]
    sends = refs[-3 - PARTS * count : -3]
    quarter = keep_ref.shape[2]
    slots, unused, sub = slots_ref.shape
    copies, targets = [], []
    for k in range(count):
        for p, offset in enumerate(offsets):
            base = (me_ref[0] ^ offset) * quarter
            for c in range(0, quarter, sub):
                columns = pl.ds(pl.multiple_of(base + c, sub), sub)
                slot = len(copies) % slots
                copies.append(
                    pltpu.make_async_copy(
                        weights[k].at[:, columns], slots_ref.at[slot], sems.at[slot]
                    )
                )
                targets.append((k, p, c))
    for copy in copies[:slots]:
        copy.start()
    for i, (k, p, c) in enumerate(targets):
        copies[i].wait()
        product = jnp.dot(rows_ref[...], slots_ref[i % slots], preferred_element_type=F32)
        if p == 0:
            parts = sends[PARTS * k : PARTS * (k + 1)]
            put([ref.at[:, c : c + sub] for ref in parts], parts[0].shape[0], product)
        else:
            keep_ref[k, :, c : c + sub] = product.astype(BF16)
        if i + slots < len(copies):
            copies[i + slots].start()


def stream_products(me, rows, weights, offsets, after):
    count, (height, depth) = len(weights), rows.shape
    quarter = weights[0].shape[1] // 4
    sub = sub_width(quarter)
    slots = min(4, 2 * count * (quarter // sub))
    shapes = result_shapes(count, height, quarter)
    *send, keep = pl.pallas_call(
        functools.partial(stream_kernel, count, offsets),
        in_specs=[IN_SMEM, IN_VMEM] + [IN_HBM] * count + [ANYWHERE] * len(after),
        out_specs=[IN_VMEM] * len(shapes),
        out_shape=shapes,
        scratch_shapes=[pltpu.VMEM((slots, depth, sub), BF16), pltpu.SemaphoreType.DMA((slots,))],
        compiler_params=params(48 * MIB),
        cost_estimate=cost(1, 1),
    )(me, rows, *weights, *after)
    return send, keep


def stacked(pieces):
    return jnp.concatenate([piece[...].astype(F32) for piece in pieces], axis=0)


def back_kernel(count, offsets, me_ref, *refs):
    pieces, weight_ref = refs[:count], refs[count]
    sends, (keep_ref, turned_ref) = refs[-2 - 2 * PARTS : -2], refs[-2:]
    unused, height, quarter = keep_ref.shape
    sub = sub_width(quarter)
    turned_ref[...] = stacked(pieces).T.astype(BF16)
    for p, offset in enumerate(offsets):
        base = (me_ref[0] ^ offset) * quarter
        for c in range(0, quarter, sub):
            piece = weight_ref[pl.ds(pl.multiple_of(base + c, sub), sub), :]
            product = jnp.dot(piece, turned_ref[...], preferred_element_type=F32).T
            if p == 0:
                put([ref.at[:, c : c + sub] for ref in sends], sends[0].shape[0], product)
            else:
                keep_ref[0, :, c : c + sub] = product[:height].astype(BF16)
                keep_ref[1, :, c : c + sub] = product[height:].astype(BF16)


def back_products(me, pieces, weight, offsets, after):
    count, (rows, depth) = len(pieces), pieces[0].shape
    height, quarter = count * rows // 2, weight.shape[0] // 4
    shapes = result_shapes(2, height, quarter)
    *send, keep = pl.pallas_call(
        functools.partial(back_kernel, count, offsets),
        in_specs=[IN_SMEM] + [IN_VMEM] * (count + 1) + [ANYWHERE] * len(after),
        out_specs=[IN_VMEM] * len(shapes),
        out_shape=shapes,
        scratch_shapes=[pltpu.VMEM((depth, 2 * height), BF16)],
        compiler_params=params(8 * MIB),
        cost_estimate=cost(1, 1),
    )(me, *pieces, weight, *after)
    return send, keep


def down_kernel(offsets, has_start, pieces, me_ref, first_ref, second_ref, weight_ref, *rest):
    outs = rest[-pieces:]
    quarter = first_ref.shape[1]
    width = weight_ref.shape[1]
    sub = sub_width(width)
    for c in range(0, width, sub):
        total = rest[0][:, c : c + sub] if has_start else 0.0
        for rows_ref, offset in zip((first_ref, second_ref), offsets):
            base = pl.multiple_of((me_ref[0] ^ offset) * quarter, quarter)
            piece = weight_ref[pl.ds(base, quarter), c : c + sub]
            total += jnp.dot(rows_ref[...], piece, preferred_element_type=F32)
        for i, out_ref in enumerate(outs):
            rows = out_ref.shape[0]
            out_ref[:, c : c + sub] = total[i * rows : (i + 1) * rows].astype(out_ref.dtype)


def down_products(me, first, second, weight, offsets, start, pieces, out_type, after=()):
    height, quarter = first.shape
    width = weight.shape[1]
    operands = [first, second, weight] + ([] if start is None else [start])
    return pl.pallas_call(
        functools.partial(down_kernel, offsets, start is not None, pieces),
        in_specs=[IN_SMEM] + [IN_VMEM] * len(operands) + [ANYWHERE] * len(after),
        out_specs=[IN_VMEM] * pieces,
        out_shape=[jax.ShapeDtypeStruct((height // pieces, width), out_type)] * pieces,
        compiler_params=params(4 * MIB),
        cost_estimate=cost(1, 1),
    )(me, *operands, *after)


def mix_kernel(count, token_total, *refs):
    pieces, spread_ref, outs = refs[:count], refs[count], refs[-EXPERTS:]
    per_expert = count // EXPERTS
    mixed = 0.0
    for e in range(EXPERTS):
        total = 0.0
        for piece in pieces[e * per_expert : (e + 1) * per_expert]:
            total += piece[...].astype(F32)
        mixed += lax.dot_general(
            spread_ref[e],
            total,
            (((0,), (0,)), ((), ())),
            precision=lax.Precision.HIGHEST,
            preferred_element_type=F32,
        )
    mixed = mixed / token_total
    for e in range(EXPERTS):
        outs[e][...] = jnp.dot(
            spread_ref[e], mixed, precision=lax.Precision.HIGHEST, preferred_element_type=F32
        ).astype(BF16)


def mix_products(pieces, spread, token_total, after=()):
    count = len(pieces)
    result = jax.ShapeDtypeStruct(pieces[0].shape, BF16)
    return pl.pallas_call(
        functools.partial(mix_kernel, count, token_total),
        in_specs=[IN_VMEM] * (count + 1) + [ANYWHERE] * len(after),
        out_specs=[IN_VMEM] * EXPERTS,
        out_shape=[result] * EXPERTS,
        compiler_params=params(8 * MIB),
        cost_estimate=cost(1, 1),
    )(*pieces, spread, *after)


def outer_kernel(offsets, me_ref, tokens_ref, *refs):
    terms, (turned_ref, slots_ref, sems) = refs[: len(offsets)], refs[-3:]
    outs = refs[-5:-3]
    if len(offsets) == 2:
        outs, flag_ref = refs[-6:-4], refs[-4]
        flag_ref[...] = jnp.zeros_like(flag_ref)
    quarter = terms[0].shape[2]
    slots, unused, sub = slots_ref.shape
    turned_ref[...] = tokens_ref[...].astype(F32).T.astype(BF16)
    copies = []
    for term_ref, offset in zip(terms, offsets):
        base = (me_ref[0] ^ offset) * quarter
        for k in range(2):
            for c in range(0, quarter, sub):
                slot = len(copies) % slots
                if len(copies) >= slots:
                    copies[-slots].wait()
                slots_ref[slot] = jnp.dot(
                    turned_ref[...], term_ref[k, :, c : c + sub], preferred_element_type=F32
                ).astype(BF16)
                columns = pl.ds(pl.multiple_of(base + c, sub), sub)
                copy = pltpu.make_async_copy(
                    slots_ref.at[slot], outs[k].at[:, columns], sems.at[slot]
                )
                copy.start()
                copies.append(copy)
    for copy in copies[-slots:]:
        copy.wait()


def outer_products(me, tokens, terms, offsets, outputs):
    height, width = tokens.shape
    quarter = terms[0].shape[2]
    sub = sub_width(quarter)
    slots = min(4, 2 * len(terms) * (quarter // sub))
    operands = [tokens, *terms]
    given = [] if outputs is None else list(outputs)
    flags = len(offsets) - 1
    return pl.pallas_call(
        functools.partial(outer_kernel, offsets),
        in_specs=[IN_SMEM] + [IN_VMEM] * len(operands) + [ANYWHERE] * len(given),
        out_specs=[ANYWHERE] * 2 + [IN_VMEM] * flags,
        out_shape=[jax.ShapeDtypeStruct((width, 4 * quarter), BF16)] * 2
        + [jax.ShapeDtypeStruct((8, 128), F32)] * flags,
        input_output_aliases={1 + len(operands) + k: k for k in range(len(given))},
        scratch_shapes=[
            pltpu.VMEM((width, height), BF16),
            pltpu.VMEM((slots, width, sub), BF16),
            pltpu.SemaphoreType.DMA((slots,)),
        ],
        compiler_params=params(14 * MIB),
        cost_estimate=cost(1, 1),
    )(me, *operands, *given)


def rows_kernel(function, count, results, *refs):
    ins, outs = refs[:count], refs[-results:]
    height = outs[0].shape[-2]
    for low in range(0, height, ROWS):

        def load(i):
            ref = ins[i]
            if ref.shape[-2] == height:
                return ref[..., low : low + ROWS, :].astype(F32)
            part, start = divmod(low, ref.shape[-2])
            return ins[i + part][start : start + ROWS].astype(F32)

        for ref, value in zip(outs, function(load)):
            ref[..., low : low + ROWS, :] = value.astype(ref.dtype)


def by_rows(function, operands, shapes, after):
    return pl.pallas_call(
        functools.partial(rows_kernel, function, len(operands), len(shapes)),
        in_specs=[IN_VMEM] * len(operands) + [ANYWHERE] * len(after),
        out_specs=[IN_VMEM] * len(shapes),
        out_shape=[jax.ShapeDtypeStruct(shape, dtype) for shape, dtype in shapes],
        compiler_params=params(12 * MIB),
        cost_estimate=cost(1, 1),
    )(*operands, *after)


def far_rows(load):
    return (load(0)[0] + load(1),)


def far_pair_rows(load):
    near = load(0)
    return (jnp.stack([near[0] + load(1), near[1] + load(1 + PARTS)]),)


def hidden_rows(load):
    near = load(0)
    gate_value = near[0] + load(1) + load(1 + 2 * PARTS)
    up_value = near[1] + load(1 + PARTS) + load(2 + 2 * PARTS)
    return gate_value * jax.nn.sigmoid(gate_value) * up_value, gate_value, up_value


def tangent_rows(load):
    near = load(0)
    gate_tangent = near[0] + load(1) + load(1 + 2 * PARTS)
    up_tangent = near[1] + load(1 + PARTS) + load(2 + 2 * PARTS)
    gate_value, up_value = load(3 + 2 * PARTS), load(4 + 2 * PARTS)
    s = jax.nn.sigmoid(gate_value)
    slope = s + gate_value * s * (1.0 - s)
    hidden_tangent = slope * gate_tangent * up_value + gate_value * s * up_tangent
    return hidden_tangent, gate_tangent, up_tangent


def term_rows(load):
    near, across = load(0), load(1)
    back_value = near[0] + load(2) + across[0]
    back_tangent = near[1] + load(2 + PARTS) + across[1]
    gate_value, up_value, gate_tangent, up_tangent = (load(2 + 2 * PARTS + i) for i in range(4))
    s = jax.nn.sigmoid(gate_value)
    slope = s + gate_value * s * (1.0 - s)
    bend = s * (1.0 - s) * (2.0 + gate_value * (1.0 - 2.0 * s))
    gate_term = (
        back_tangent * up_value * slope
        + back_value * up_tangent * slope
        + back_value * up_value * bend * gate_tangent
    )
    up_term = back_tangent * (gate_value * s) + back_value * slope * gate_tangent
    return (jnp.stack([gate_term, up_term]),)


def pass_kernel(value_ref, *refs):
    refs[-1][...] = value_ref[...]


def pass_on(value, after):
    return pl.pallas_call(
        pass_kernel,
        in_specs=[IN_VMEM] + [ANYWHERE] * len(after),
        out_specs=IN_VMEM,
        out_shape=jax.ShapeDtypeStruct(value.shape, value.dtype),
        compiler_params=params(4 * MIB),
        cost_estimate=cost(1, 1),
    )(value, *after)


def exchange(pieces):
    ranks = lax.axis_size("expert")
    if ranks <= 4:
        return [pieces[0]] + [swap(pieces[i], "expert", i) for i in range(1, ranks)]
    order = lax.axis_index("expert") ^ jnp.arange(ranks)
    stacked = jnp.take(jnp.stack(pieces), order, axis=0)
    moved = lax.all_to_all(stacked, "expert", split_axis=0, concat_axis=0, tiled=True)
    moved = jnp.take(moved, order, axis=0)
    return [moved[i] for i in range(ranks)]


def routing_tables(expert_ids, route_weights, expert_list, capacity):
    matches = expert_ids[None, :, :] == expert_list[:, None, None]
    chosen = jnp.any(matches, axis=2)
    route_share = jnp.sum(jnp.where(matches, route_weights[None, :, :], F32(0.0)), axis=2)
    place = jnp.cumsum(chosen.astype(jnp.int32), axis=1) - 1
    slot_ids = jnp.arange(capacity, dtype=jnp.int32)
    route_table = chosen[:, None, :] & (place[:, None, :] == slot_ids[None, :, None])
    return route_table, route_share


def per_device(
    tokens, expert_ids, route_weights, gate_weight, up_weight, down_weight, gate_probe, up_probe
):
    tok_rows, width_dev = tokens.shape
    capacity = tok_rows // 2
    ranks = lax.axis_size("expert")
    per_expert = ranks // EXPERTS
    token_total = ranks * tok_rows
    me = lax.axis_index("dp").astype(jnp.int32).reshape(1)
    mine = lax.axis_index("expert") // per_expert
    expert_list = jnp.stack([mine, 1 - mine]).astype(expert_ids.dtype)

    route_table, route_share = routing_tables(expert_ids, route_weights, expert_list, capacity)
    spread = route_table.astype(F32) * route_share[:, None, :]
    slots = jnp.einsum(
        "ect,tf->ecf", route_table.astype(BF16), tokens, preferred_element_type=F32
    ).astype(BF16)
    slot_rows = jnp.concatenate(exchange([slots[i // per_expert] for i in range(ranks)]), axis=0)

    def core(parts):
        return [swap(part, "dp", 1) for part in parts]

    height, quarter = slot_rows.shape[0], down_weight.shape[0] // 4
    part_type = ((height, quarter), BF16)
    wide_type = ((height, quarter), F32)

    def far_sum(keep, got, after):
        (far,) = by_rows(far_rows, [keep, *got], [part_type], after)
        return far, swap(far, "dp", 2)

    halves = prefetch(me, [gate_weight, up_weight, gate_probe], (3, 2))
    send, keep = resident_products(slot_rows, halves[0], [])
    gate_far = (keep, core(send))
    send, keep = resident_products(slot_rows, halves[1], [keep])
    up_far = (keep, core(send))
    far, gate_across = far_sum(*gate_far, [keep])
    send, keep = resident_products(slot_rows, halves[2], [far])
    gate_tangent_far = (keep, core(send))
    far, up_across = far_sum(*up_far, [keep])
    send, near = stream_products(me, slot_rows, [gate_weight, up_weight], (1, 0), [far])
    near_got = core(send)
    far, gate_tangent_across = far_sum(*gate_tangent_far, [near])
    send, near_tangent = stream_products(
        me, slot_rows, [gate_probe, up_probe], (1, 0), [far, gate_across]
    )
    near_tangent_got = core(send)
    hidden, gate_value, up_value = by_rows(
        hidden_rows,
        [near, *near_got, gate_across, up_across],
        [part_type, wide_type, wide_type],
        [near_tangent, gate_tangent_across],
    )
    beside, across = swap(hidden, "dp", 1), swap(hidden, "dp", 2)
    send, keep = stream_products(
        me, slot_rows, [up_probe], (3, 2), [hidden]
    )
    got = core(send)
    (half,) = down_products(
        me, hidden, beside, down_weight, (0, 1), None, 1, F32, [keep]
    )
    far, up_tangent_across = far_sum(keep, got, [half])
    across = pass_on(across, [far])
    out = down_products(
        me, across, swap(across, "dp", 1), down_weight, (2, 3), half, ranks, BF16, [far]
    )
    came = exchange(out)

    hidden_tangent, gate_tangent, up_tangent = by_rows(
        tangent_rows,
        [
            near_tangent,
            *near_tangent_got,
            gate_tangent_across,
            up_tangent_across,
            gate_value,
            up_value,
        ],
        [part_type, wide_type, wide_type],
        [out[0], came[1]],
    )
    beside, across = swap(hidden_tangent, "dp", 1), swap(hidden_tangent, "dp", 2)
    (half,) = down_products(
        me, hidden_tangent, beside, down_weight, (0, 1), None, 1, F32, [hidden_tangent]
    )
    across = pass_on(across, [half])
    out = down_products(
        me, across, swap(across, "dp", 1), down_weight, (2, 3), half, ranks, BF16, []
    )
    came_tangent = exchange(out)
    cot = mix_products(came, spread, token_total, [out[0], came_tangent[1]])
    came = exchange([cot[i // per_expert] for i in range(ranks)])
    cot = mix_products(came_tangent, spread, token_total, [cot[0], came[1]])
    came += exchange([cot[i // per_expert] for i in range(ranks)])

    send, keep = back_products(me, came, down_weight, (3, 2), [])
    got = core(send)
    send, near = back_products(me, came, down_weight, (1, 0), [keep])
    pair_type = ((2, height, quarter), BF16)
    (far,) = by_rows(far_pair_rows, [keep, *got], [pair_type], [near])
    got = core(send)
    (terms,) = by_rows(
        term_rows,
        [near, swap(far, "dp", 2), *got, gate_value, up_value, gate_tangent, up_tangent],
        [pair_type],
        [far],
    )

    across, beside = swap(terms, "dp", 2), swap(terms, "dp", 1)
    *outputs, flag = outer_products(me, slot_rows, [terms, beside], (0, 1), None)
    across = pass_on(across, [flag])
    beyond = swap(across, "dp", 1)
    outputs = outer_products(me, slot_rows, [across], (2,), outputs)
    return tuple(outer_products(me, slot_rows, [beyond], (3,), outputs))


def solution(mesh):
    return jax.shard_map(
        per_device,
        mesh=mesh,
        in_specs=(
            P(("groups", "expert"), "dp"),
            P(("groups", "expert"), None),
            P(("groups", "expert"), None),
            P("dp", "expert"),
            P("dp", "expert"),
            P("expert", "dp"),
            P("dp", "expert"),
            P("dp", "expert"),
        ),
        out_specs=(P(("groups", "dp"), "expert"), P(("groups", "dp"), "expert")),
        check_vma=False,
    )
```

time: 142 us -> 127 us (0.89)
  waiting for transfers between devices: 43.3 us -> 32.6 us
  local copies, waits for them, and re-layouts: 9.7 us -> 0.05 us
  starting transfers between devices: 34.3 us -> 41.9 us
  other arithmetic: 3.42 us -> 1.21 us
  Pallas kernels: 47.2 us -> 49.4 us
  matrix products: 1.84 us -> 0.17 us
    ppermute x40 -> x53, waiting for transfers between devices: 43.3 us -> 32.6 us  [swap(): return lax.ppermute(value, axis, [(i, i ^ mask) for i in range(size)])]
    unnamed x46 -> x14, local copies, waits for them, and re-layouts: 9.58 us -> 0.04 us
    ppermute x40 -> x53, starting transfers between devices: 34.3 us -> 41.9 us  [swap(): return lax.ppermute(value, axis, [(i, i ^ mask) for i in range(size)])]
    pallas_call x17 -> x29, Pallas kernels: 47.2 us -> 49.4 us  [the longest x3 15 us: stream_products(): pl.pallas_call(functools.partial(stream_kernel, count, offsets), in_specs...]
    dot_general x4 -> x0, matrix products: 1.67 us -> none  [the longest x2 0.89 us: mix(): jnp.einsum('ect,ecf->tf', spread, sums, precision=lax.Precision.HIGHEST)]
  transfers between devices with their start and end apart: 40 -> 53, of which waited for: 15 -> 16; matrix products, arithmetic and copies ran while one was open for 2% -> 0% of each run, Pallas kernels for 28% -> 33%
where the time goes in v2:
time: 127 us
  Pallas kernels  49.4 us (39%)
  starting transfers between devices  41.9 us (33%)
  waiting for transfers between devices  32.6 us (26%)
  between operations  1.27 us (1%)
    ppermute x53, starting transfers between devices, swap(): return lax.ppermute(value, axis, [(i, i ^ mask) for i in range(size)])  41.9 us
    ppermute x53, waiting for transfers between devices, swap(): return lax.ppermute(value, axis, [(i, i ^ mask) for i in range(size)])  32.6 us
    pallas_call x3, Pallas kernels, stream_products(): pl.pallas_call(functools.partial(stream_kernel, count, offsets), in_specs...  15 us
    pallas_call x3, Pallas kernels, outer_products(): pl.pallas_call(functools.partial(outer_kernel, offsets), in_specs=[IN_SME...  12 us
    pallas_call x1, Pallas kernels, prefetch(): pl.pallas_call(functools.partial(prefetch_kernel, offsets), in_specs=[IN_...  6.55 us
    pallas_call x4, Pallas kernels, down_products(): pl.pallas_call(functools.partial(down_kernel, offsets, start is not None,...  4.74 us
    pallas_call x2, Pallas kernels, back_products(): pl.pallas_call(functools.partial(back_kernel, count, offsets), in_specs=[...  4.14 us
    pallas_call x3, Pallas kernels, resident_products(): pl.pallas_call(resident_kernel, in_specs=[IN_VMEM] * 2 + [ANYWHERE] * len...  3.61 us
  transfers between devices with their start and end apart: 53, of which 16 were waited for; matrix products, arithmetic and copies ran while one was open for 0% of the time, Pallas kernels for 33%

profile of v2, /device:TPU:0, one launch (start us, length us, event | category | flops | bytes accessed | tf_op | source)
XLA Modules:
  0.0 126.6 jit_solution(9923842294178556685)
XLA Ops:
  1.9 3.1 %collective-permute-start = (bf16[24,1536]{1,0:T(8,128)(2,1)S(1)}, bf16[24,1536]{1,0:T(8,128)(2,1)S(1)}, u32[]{:S(2)}, u32[]{:S(2)}) collective-permute-start(bf16[24,1536]{1,0:T(8,128)(2,1)S(1)} %get-tuple-element.118), channel_id=1, source_target_pairs={{0,4},{4,0},{8,12},{12,8},{1,5},{5,1},{9,13},{13,9},{2,6},{6,2},{1... | collective-permute-start | bytes 221192 | tf_op jit(solution)/shard_map/ppermute | solution.py:25
  5.0 2.5 %collective-permute-start.2 = (bf16[24,1536]{1,0:T(8,128)(2,1)S(1)}, bf16[24,1536]{1,0:T(8,128)(2,1)S(1)}, u32[]{:S(2)}, u32[]{:S(2)}) collective-permute-start(bf16[24,1536]{1,0:T(8,128)(2,1)S(1)} %get-tuple-element.119), channel_id=1, source_target_pairs={{0,12},{4,8},{8,4},{12,0},{1,13},{5,9},{9,5},{13,1},{2,14},{6,10},... | collective-permute-start | bytes 221192 | tf_op jit(solution)/shard_map/ppermute | solution.py:25
  7.6 6.6 %shard_map.95 = (bf16[2,1536,1024]{2,1,0:T(8,128)(2,1)S(1)}, bf16[2,1536,1024]{2,1,0:T(8,128)(2,1)S(1)}, bf16[2,1536,1024]{2,1,0:T(8,128)(2,1)S(1)}) custom-call(s32[1]{0:T(128)} %bitcast.me_ref, bf16[1536,4096]{1,0:T(8,128)(2,1)} %refs_0_.5, bf16[1536,4096]{1,0:T(8,128)(2,1)} %refs_1_.4, bf16[1536,4096]{1,0:T(8,128)(2,1)} %refs_0_.6), custom_call_target="tpu_custom_call" | custom-call | flops 1 | bytes 37748736 | tf_op jit(solution)/shard_map/pallas_call | solution.py:61
  21.6 5.4 %shard_map.101 = (bf16[48,1024]{1,0:T(8,128)(2,1)S(1)}, bf16[48,1024]{1,0:T(8,128)(2,1)S(1)}, bf16[48,1024]{1,0:T(8,128)(2,1)S(1)}, bf16[48,1024]{1,0:T(8,128)(2,1)S(1)}, bf16[2,96,1024]{2,1,0:T(8,128)(2,1)S(1)}) custom-call(s32[1]{0:T(128)} %bitcast.me_ref, bf16[96,1536]{1,0:T(8,128)(2,1)S(1)} %pad_maximum_fusion.rows_ref.tokens_ref, ...), custom_call_target="tpu_custom_call" | custom-call | flops 1 | bytes 1 | tf_op jit(solution)/shard_map/pallas_call | solution.py:148
  27.8 1.6 %collective-permute-start.15 = (bf16[96,1024]{1,0:T(8,128)(2,1)S(1)}, bf16[96,1024]{1,0:T(8,128)(2,1)S(1)}, u32[]{:S(2)}, u32[]{:S(2)}) collective-permute-start(bf16[96,1024]{1,0:T(8,128)(2,1)S(1)} %shard_map.102.refs_2_), channel_id=1, source_target_pairs={{0,2},{1,3},{2,0},{3,1},{4,6},{5,7},{6,4},{7,5},{8,10},{9,11},{10,... | collective-permute-start | bytes 589832 | tf_op jit(solution)/shard_map/ppermute | solution.py:25
  29.9 6.0 %shard_map.103 = (bf16[48,1024]{1,0:T(8,128)(2,1)S(1)}, bf16[48,1024]{1,0:T(8,128)(2,1)S(1)}, bf16[48,1024]{1,0:T(8,128)(2,1)S(1)}, bf16[48,1024]{1,0:T(8,128)(2,1)S(1)}, bf16[2,96,1024]{2,1,0:T(8,128)(2,1)S(1)}) custom-call(s32[1]{0:T(128)} %bitcast.me_ref, bf16[96,1536]{1,0:T(8,128)(2,1)S(1)} %pad_maximum_fusion.rows_ref.tokens_ref, ...), custom_call_target="tpu_custom_call" | custom-call | flops 1 | bytes 1 | tf_op jit(solution)/shard_map/pallas_call | solution.py:148
  35.9 2.7 %collective-permute-done.15.refs_8_.refs_5_ = bf16[96,1024]{1,0:T(8,128)(2,1)S(1)} collective-permute-done((bf16[96,1024]{1,0:T(8,128)(2,1)S(1)}, bf16[96,1024]{1,0:T(8,128)(2,1)S(1)}, u32[]{:S(2)}, u32[]{:S(2)}) %collective-permute-start.15) | collective-permute-done | bytes 196640 | tf_op jit(solution)/shard_map/ppermute | solution.py:25
  39.5 3.7 %shard_map.105 = (bf16[48,1024]{1,0:T(8,128)(2,1)S(1)}, bf16[48,1024]{1,0:T(8,128)(2,1)S(1)}, bf16[1,96,1024]{2,1,0:T(8,128)(2,1)S(1)}) custom-call(s32[1]{0:T(128)} %bitcast.me_ref, bf16[96,1536]{1,0:T(8,128)(2,1)S(1)} %pad_maximum_fusion.rows_ref.tokens_ref, bf16[1536,4096]{1,0:T(8,128)(2,1)} %refs_0_.7, ...), custom_call_target="tpu_custom_call" | custom-call | flops 1 | bytes 1 | tf_op jit(solution)/shard_map/pallas_call | solution.py:148
  50.6 3.0 %collective-permute-done.28.refs_6_ = bf16[96,1024]{1,0:T(8,128)(2,1)S(1)} collective-permute-done((bf16[96,1024]{1,0:T(8,128)(2,1)S(1)}, bf16[96,1024]{1,0:T(8,128)(2,1)S(1)}, u32[]{:S(2)}, u32[]{:S(2)}) %collective-permute-start.28) | collective-permute-done | bytes 196640 | tf_op jit(solution)/shard_map/ppermute | solution.py:25
  56.6 4.7 %collective-permute-done.29.value_ref = bf16[96,1024]{1,0:T(8,128)(2,1)S(1)} collective-permute-done((bf16[96,1024]{1,0:T(8,128)(2,1)S(1)}, bf16[96,1024]{1,0:T(8,128)(2,1)S(1)}, u32[]{:S(2)}, u32[]{:S(2)}) %collective-permute-start.29) | collective-permute-done | bytes 196640 | tf_op jit(solution)/shard_map/ppermute | solution.py:25
  61.6 2.5 %collective-permute-start.22 = (bf16[24,1536]{1,0:T(8,128)(2,1)S(1)}, bf16[24,1536]{1,0:T(8,128)(2,1)S(1)}, u32[]{:S(2)}, u32[]{:S(2)}) collective-permute-start(bf16[24,1536]{1,0:T(8,128)(2,1)S(1)} %get-tuple-element.84), channel_id=1, source_target_pairs={{0,8},{4,12},{8,0},{12,4},{1,9},{5,13},{9,1},{13,5},{2,10},{6,14},... | collective-permute-start | bytes 221192 | tf_op jit(solution)/shard_map/ppermute | solution.py:25
  66.8 3.1 %collective-permute-start.36 = (bf16[24,1536]{1,0:T(8,128)(2,1)S(1)}, bf16[24,1536]{1,0:T(8,128)(2,1)S(1)}, u32[]{:S(2)}, u32[]{:S(2)}) collective-permute-start(bf16[24,1536]{1,0:T(8,128)(2,1)S(1)} %get-tuple-element.97), channel_id=1, source_target_pairs={{0,8},{4,12},{8,0},{12,4},{1,9},{5,13},{9,1},{13,5},{2,10},{6,14},... | collective-permute-start | bytes 221192 | tf_op jit(solution)/shard_map/ppermute | solution.py:25
  73.3 3.0 %collective-permute-start.33 = (bf16[24,1536]{1,0:T(8,128)(2,1)S(1)}, bf16[24,1536]{1,0:T(8,128)(2,1)S(1)}, u32[]{:S(2)}, u32[]{:S(2)}) collective-permute-start(bf16[24,1536]{1,0:T(8,128)(2,1)S(1)} %get-tuple-element.95.refs_5_.refs_0_), channel_id=1, source_target_pairs={{0,4},{4,0},{8,12},{12,8},{1,5},{5,1},{9,13},{13,9},{2,6},{6,2},{1... | collective-permute-start | bytes 221192 | tf_op jit(solution)/shard_map/ppermute | solution.py:25
  76.3 3.4 %collective-permute-start.35 = (bf16[24,1536]{1,0:T(8,128)(2,1)S(1)}, bf16[24,1536]{1,0:T(8,128)(2,1)S(1)}, u32[]{:S(2)}, u32[]{:S(2)}) collective-permute-start(bf16[24,1536]{1,0:T(8,128)(2,1)S(1)} %get-tuple-element.96), channel_id=1, source_target_pairs={{0,12},{4,8},{8,4},{12,0},{1,13},{5,9},{9,5},{13,1},{2,14},{6,10},... | collective-permute-start | bytes 221192 | tf_op jit(solution)/shard_map/ppermute | solution.py:25
  80.7 2.7 %collective-permute-start.40 = (bf16[24,1536]{1,0:T(8,128)(2,1)S(1)}, bf16[24,1536]{1,0:T(8,128)(2,1)S(1)}, u32[]{:S(2)}, u32[]{:S(2)}) collective-permute-start(bf16[24,1536]{1,0:T(8,128)(2,1)S(1)} %get-tuple-element.100), channel_id=1, source_target_pairs={{0,12},{4,8},{8,4},{12,0},{1,13},{5,9},{9,5},{13,1},{2,14},{6,10},... | collective-permute-start | bytes 221192 | tf_op jit(solution)/shard_map/ppermute | solution.py:25
  85.1 2.6 %collective-permute-done.34.refs_2_ = bf16[24,1536]{1,0:T(8,128)(2,1)S(1)} collective-permute-done((bf16[24,1536]{1,0:T(8,128)(2,1)S(1)}, bf16[24,1536]{1,0:T(8,128)(2,1)S(1)}, u32[]{:S(2)}, u32[]{:S(2)}) %collective-permute-start.34) | collective-permute-done | bytes 73760 | tf_op jit(solution)/shard_map/ppermute | solution.py:25
  87.7 3.2 %collective-permute-done.39.refs_6_ = bf16[24,1536]{1,0:T(8,128)(2,1)S(1)} collective-permute-done((bf16[24,1536]{1,0:T(8,128)(2,1)S(1)}, bf16[24,1536]{1,0:T(8,128)(2,1)S(1)}, u32[]{:S(2)}, u32[]{:S(2)}) %collective-permute-start.39) | collective-permute-done | bytes 73760 | tf_op jit(solution)/shard_map/ppermute | solution.py:25
  90.9 2.1 %shard_map.116 = (bf16[48,1024]{1,0:T(8,128)(2,1)S(1)}, bf16[48,1024]{1,0:T(8,128)(2,1)S(1)}, bf16[48,1024]{1,0:T(8,128)(2,1)S(1)}, bf16[48,1024]{1,0:T(8,128)(2,1)S(1)}, bf16[2,96,1024]{2,1,0:T(8,128)(2,1)S(1)}) custom-call(s32[1]{0:T(128)} %bitcast.me_ref, bf16[24,1536]{1,0:T(8,128)(2,1)S(1)} %get-tuple-element.95.refs_5_.refs_0_, ...), custom_call_target="tpu_custom_call" | custom-call | flops 1 | bytes 1 | tf_op jit(solution)/shard_map/pallas_call | solution.py:186
  94.0 2.1 %shard_map.117 = (bf16[48,1024]{1,0:T(8,128)(2,1)S(1)}, bf16[48,1024]{1,0:T(8,128)(2,1)S(1)}, bf16[48,1024]{1,0:T(8,128)(2,1)S(1)}, bf16[48,1024]{1,0:T(8,128)(2,1)S(1)}, bf16[2,96,1024]{2,1,0:T(8,128)(2,1)S(1)}) custom-call(s32[1]{0:T(128)} %bitcast.me_ref, bf16[24,1536]{1,0:T(8,128)(2,1)S(1)} %get-tuple-element.95.refs_5_.refs_0_, ...), custom_call_target="tpu_custom_call" | custom-call | flops 1 | bytes 1 | tf_op jit(solution)/shard_map/pallas_call | solution.py:186
  99.6 7.8 %collective-permute-done.45.refs_1_ = bf16[2,96,1024]{2,1,0:T(8,128)(2,1)S(1)} collective-permute-done((bf16[2,96,1024]{2,1,0:T(8,128)(2,1)S(1)}, bf16[2,96,1024]{2,1,0:T(8,128)(2,1)S(1)}, u32[]{:S(2)}, u32[]{:S(2)}) %collective-permute-start.45) | collective-permute-done | bytes 393248 | tf_op jit(solution)/shard_map/ppermute | solution.py:25
  109.7 5.3 %shard_map.120 = (bf16[1536,4096]{1,0:T(8,128)(2,1)}, bf16[1536,4096]{1,0:T(8,128)(2,1)}, f32[8,128]{1,0:T(8,128)S(1)}) custom-call(s32[1]{0:T(128)} %bitcast.me_ref, bf16[96,1536]{1,0:T(8,128)(2,1)S(1)} %pad_maximum_fusion.rows_ref.tokens_ref, bf16[2,96,1024]{2,1,0:T(8,128)(2,1)S(1)} %shard_map.119.refs_0_, ...), custom_call_target="tpu_custom_call" | custom-call | flops 1 | bytes 1 | tf_op jit(solution)/shard_map/pallas_call | solution.py:301
  115.0 4.5 %collective-permute-done.50.value_ref = bf16[2,96,1024]{2,1,0:T(8,128)(2,1)S(1)} collective-permute-done((bf16[2,96,1024]{2,1,0:T(8,128)(2,1)S(1)}, bf16[2,96,1024]{2,1,0:T(8,128)(2,1)S(1)}, u32[]{:S(2)}, u32[]{:S(2)}) %collective-permute-start.50) | collective-permute-done | bytes 393248 | tf_op jit(solution)/shard_map/ppermute | solution.py:25
  119.6 3.4 %shard_map.122 = (bf16[1536,4096]{1,0:T(8,128)(2,1)}, bf16[1536,4096]{1,0:T(8,128)(2,1)}) custom-call(s32[1]{0:T(128)} %bitcast.me_ref, bf16[96,1536]{1,0:T(8,128)(2,1)S(1)} %pad_maximum_fusion.rows_ref.tokens_ref, bf16[2,96,1024]{2,1,0:T(8,128)(2,1)S(1)} %shard_map.121.refs_0_, ...), custom_call_target="tpu_custom_call", output_to_operand_aliasing={{0}: (3, {}), {1}: (4, {})} | custom-call | flops 1 | bytes 1 | tf_op jit(solution)/shard_map/pallas_call | solution.py:301
  123.0 3.4 %shard_map.123 = (bf16[1536,4096]{1,0:T(8,128)(2,1)}, bf16[1536,4096]{1,0:T(8,128)(2,1)}) custom-call(s32[1]{0:T(128)} %bitcast.me_ref, bf16[96,1536]{1,0:T(8,128)(2,1)S(1)} %pad_maximum_fusion.rows_ref.tokens_ref, bf16[2,96,1024]{2,1,0:T(8,128)(2,1)S(1)} %collective-permute-done.52.refs_0_, ...), custom_call_target="tpu_custom_call", output_to_operand_aliasing={{0}: (3, {}), {1}: (4, {})} | custom-call | flops 1 | bytes 1 | tf_op jit(solution)/shard_map/pallas_call | solution.py:301
  (136 shorter events, 37.3 us)
Async XLA Ops:
  1.9 12.2 %collective-permute-start = (bf16[24,1536]{1,0:T(8,128)(2,1)S(1)}, bf16[24,1536]{1,0:T(8,128)(2,1)S(1)}, u32[]{:S(2)}, u32[]{:S(2)}) collective-permute-start(bf16[24,1536]{1,0:T(8,128)(2,1)S(1)} %get-tuple-element.118), channel_id=1, source_target_pairs={{0,4},{4,0},{8,12},{12,8},{1,5},{5,1},{9,13},{13,9},{2,6},{6,2},{1... | collective-permute-start | bytes 221192 | tf_op jit(solution)/shard_map/ppermute | solution.py:25
  5.0 9.2 %collective-permute-start.2 = (bf16[24,1536]{1,0:T(8,128)(2,1)S(1)}, bf16[24,1536]{1,0:T(8,128)(2,1)S(1)}, u32[]{:S(2)}, u32[]{:S(2)}) collective-permute-start(bf16[24,1536]{1,0:T(8,128)(2,1)S(1)} %get-tuple-element.119), channel_id=1, source_target_pairs={{0,12},{4,8},{8,4},{12,0},{1,13},{5,9},{9,5},{13,1},{2,14},{6,10},... | collective-permute-start | bytes 221192 | tf_op jit(solution)/shard_map/ppermute | solution.py:25
  7.5 7.1 %collective-permute-start.1 = (bf16[24,1536]{1,0:T(8,128)(2,1)S(1)}, bf16[24,1536]{1,0:T(8,128)(2,1)S(1)}, u32[]{:S(2)}, u32[]{:S(2)}) collective-permute-start(bf16[24,1536]{1,0:T(8,128)(2,1)S(1)} %get-tuple-element.119), channel_id=1, source_target_pairs={{0,8},{4,12},{8,0},{12,4},{1,9},{5,13},{9,1},{13,5},{2,10},{6,14},... | collective-permute-start | bytes 221192 | tf_op jit(solution)/shard_map/ppermute | solution.py:25
  18.2 11.6 %collective-permute-start.11 = (bf16[96,1024]{1,0:T(8,128)(2,1)S(1)}, bf16[96,1024]{1,0:T(8,128)(2,1)S(1)}, u32[]{:S(2)}, u32[]{:S(2)}) collective-permute-start(bf16[96,1024]{1,0:T(8,128)(2,1)S(1)} %shard_map.98.refs_0_), channel_id=1, source_target_pairs={{0,2},{1,3},{2,0},{3,1},{4,6},{5,7},{6,4},{7,5},{8,10},{9,11},{10,... | collective-permute-start | bytes 589832 | tf_op jit(solution)/shard_map/ppermute | solution.py:25
  21.0 6.7 %collective-permute-start.13 = (bf16[48,1024]{1,0:T(8,128)(2,1)S(1)}, bf16[48,1024]{1,0:T(8,128)(2,1)S(1)}, u32[]{:S(2)}, u32[]{:S(2)}) collective-permute-start(bf16[48,1024]{1,0:T(8,128)(2,1)S(1)} %get-tuple-element.75), channel_id=1, source_target_pairs={{0,1},{1,0},{2,3},{3,2},{4,5},{5,4},{6,7},{7,6},{8,9},{9,8},{10,11... | collective-permute-start | bytes 294920 | tf_op jit(solution)/shard_map/ppermute | solution.py:25
  21.1 6.6 %collective-permute-start.14 = (bf16[48,1024]{1,0:T(8,128)(2,1)S(1)}, bf16[48,1024]{1,0:T(8,128)(2,1)S(1)}, u32[]{:S(2)}, u32[]{:S(2)}) collective-permute-start(bf16[48,1024]{1,0:T(8,128)(2,1)S(1)} %get-tuple-element.76), channel_id=1, source_target_pairs={{0,1},{1,0},{2,3},{3,2},{4,5},{5,4},{6,7},{7,6},{8,9},{9,8},{10,11... | collective-permute-start | bytes 294920 | tf_op jit(solution)/shard_map/ppermute | solution.py:25
  27.2 8.8 %collective-permute-start.12 = (bf16[96,1024]{1,0:T(8,128)(2,1)S(1)}, bf16[96,1024]{1,0:T(8,128)(2,1)S(1)}, u32[]{:S(2)}, u32[]{:S(2)}) collective-permute-start(bf16[96,1024]{1,0:T(8,128)(2,1)S(1)} %shard_map.100.refs_2_), channel_id=1, source_target_pairs={{0,2},{1,3},{2,0},{3,1},{4,6},{5,7},{6,4},{7,5},{8,10},{9,11},{10,... | collective-permute-start | bytes 589832 | tf_op jit(solution)/shard_map/ppermute | solution.py:25
  27.8 10.9 %collective-permute-start.15 = (bf16[96,1024]{1,0:T(8,128)(2,1)S(1)}, bf16[96,1024]{1,0:T(8,128)(2,1)S(1)}, u32[]{:S(2)}, u32[]{:S(2)}) collective-permute-start(bf16[96,1024]{1,0:T(8,128)(2,1)S(1)} %shard_map.102.refs_2_), channel_id=1, source_target_pairs={{0,2},{1,3},{2,0},{3,1},{4,6},{5,7},{6,4},{7,5},{8,10},{9,11},{10,... | collective-permute-start | bytes 589832 | tf_op jit(solution)/shard_map/ppermute | solution.py:25
  29.3 6.6 %collective-permute-start.8 = (bf16[48,1024]{1,0:T(8,128)(2,1)S(1)}, bf16[48,1024]{1,0:T(8,128)(2,1)S(1)}, u32[]{:S(2)}, u32[]{:S(2)}) collective-permute-start(bf16[48,1024]{1,0:T(8,128)(2,1)S(1)} %get-tuple-element.72), channel_id=1, source_target_pairs={{0,1},{1,0},{2,3},{3,2},{4,5},{5,4},{6,7},{7,6},{8,9},{9,8},{10,11... | collective-permute-start | bytes 294920 | tf_op jit(solution)/shard_map/ppermute | solution.py:25
  29.3 6.6 %collective-permute-start.9 = (bf16[48,1024]{1,0:T(8,128)(2,1)S(1)}, bf16[48,1024]{1,0:T(8,128)(2,1)S(1)}, u32[]{:S(2)}, u32[]{:S(2)}) collective-permute-start(bf16[48,1024]{1,0:T(8,128)(2,1)S(1)} %get-tuple-element.73), channel_id=1, source_target_pairs={{0,1},{1,0},{2,3},{3,2},{4,5},{5,4},{6,7},{7,6},{8,9},{9,8},{10,11... | collective-permute-start | bytes 294920 | tf_op jit(solution)/shard_map/ppermute | solution.py:25
  38.9 7.3 %collective-permute-start.16 = (bf16[96,1024]{1,0:T(8,128)(2,1)S(1)}, bf16[96,1024]{1,0:T(8,128)(2,1)S(1)}, u32[]{:S(2)}, u32[]{:S(2)}) collective-permute-start(bf16[96,1024]{1,0:T(8,128)(2,1)S(1)} %get-tuple-element.78.refs_1_.first_ref), channel_id=1, source_target_pairs={{0,2},{1,3},{2,0},{3,1},{4,6},{5,7},{6,4},{7,5},{8,10},{9,11},{10,... | collective-permute-start | bytes 589832 | tf_op jit(solution)/shard_map/ppermute | solution.py:25
  46.3 7.3 %collective-permute-start.28 = (bf16[96,1024]{1,0:T(8,128)(2,1)S(1)}, bf16[96,1024]{1,0:T(8,128)(2,1)S(1)}, u32[]{:S(2)}, u32[]{:S(2)}) collective-permute-start(bf16[96,1024]{1,0:T(8,128)(2,1)S(1)} %shard_map.107.refs_0_.rest_1_), channel_id=1, source_target_pairs={{0,2},{1,3},{2,0},{3,1},{4,6},{5,7},{6,4},{7,5},{8,10},{9,11},{10,... | collective-permute-start | bytes 589832 | tf_op jit(solution)/shard_map/ppermute | solution.py:25
  54.0 7.3 %collective-permute-start.29 = (bf16[96,1024]{1,0:T(8,128)(2,1)S(1)}, bf16[96,1024]{1,0:T(8,128)(2,1)S(1)}, u32[]{:S(2)}, u32[]{:S(2)}) collective-permute-start(bf16[96,1024]{1,0:T(8,128)(2,1)S(1)} %get-tuple-element.92.first_ref.rest_0_), channel_id=1, source_target_pairs={{0,2},{1,3},{2,0},{3,1},{4,6},{5,7},{6,4},{7,5},{8,10},{9,11},{10,... | collective-permute-start | bytes 589832 | tf_op jit(solution)/shard_map/ppermute | solution.py:25
  61.6 9.7 %collective-permute-start.22 = (bf16[24,1536]{1,0:T(8,128)(2,1)S(1)}, bf16[24,1536]{1,0:T(8,128)(2,1)S(1)}, u32[]{:S(2)}, u32[]{:S(2)}) collective-permute-start(bf16[24,1536]{1,0:T(8,128)(2,1)S(1)} %get-tuple-element.84), channel_id=1, source_target_pairs={{0,8},{4,12},{8,0},{12,4},{1,9},{5,13},{9,1},{13,5},{2,10},{6,14},... | collective-permute-start | bytes 221192 | tf_op jit(solution)/shard_map/ppermute | solution.py:25
  64.1 7.2 %collective-permute-start.23 = (bf16[24,1536]{1,0:T(8,128)(2,1)S(1)}, bf16[24,1536]{1,0:T(8,128)(2,1)S(1)}, u32[]{:S(2)}, u32[]{:S(2)}) collective-permute-start(bf16[24,1536]{1,0:T(8,128)(2,1)S(1)} %get-tuple-element.85), channel_id=1, source_target_pairs={{0,12},{4,8},{8,4},{12,0},{1,13},{5,9},{9,5},{13,1},{2,14},{6,10},... | collective-permute-start | bytes 221192 | tf_op jit(solution)/shard_map/ppermute | solution.py:25
  66.8 12.8 %collective-permute-start.36 = (bf16[24,1536]{1,0:T(8,128)(2,1)S(1)}, bf16[24,1536]{1,0:T(8,128)(2,1)S(1)}, u32[]{:S(2)}, u32[]{:S(2)}) collective-permute-start(bf16[24,1536]{1,0:T(8,128)(2,1)S(1)} %get-tuple-element.97), channel_id=1, source_target_pairs={{0,8},{4,12},{8,0},{12,4},{1,9},{5,13},{9,1},{13,5},{2,10},{6,14},... | collective-permute-start | bytes 221192 | tf_op jit(solution)/shard_map/ppermute | solution.py:25
  69.9 9.7 %collective-permute-start.37 = (bf16[24,1536]{1,0:T(8,128)(2,1)S(1)}, bf16[24,1536]{1,0:T(8,128)(2,1)S(1)}, u32[]{:S(2)}, u32[]{:S(2)}) collective-permute-start(bf16[24,1536]{1,0:T(8,128)(2,1)S(1)} %get-tuple-element.98), channel_id=1, source_target_pairs={{0,12},{4,8},{8,4},{12,0},{1,13},{5,9},{9,5},{13,1},{2,14},{6,10},... | collective-permute-start | bytes 221192 | tf_op jit(solution)/shard_map/ppermute | solution.py:25
  76.3 8.8 %collective-permute-start.35 = (bf16[24,1536]{1,0:T(8,128)(2,1)S(1)}, bf16[24,1536]{1,0:T(8,128)(2,1)S(1)}, u32[]{:S(2)}, u32[]{:S(2)}) collective-permute-start(bf16[24,1536]{1,0:T(8,128)(2,1)S(1)} %get-tuple-element.96), channel_id=1, source_target_pairs={{0,12},{4,8},{8,4},{12,0},{1,13},{5,9},{9,5},{13,1},{2,14},{6,10},... | collective-permute-start | bytes 221192 | tf_op jit(solution)/shard_map/ppermute | solution.py:25
  79.7 8.0 %collective-permute-start.34 = (bf16[24,1536]{1,0:T(8,128)(2,1)S(1)}, bf16[24,1536]{1,0:T(8,128)(2,1)S(1)}, u32[]{:S(2)}, u32[]{:S(2)}) collective-permute-start(bf16[24,1536]{1,0:T(8,128)(2,1)S(1)} %get-tuple-element.96), channel_id=1, source_target_pairs={{0,8},{4,12},{8,0},{12,4},{1,9},{5,13},{9,1},{13,5},{2,10},{6,14},... | collective-permute-start | bytes 221192 | tf_op jit(solution)/shard_map/ppermute | solution.py:25
  80.7 7.0 %collective-permute-start.40 = (bf16[24,1536]{1,0:T(8,128)(2,1)S(1)}, bf16[24,1536]{1,0:T(8,128)(2,1)S(1)}, u32[]{:S(2)}, u32[]{:S(2)}) collective-permute-start(bf16[24,1536]{1,0:T(8,128)(2,1)S(1)} %get-tuple-element.100), channel_id=1, source_target_pairs={{0,12},{4,8},{8,4},{12,0},{1,13},{5,9},{9,5},{13,1},{2,14},{6,10},... | collective-permute-start | bytes 221192 | tf_op jit(solution)/shard_map/ppermute | solution.py:25
  83.4 7.5 %collective-permute-start.39 = (bf16[24,1536]{1,0:T(8,128)(2,1)S(1)}, bf16[24,1536]{1,0:T(8,128)(2,1)S(1)}, u32[]{:S(2)}, u32[]{:S(2)}) collective-permute-start(bf16[24,1536]{1,0:T(8,128)(2,1)S(1)} %get-tuple-element.100), channel_id=1, source_target_pairs={{0,8},{4,12},{8,0},{12,4},{1,9},{5,13},{9,1},{13,5},{2,10},{6,14},... | collective-permute-start | bytes 221192 | tf_op jit(solution)/shard_map/ppermute | solution.py:25
  83.8 7.1 %collective-permute-start.38 = (bf16[24,1536]{1,0:T(8,128)(2,1)S(1)}, bf16[24,1536]{1,0:T(8,128)(2,1)S(1)}, u32[]{:S(2)}, u32[]{:S(2)}) collective-permute-start(bf16[24,1536]{1,0:T(8,128)(2,1)S(1)} %get-tuple-element.99.refs_4_), channel_id=1, source_target_pairs={{0,4},{4,0},{8,12},{12,8},{1,5},{5,1},{9,13},{13,9},{2,6},{6,2},{1... | collective-permute-start | bytes 221192 | tf_op jit(solution)/shard_map/ppermute | solution.py:25
  96.2 11.2 %collective-permute-start.45 = (bf16[2,96,1024]{2,1,0:T(8,128)(2,1)S(1)}, bf16[2,96,1024]{2,1,0:T(8,128)(2,1)S(1)}, u32[]{:S(2)}, u32[]{:S(2)}) collective-permute-start(bf16[2,96,1024]{2,1,0:T(8,128)(2,1)S(1)} %shard_map.118.refs_10_), channel_id=1, source_target_pairs={{0,2},{1,3},{2,0},{3,1},{4,6},{5,7},{6,4},{7,5},{8,10},{9,11},{10,... | collective-permute-start | bytes 1179656 | tf_op jit(solution)/shard_map/ppermute | solution.py:25
  108.0 11.5 %collective-permute-start.50 = (bf16[2,96,1024]{2,1,0:T(8,128)(2,1)S(1)}, bf16[2,96,1024]{2,1,0:T(8,128)(2,1)S(1)}, u32[]{:S(2)}, u32[]{:S(2)}) collective-permute-start(bf16[2,96,1024]{2,1,0:T(8,128)(2,1)S(1)} %shard_map.119.refs_0_), channel_id=1, source_target_pairs={{0,2},{1,3},{2,0},{3,1},{4,6},{5,7},{6,4},{7,5},{8,10},{9,11},{10,... | collective-permute-start | bytes 1179656 | tf_op jit(solution)/shard_map/ppermute | solution.py:25
  (36 other events, 151.6 us)

commit v3 on v2

--- a/solution.py
+++ b/solution.py
@@ -161,38 +161,47 @@
     return jnp.concatenate([piece[...].astype(F32) for piece in pieces], axis=0)
 
 
-def back_kernel(count, offsets, me_ref, *refs):
-    pieces, weight_ref = refs[:count], refs[count]
-    sends, (keep_ref, turned_ref) = refs[-2 - 2 * PARTS : -2], refs[-2:]
-    unused, height, quarter = keep_ref.shape
-    sub = sub_width(quarter)
+def back_kernel(count, jobs, width, me_ref, *refs):
+    pieces, weight_ref, turned_ref = refs[:count], refs[count], refs[-1]
+    each = 3
+    outs = refs[-1 - each * len(jobs) : -1]
+    sub = sub_width(width)
     turned_ref[...] = stacked(pieces).T.astype(BF16)
-    for p, offset in enumerate(offsets):
-        base = (me_ref[0] ^ offset) * quarter
-        for c in range(0, quarter, sub):
-            piece = weight_ref[pl.ds(pl.multiple_of(base + c, sub), sub), :]
-            product = jnp.dot(piece, turned_ref[...], preferred_element_type=F32).T
-            if p == 0:
-                put([ref.at[:, c : c + sub] for ref in sends], sends[0].shape[0], product)
-            else:
-                keep_ref[0, :, c : c + sub] = product[:height].astype(BF16)
-                keep_ref[1, :, c : c + sub] = product[height:].astype(BF16)
-
-
-def back_products(me, pieces, weight, offsets, after):
+    for job, (offsets, chunk, chunks) in enumerate(jobs):
+        sends, keep_ref = outs[each * job : each * job + each - 1], outs[each * job + each - 1]
+        height = keep_ref.shape[1]
+        for p, offset in enumerate(offsets):
+            base = (me_ref[0] ^ offset) * (width * chunks) + chunk * width
+            for c in range(0, width, sub):
+                piece = weight_ref[pl.ds(pl.multiple_of(base + c, sub), sub), :]
+                product = jnp.dot(piece, turned_ref[...], preferred_element_type=F32).T
+                if p == 0:
+                    put([ref.at[:, c : c + sub] for ref in sends], height, product)
+                else:
+                    keep_ref[0, :, c : c + sub] = product[:height].astype(BF16)
+                    keep_ref[1, :, c : c + sub] = product[height:].astype(BF16)
+
+
+def back_products(me, pieces, weight, offsets, chunk_list, chunks, after):
     count, (rows, depth) = len(pieces), pieces[0].shape
-    height, quarter = count * rows // 2, weight.shape[0] // 4
-    shapes = result_shapes(2, height, quarter)
-    *send, keep = pl.pallas_call(
-        functools.partial(back_kernel, count, offsets),
+    height, width = count * rows // 2, weight.shape[0] // (4 * chunks)
+    part = jax.ShapeDtypeStruct((height, width), BF16)
+    shapes = [part, part, jax.ShapeDtypeStruct((2, height, width), BF16)]
+    each = len(shapes)
+    jobs = [(offsets, chunk, chunks) for chunk in chunk_list]
+    results = pl.pallas_call(
+        functools.partial(back_kernel, count, jobs, width),
         in_specs=[IN_SMEM] + [IN_VMEM] * (count + 1) + [ANYWHERE] * len(after),
-        out_specs=[IN_VMEM] * len(shapes),
-        out_shape=shapes,
+        out_specs=[IN_VMEM] * (each * len(jobs)),
+        out_shape=shapes * len(jobs),
         scratch_shapes=[pltpu.VMEM((depth, 2 * height), BF16)],
         compiler_params=params(8 * MIB),
         cost_estimate=cost(1, 1),
     )(me, *pieces, weight, *after)
-    return send, keep
+    return [
+        (results[each * i : each * i + each - 1], results[each * i + each - 1])
+        for i in range(len(jobs))
+    ]
 
 
 def down_kernel(offsets, has_start, pieces, me_ref, first_ref, second_ref, weight_ref, *rest):
@@ -260,20 +269,20 @@
     )(*pieces, spread, *after)
 
 
-def outer_kernel(offsets, me_ref, tokens_ref, *refs):
-    terms, (turned_ref, slots_ref, sems) = refs[: len(offsets)], refs[-3:]
-    outs = refs[-5:-3]
-    if len(offsets) == 2:
-        outs, flag_ref = refs[-6:-4], refs[-4]
-        flag_ref[...] = jnp.zeros_like(flag_ref)
-    quarter = terms[0].shape[2]
+def outer_kernel(places, chunks, flags, me_ref, tokens_ref, *refs):
+    terms = refs[: len(places)]
+    outs, (turned_ref, slots_ref, sems) = refs[-5:-3], refs[-3:]
+    if flags:
+        outs = refs[-6:-4]
+        refs[-4][...] = jnp.zeros_like(refs[-4])
+    width = terms[0].shape[2]
     slots, unused, sub = slots_ref.shape
     turned_ref[...] = tokens_ref[...].astype(F32).T.astype(BF16)
     copies = []
-    for term_ref, offset in zip(terms, offsets):
-        base = (me_ref[0] ^ offset) * quarter
+    for term_ref, (offset, chunk) in zip(terms, places):
+        base = (me_ref[0] ^ offset) * (width * chunks) + chunk * width
         for k in range(2):
-            for c in range(0, quarter, sub):
+            for c in range(0, width, sub):
                 slot = len(copies) % slots
                 if len(copies) >= slots:
                     copies[-slots].wait()
@@ -290,19 +299,21 @@
         copy.wait()
 
 
-def outer_products(me, tokens, terms, offsets, outputs):
+def outer_products(me, tokens, terms, places, chunks, outputs, after=()):
     height, width = tokens.shape
-    quarter = terms[0].shape[2]
-    sub = sub_width(quarter)
-    slots = min(4, 2 * len(terms) * (quarter // sub))
+    columns = terms[0].shape[2]
+    sub = sub_width(columns)
+    slots = min(4, 2 * len(terms) * (columns // sub))
     operands = [tokens, *terms]
     given = [] if outputs is None else list(outputs)
-    flags = len(offsets) - 1
+    flags = int(outputs is None)
     return pl.pallas_call(
-        functools.partial(outer_kernel, offsets),
-        in_specs=[IN_SMEM] + [IN_VMEM] * len(operands) + [ANYWHERE] * len(given),
+        functools.partial(outer_kernel, places, chunks, flags),
+        in_specs=[IN_SMEM]
+        + [IN_VMEM] * len(operands)
+        + [ANYWHERE] * (len(given) + len(after)),
         out_specs=[ANYWHERE] * 2 + [IN_VMEM] * flags,
-        out_shape=[jax.ShapeDtypeStruct((width, 4 * quarter), BF16)] * 2
+        out_shape=[jax.ShapeDtypeStruct((width, 4 * chunks * columns), BF16)] * 2
         + [jax.ShapeDtypeStruct((8, 128), F32)] * flags,
         input_output_aliases={1 + len(operands) + k: k for k in range(len(given))},
         scratch_shapes=[
@@ -312,16 +323,18 @@
         ],
         compiler_params=params(14 * MIB),
         cost_estimate=cost(1, 1),
-    )(me, *operands, *given)
-
-
-def rows_kernel(function, count, results, *refs):
+    )(me, *operands, *given, *after)
+
+
+def rows_kernel(function, count, results, start_column, *refs):
     ins, outs = refs[:count], refs[-results:]
-    height = outs[0].shape[-2]
+    height, width = outs[0].shape[-2:]
     for low in range(0, height, ROWS):
 
         def load(i):
             ref = ins[i]
+            if ref.shape[-1] > width:
+                return ref[low : low + ROWS, start_column : start_column + width].astype(F32)
             if ref.shape[-2] == height:
                 return ref[..., low : low + ROWS, :].astype(F32)
             part, start = divmod(low, ref.shape[-2])
@@ -331,9 +344,9 @@
             ref[..., low : low + ROWS, :] = value.astype(ref.dtype)
 
 
-def by_rows(function, operands, shapes, after):
+def by_rows(function, operands, shapes, after, start_column=0):
     return pl.pallas_call(
-        functools.partial(rows_kernel, function, len(operands), len(shapes)),
+        functools.partial(rows_kernel, function, len(operands), len(shapes), start_column),
         in_specs=[IN_VMEM] * len(operands) + [ANYWHERE] * len(after),
         out_specs=[IN_VMEM] * len(shapes),
         out_shape=[jax.ShapeDtypeStruct(shape, dtype) for shape, dtype in shapes],
@@ -348,7 +361,7 @@
 
 def far_pair_rows(load):
     near = load(0)
-    return (jnp.stack([near[0] + load(1), near[1] + load(1 + PARTS)]),)
+    return (jnp.stack([near[0] + load(1), near[1] + load(2)]),)
 
 
 def hidden_rows(load):
@@ -372,8 +385,8 @@
 def term_rows(load):
     near, across = load(0), load(1)
     back_value = near[0] + load(2) + across[0]
-    back_tangent = near[1] + load(2 + PARTS) + across[1]
-    gate_value, up_value, gate_tangent, up_tangent = (load(2 + 2 * PARTS + i) for i in range(4))
+    back_tangent = near[1] + load(3) + across[1]
+    gate_value, up_value, gate_tangent, up_tangent = (load(4 + i) for i in range(4))
     s = jax.nn.sigmoid(gate_value)
     slope = s + gate_value * s * (1.0 - s)
     bend = s * (1.0 - s) * (2.0 + gate_value * (1.0 - 2.0 * s))
@@ -463,50 +476,55 @@
     far, up_across = far_sum(*up_far, [keep])
     send, near = stream_products(me, slot_rows, [gate_weight, up_weight], (1, 0), [far])
     near_got = core(send)
-    far, gate_tangent_across = far_sum(*gate_tangent_far, [near])
-    send, near_tangent = stream_products(
-        me, slot_rows, [gate_probe, up_probe], (1, 0), [far, gate_across]
-    )
-    near_tangent_got = core(send)
+    far, gate_tangent_across = far_sum(*gate_tangent_far, [near, gate_across, up_across])
     hidden, gate_value, up_value = by_rows(
         hidden_rows,
         [near, *near_got, gate_across, up_across],
         [part_type, wide_type, wide_type],
-        [near_tangent, gate_tangent_across],
+        [far],
     )
     beside, across = swap(hidden, "dp", 1), swap(hidden, "dp", 2)
-    send, keep = stream_products(
-        me, slot_rows, [up_probe], (3, 2), [hidden]
-    )
+    send, keep = stream_products(me, slot_rows, [up_probe], (3, 2), [hidden])
     got = core(send)
-    (half,) = down_products(
+    (half_value,) = down_products(
         me, hidden, beside, down_weight, (0, 1), None, 1, F32, [keep]
     )
-    far, up_tangent_across = far_sum(keep, got, [half])
-    across = pass_on(across, [far])
-    out = down_products(
-        me, across, swap(across, "dp", 1), down_weight, (2, 3), half, ranks, BF16, [far]
-    )
-    came = exchange(out)
-
+    far, up_tangent_across = far_sum(keep, got, [half_value])
+    send, near_tangent = stream_products(
+        me, slot_rows, [gate_probe, up_probe], (1, 0), [far, gate_tangent_across]
+    )
+    got = core(send)
     hidden_tangent, gate_tangent, up_tangent = by_rows(
         tangent_rows,
         [
             near_tangent,
-            *near_tangent_got,
+            *got,
             gate_tangent_across,
             up_tangent_across,
             gate_value,
             up_value,
         ],
         [part_type, wide_type, wide_type],
-        [out[0], came[1]],
-    )
+        [],
+    )
+    out = down_products(
+        me,
+        across,
+        swap(across, "dp", 1),
+        down_weight,
+        (2, 3),
+        half_value,
+        ranks,
+        BF16,
+        [hidden_tangent],
+    )
+    came = exchange(out)
+
     beside, across = swap(hidden_tangent, "dp", 1), swap(hidden_tangent, "dp", 2)
     (half,) = down_products(
-        me, hidden_tangent, beside, down_weight, (0, 1), None, 1, F32, [hidden_tangent]
-    )
-    across = pass_on(across, [half])
+        me, hidden_tangent, beside, down_weight, (0, 1), None, 1, F32, [out[0]]
+    )
+    across = pass_on(across, [half, came[1]])
     out = down_products(
         me, across, swap(across, "dp", 1), down_weight, (2, 3), half, ranks, BF16, []
     )
@@ -516,25 +534,45 @@
     cot = mix_products(came_tangent, spread, token_total, [cot[0], came[1]])
     came += exchange([cot[i // per_expert] for i in range(ranks)])
 
-    send, keep = back_products(me, came, down_weight, (3, 2), [])
-    got = core(send)
-    send, near = back_products(me, came, down_weight, (1, 0), [keep])
-    pair_type = ((2, height, quarter), BF16)
-    (far,) = by_rows(far_pair_rows, [keep, *got], [pair_type], [near])
-    got = core(send)
-    (terms,) = by_rows(
-        term_rows,
-        [near, swap(far, "dp", 2), *got, gate_value, up_value, gate_tangent, up_tangent],
-        [pair_type],
-        [far],
-    )
-
-    across, beside = swap(terms, "dp", 2), swap(terms, "dp", 1)
-    *outputs, flag = outer_products(me, slot_rows, [terms, beside], (0, 1), None)
-    across = pass_on(across, [flag])
-    beyond = swap(across, "dp", 1)
-    outputs = outer_products(me, slot_rows, [across], (2,), outputs)
-    return tuple(outer_products(me, slot_rows, [beyond], (3,), outputs))
+    chunks = 2 if quarter % 256 == 0 else 1
+    width = quarter // chunks
+    pair_type = ((2, height, width), BF16)
+    keep, ends = cot[0], []
+    for i in range(chunks):
+        ((send, keep),) = back_products(me, came, down_weight, (3, 2), [i], chunks, [keep])
+        ends.append((keep, core(send)))
+    fars = []
+    for i in range(chunks - 1):
+        fars += by_rows(far_pair_rows, [ends[i][0], *ends[i][1]], [pair_type], [keep])
+    nears = back_products(me, came, down_weight, (1, 0), range(chunks), chunks, fars + [keep])
+    fars += by_rows(far_pair_rows, [ends[-1][0], *ends[-1][1]], [pair_type], [nears[0][1]])
+    sums = [swap(far, "dp", 2) for far in fars]
+    nears = [[keep, *core(send)] for send, keep in nears]
+
+    last, terms = fars[-1], []
+    for i in range(chunks):
+        (near, *got) = nears[i]
+        terms += by_rows(
+            term_rows,
+            [near, sums[i], *got, gate_value, up_value, gate_tangent, up_tangent],
+            [pair_type],
+            [last],
+            i * width,
+        )
+        last = terms[-1]
+    across = [swap(term, "dp", 2) for term in terms]
+    beside = [swap(term, "dp", 1) for term in terms]
+    places = [(offset, i) for offset in (0, 1) for i in range(chunks)]
+    *outputs, last = outer_products(me, slot_rows, terms + beside, places, chunks, None)
+    passed = []
+    for i in range(chunks):
+        last = pass_on(across[i], [last])
+        passed.append((last, swap(last, "dp", 1)))
+    for i in range(chunks):
+        outputs = outer_products(
+            me, slot_rows, passed[i], [(2, i), (3, i)], chunks, outputs, [last]
+        )
+    return tuple(outputs)
 
 
 def solution(mesh):

time: 127 us -> 119 us (0.937)
  waiting for transfers between devices: 32.6 us -> 21.9 us
  starting transfers between devices: 41.9 us -> 44.5 us
    ppermute x53 -> x57, waiting for transfers between devices: 32.6 us -> 21.9 us  [swap(): return lax.ppermute(value, axis, [(i, i ^ mask) for i in range(size)])]
    ppermute x53 -> x57, starting transfers between devices: 41.9 us -> 44.5 us  [swap(): return lax.ppermute(value, axis, [(i, i ^ mask) for i in range(size)])]
    pallas_call x5 -> x6, Pallas kernels: 16.2 us -> 16.6 us  [the longest x3 12 us: outer_products(): pl.pallas_call(functools.partial(outer_kernel, places, chunks, flags), in...]
  transfers between devices with their start and end apart: 53 -> 57, of which waited for: 16 -> 13; matrix products, arithmetic and copies ran while one was open for 0% -> 0% of each run, Pallas kernels for 33% -> 36%
where the time goes in v3:
time: 119 us
  Pallas kernels  49.4 us (42%)
  starting transfers between devices  44.5 us (37%)
  waiting for transfers between devices  21.9 us (18%)
  between operations  1.32 us (1%)
  other arithmetic  1.21 us (1%)
    ppermute x57, starting transfers between devices, swap(): return lax.ppermute(value, axis, [(i, i ^ mask) for i in range(size)])  44.5 us
    ppermute x57, waiting for transfers between devices, swap(): return lax.ppermute(value, axis, [(i, i ^ mask) for i in range(size)])  21.9 us
    pallas_call x3, Pallas kernels, stream_products(): pl.pallas_call(functools.partial(stream_kernel, count, offsets), in_specs...  14.6 us
    pallas_call x3, Pallas kernels, outer_products(): pl.pallas_call(functools.partial(outer_kernel, places, chunks, flags), in...  12 us
    pallas_call x1, Pallas kernels, prefetch(): pl.pallas_call(functools.partial(prefetch_kernel, offsets), in_specs=[IN_...  6.55 us
    pallas_call x4, Pallas kernels, down_products(): pl.pallas_call(functools.partial(down_kernel, offsets, start is not None,...  4.7 us
    pallas_call x3, Pallas kernels, back_products(): pl.pallas_call(functools.partial(back_kernel, count, jobs, width), in_spe...  4.59 us
    pallas_call x3, Pallas kernels, resident_products(): pl.pallas_call(resident_kernel, in_specs=[IN_VMEM] * 2 + [ANYWHERE] * len...  3.61 us
  transfers between devices with their start and end apart: 57, of which 13 were waited for; matrix products, arithmetic and copies ran while one was open for 0% of the time, Pallas kernels for 36%

profile of v3, /device:TPU:0, one launch (start us, length us, event | category | flops | bytes accessed | tf_op | source)
XLA Modules:
  0.0 118.5 jit_solution(7970724470534635975)
XLA Ops:
  1.9 3.1 %collective-permute-start = (bf16[24,1536]{1,0:T(8,128)(2,1)S(1)}, bf16[24,1536]{1,0:T(8,128)(2,1)S(1)}, u32[]{:S(2)}, u32[]{:S(2)}) collective-permute-start(bf16[24,1536]{1,0:T(8,128)(2,1)S(1)} %get-tuple-element.122), channel_id=1, source_target_pairs={{0,4},{4,0},{8,12},{12,8},{1,5},{5,1},{9,13},{13,9},{2,6},{6,2},{1... | collective-permute-start | bytes 221192 | tf_op jit(solution)/shard_map/ppermute | solution.py:25
  5.0 2.6 %collective-permute-start.1 = (bf16[24,1536]{1,0:T(8,128)(2,1)S(1)}, bf16[24,1536]{1,0:T(8,128)(2,1)S(1)}, u32[]{:S(2)}, u32[]{:S(2)}) collective-permute-start(bf16[24,1536]{1,0:T(8,128)(2,1)S(1)} %get-tuple-element.123), channel_id=1, source_target_pairs={{0,8},{4,12},{8,0},{12,4},{1,9},{5,13},{9,1},{13,5},{2,10},{6,14},... | collective-permute-start | bytes 221192 | tf_op jit(solution)/shard_map/ppermute | solution.py:25
  7.6 6.6 %shard_map.95 = (bf16[2,1536,1024]{2,1,0:T(8,128)(2,1)S(1)}, bf16[2,1536,1024]{2,1,0:T(8,128)(2,1)S(1)}, bf16[2,1536,1024]{2,1,0:T(8,128)(2,1)S(1)}) custom-call(s32[1]{0:T(128)} %bitcast.me_ref, bf16[1536,4096]{1,0:T(8,128)(2,1)} %refs_0_.5, bf16[1536,4096]{1,0:T(8,128)(2,1)} %refs_1_.4, bf16[1536,4096]{1,0:T(8,128)(2,1)} %refs_0_.7), custom_call_target="tpu_custom_call" | custom-call | flops 1 | bytes 37748736 | tf_op jit(solution)/shard_map/pallas_call | solution.py:61
  19.2 1.8 %collective-permute-start.12 = (bf16[96,1024]{1,0:T(8,128)(2,1)S(1)}, bf16[96,1024]{1,0:T(8,128)(2,1)S(1)}, u32[]{:S(2)}, u32[]{:S(2)}) collective-permute-start(bf16[96,1024]{1,0:T(8,128)(2,1)S(1)} %shard_map.100.refs_2_), channel_id=1, source_target_pairs={{0,2},{1,3},{2,0},{3,1},{4,6},{5,7},{6,4},{7,5},{8,10},{9,11},{10,... | collective-permute-start | bytes 589832 | tf_op jit(solution)/shard_map/ppermute | solution.py:25
  21.5 6.0 %shard_map.101 = (bf16[48,1024]{1,0:T(8,128)(2,1)S(1)}, bf16[48,1024]{1,0:T(8,128)(2,1)S(1)}, bf16[48,1024]{1,0:T(8,128)(2,1)S(1)}, bf16[48,1024]{1,0:T(8,128)(2,1)S(1)}, bf16[2,96,1024]{2,1,0:T(8,128)(2,1)S(1)}) custom-call(s32[1]{0:T(128)} %bitcast.me_ref, bf16[96,1536]{1,0:T(8,128)(2,1)S(1)} %pad_maximum_fusion.rows_ref.tokens_ref, ...), custom_call_target="tpu_custom_call" | custom-call | flops 1 | bytes 1 | tf_op jit(solution)/shard_map/pallas_call | solution.py:148
  30.7 1.8 %collective-permute-start.20 = (bf16[96,1024]{1,0:T(8,128)(2,1)S(1)}, bf16[96,1024]{1,0:T(8,128)(2,1)S(1)}, u32[]{:S(2)}, u32[]{:S(2)}) collective-permute-start(bf16[96,1024]{1,0:T(8,128)(2,1)S(1)} %shard_map.102.refs_7_), channel_id=1, source_target_pairs={{0,2},{1,3},{2,0},{3,1},{4,6},{5,7},{6,4},{7,5},{8,10},{9,11},{10,... | collective-permute-start | bytes 589832 | tf_op jit(solution)/shard_map/ppermute | solution.py:25
  32.8 3.3 %shard_map.104 = (bf16[48,1024]{1,0:T(8,128)(2,1)S(1)}, bf16[48,1024]{1,0:T(8,128)(2,1)S(1)}, bf16[1,96,1024]{2,1,0:T(8,128)(2,1)S(1)}) custom-call(s32[1]{0:T(128)} %bitcast.me_ref, bf16[96,1536]{1,0:T(8,128)(2,1)S(1)} %pad_maximum_fusion.rows_ref.tokens_ref, bf16[1536,4096]{1,0:T(8,128)(2,1)} %refs_1_.5, ...), custom_call_target="tpu_custom_call" | custom-call | flops 1 | bytes 1 | tf_op jit(solution)/shard_map/pallas_call | solution.py:148
  37.9 1.8 %collective-permute-start.25 = (bf16[96,1024]{1,0:T(8,128)(2,1)S(1)}, bf16[96,1024]{1,0:T(8,128)(2,1)S(1)}, u32[]{:S(2)}, u32[]{:S(2)}) collective-permute-start(bf16[96,1024]{1,0:T(8,128)(2,1)S(1)} %shard_map.106.refs_2_), channel_id=1, source_target_pairs={{0,2},{1,3},{2,0},{3,1},{4,6},{5,7},{6,4},{7,5},{8,10},{9,11},{10,... | collective-permute-start | bytes 589832 | tf_op jit(solution)/shard_map/ppermute | solution.py:25
  39.7 5.4 %shard_map.107 = (bf16[48,1024]{1,0:T(8,128)(2,1)S(1)}, bf16[48,1024]{1,0:T(8,128)(2,1)S(1)}, bf16[48,1024]{1,0:T(8,128)(2,1)S(1)}, bf16[48,1024]{1,0:T(8,128)(2,1)S(1)}, bf16[2,96,1024]{2,1,0:T(8,128)(2,1)S(1)}) custom-call(s32[1]{0:T(128)} %bitcast.me_ref, bf16[96,1536]{1,0:T(8,128)(2,1)S(1)} %pad_maximum_fusion.rows_ref.tokens_ref, ...), custom_call_target="tpu_custom_call" | custom-call | flops 1 | bytes 1 | tf_op jit(solution)/shard_map/pallas_call | solution.py:148
  51.7 2.5 %collective-permute-done.26.refs_1_ = bf16[24,1536]{1,0:T(8,128)(2,1)S(1)} collective-permute-done((bf16[24,1536]{1,0:T(8,128)(2,1)S(1)}, bf16[24,1536]{1,0:T(8,128)(2,1)S(1)}, u32[]{:S(2)}, u32[]{:S(2)}) %collective-permute-start.26) | collective-permute-done | bytes 73760 | tf_op jit(solution)/shard_map/ppermute | solution.py:25
  55.0 1.8 %collective-permute-start.27 = (bf16[24,1536]{1,0:T(8,128)(2,1)S(1)}, bf16[24,1536]{1,0:T(8,128)(2,1)S(1)}, u32[]{:S(2)}, u32[]{:S(2)}) collective-permute-start(bf16[24,1536]{1,0:T(8,128)(2,1)S(1)} %get-tuple-element.93), channel_id=1, source_target_pairs={{0,8},{4,12},{8,0},{12,4},{1,9},{5,13},{9,1},{13,5},{2,10},{6,14},... | collective-permute-start | bytes 221192 | tf_op jit(solution)/shard_map/ppermute | solution.py:25
  56.9 1.9 %collective-permute-start.28 = (bf16[24,1536]{1,0:T(8,128)(2,1)S(1)}, bf16[24,1536]{1,0:T(8,128)(2,1)S(1)}, u32[]{:S(2)}, u32[]{:S(2)}) collective-permute-start(bf16[24,1536]{1,0:T(8,128)(2,1)S(1)} %get-tuple-element.94), channel_id=1, source_target_pairs={{0,12},{4,8},{8,4},{12,0},{1,13},{5,9},{9,5},{13,1},{2,14},{6,10},... | collective-permute-start | bytes 221192 | tf_op jit(solution)/shard_map/ppermute | solution.py:25
  60.6 2.1 %collective-permute-start.36 = (bf16[24,1536]{1,0:T(8,128)(2,1)S(1)}, bf16[24,1536]{1,0:T(8,128)(2,1)S(1)}, u32[]{:S(2)}, u32[]{:S(2)}) collective-permute-start(bf16[24,1536]{1,0:T(8,128)(2,1)S(1)} %get-tuple-element.99), channel_id=1, source_target_pairs={{0,8},{4,12},{8,0},{12,4},{1,9},{5,13},{9,1},{13,5},{2,10},{6,14},... | collective-permute-start | bytes 221192 | tf_op jit(solution)/shard_map/ppermute | solution.py:25
  62.7 1.9 %collective-permute-start.37 = (bf16[24,1536]{1,0:T(8,128)(2,1)S(1)}, bf16[24,1536]{1,0:T(8,128)(2,1)S(1)}, u32[]{:S(2)}, u32[]{:S(2)}) collective-permute-start(bf16[24,1536]{1,0:T(8,128)(2,1)S(1)} %get-tuple-element.100), channel_id=1, source_target_pairs={{0,12},{4,8},{8,4},{12,0},{1,13},{5,9},{9,5},{13,1},{2,14},{6,10},... | collective-permute-start | bytes 221192 | tf_op jit(solution)/shard_map/ppermute | solution.py:25
  66.5 3.0 %collective-permute-start.33 = (bf16[24,1536]{1,0:T(8,128)(2,1)S(1)}, bf16[24,1536]{1,0:T(8,128)(2,1)S(1)}, u32[]{:S(2)}, u32[]{:S(2)}) collective-permute-start(bf16[24,1536]{1,0:T(8,128)(2,1)S(1)} %get-tuple-element.97.refs_5_.refs_0_), channel_id=1, source_target_pairs={{0,4},{4,0},{8,12},{12,8},{1,5},{5,1},{9,13},{13,9},{2,6},{6,2},{1... | collective-permute-start | bytes 221192 | tf_op jit(solution)/shard_map/ppermute | solution.py:25
  69.5 2.0 %collective-permute-start.34 = (bf16[24,1536]{1,0:T(8,128)(2,1)S(1)}, bf16[24,1536]{1,0:T(8,128)(2,1)S(1)}, u32[]{:S(2)}, u32[]{:S(2)}) collective-permute-start(bf16[24,1536]{1,0:T(8,128)(2,1)S(1)} %get-tuple-element.98), channel_id=1, source_target_pairs={{0,8},{4,12},{8,0},{12,4},{1,9},{5,13},{9,1},{13,5},{2,10},{6,14},... | collective-permute-start | bytes 221192 | tf_op jit(solution)/shard_map/ppermute | solution.py:25
  74.9 2.8 %collective-permute-start.39 = (bf16[24,1536]{1,0:T(8,128)(2,1)S(1)}, bf16[24,1536]{1,0:T(8,128)(2,1)S(1)}, u32[]{:S(2)}, u32[]{:S(2)}) collective-permute-start(bf16[24,1536]{1,0:T(8,128)(2,1)S(1)} %get-tuple-element.102), channel_id=1, source_target_pairs={{0,8},{4,12},{8,0},{12,4},{1,9},{5,13},{9,1},{13,5},{2,10},{6,14},... | collective-permute-start | bytes 221192 | tf_op jit(solution)/shard_map/ppermute | solution.py:25
  79.1 5.6 %collective-permute-done.39.refs_6_ = bf16[24,1536]{1,0:T(8,128)(2,1)S(1)} collective-permute-done((bf16[24,1536]{1,0:T(8,128)(2,1)S(1)}, bf16[24,1536]{1,0:T(8,128)(2,1)S(1)}, u32[]{:S(2)}, u32[]{:S(2)}) %collective-permute-start.39) | collective-permute-done | bytes 73760 | tf_op jit(solution)/shard_map/ppermute | solution.py:25
  89.4 2.1 %shard_map.118 = (bf16[96,512]{1,0:T(8,128)(2,1)S(1)}, bf16[96,512]{1,0:T(8,128)(2,1)S(1)}, bf16[2,96,512]{2,1,0:T(8,128)(2,1)S(1)}, bf16[96,512]{1,0:T(8,128)(2...) custom-call(s32[1]{0:T(128)} %bitcast.me_ref, ...), custom_call_target="tpu_custom_call" | custom-call | flops 1 | bytes 1 | tf_op jit(solution)/shard_map/pallas_call | solution.py:192
  96.1 3.5 %collective-permute-done.45.refs_1_ = bf16[2,96,512]{2,1,0:T(8,128)(2,1)S(1)} collective-permute-done((bf16[2,96,512]{2,1,0:T(8,128)(2,1)S(1)}, bf16[2,96,512]{2,1,0:T(8,128)(2,1)S(1)}, u32[]{:S(2)}, u32[]{:S(2)}) %collective-permute-start.45) | collective-permute-done | bytes 196640 | tf_op jit(solution)/shard_map/ppermute | solution.py:25
  102.4 5.3 %shard_map.122 = (bf16[1536,4096]{1,0:T(8,128)(2,1)}, bf16[1536,4096]{1,0:T(8,128)(2,1)}, f32[8,128]{1,0:T(8,128)S(1)}) custom-call(s32[1]{0:T(128)} %bitcast.me_ref, bf16[96,1536]{1,0:T(8,128)(2,1)S(1)} %pad_maximum_fusion.rows_ref.tokens_ref, bf16[2,96,512]{2,1,0:T(8,128)(2,1)S(1)} %shard_map.120.refs_8_.refs_0_, ...), custom_call_target="tpu_custom_call" | custom-call | flops 1 | bytes 1 | tf_op jit(solution)/shard_map/pallas_call | solution.py:310
  108.2 3.2 %collective-permute-done.51.value_ref = bf16[2,96,512]{2,1,0:T(8,128)(2,1)S(1)} collective-permute-done((bf16[2,96,512]{2,1,0:T(8,128)(2,1)S(1)}, bf16[2,96,512]{2,1,0:T(8,128)(2,1)S(1)}, u32[]{:S(2)}, u32[]{:S(2)}) %collective-permute-start.51) | collective-permute-done | bytes 196640 | tf_op jit(solution)/shard_map/ppermute | solution.py:25
  111.6 3.4 %shard_map.125 = (bf16[1536,4096]{1,0:T(8,128)(2,1)}, bf16[1536,4096]{1,0:T(8,128)(2,1)}) custom-call(s32[1]{0:T(128)} %bitcast.me_ref, bf16[96,1536]{1,0:T(8,128)(2,1)S(1)} %pad_maximum_fusion.rows_ref.tokens_ref, bf16[2,96,512]{2,1,0:T(8,128)(2,1)S(1)} %shard_map.123.refs_0_, ...), custom_call_target="tpu_custom_call", output_to_operand_aliasing={{0}: (4, {}), {1}: (5, {})} | custom-call | flops 1 | bytes 1 | tf_op jit(solution)/shard_map/pallas_call | solution.py:310
  115.0 3.4 %shard_map.126 = (bf16[1536,4096]{1,0:T(8,128)(2,1)}, bf16[1536,4096]{1,0:T(8,128)(2,1)}) custom-call(s32[1]{0:T(128)} %bitcast.me_ref, bf16[96,1536]{1,0:T(8,128)(2,1)S(1)} %pad_maximum_fusion.rows_ref.tokens_ref, bf16[2,96,512]{2,1,0:T(8,128)(2,1)S(1)} %shard_map.124.refs_4_.refs_0_, ...), custom_call_target="tpu_custom_call", output_to_operand_aliasing={{0}: (4, {}), {1}: (5, {})} | custom-call | flops 1 | bytes 1 | tf_op jit(solution)/shard_map/pallas_call | solution.py:310
  (147 shorter events, 40.6 us)
Async XLA Ops:
  1.9 12.2 %collective-permute-start = (bf16[24,1536]{1,0:T(8,128)(2,1)S(1)}, bf16[24,1536]{1,0:T(8,128)(2,1)S(1)}, u32[]{:S(2)}, u32[]{:S(2)}) collective-permute-start(bf16[24,1536]{1,0:T(8,128)(2,1)S(1)} %get-tuple-element.122), channel_id=1, source_target_pairs={{0,4},{4,0},{8,12},{12,8},{1,5},{5,1},{9,13},{13,9},{2,6},{6,2},{1... | collective-permute-start | bytes 221192 | tf_op jit(solution)/shard_map/ppermute | solution.py:25
  5.0 9.2 %collective-permute-start.1 = (bf16[24,1536]{1,0:T(8,128)(2,1)S(1)}, bf16[24,1536]{1,0:T(8,128)(2,1)S(1)}, u32[]{:S(2)}, u32[]{:S(2)}) collective-permute-start(bf16[24,1536]{1,0:T(8,128)(2,1)S(1)} %get-tuple-element.123), channel_id=1, source_target_pairs={{0,8},{4,12},{8,0},{12,4},{1,9},{5,13},{9,1},{13,5},{2,10},{6,14},... | collective-permute-start | bytes 221192 | tf_op jit(solution)/shard_map/ppermute | solution.py:25
  7.6 6.6 %collective-permute-start.2 = (bf16[24,1536]{1,0:T(8,128)(2,1)S(1)}, bf16[24,1536]{1,0:T(8,128)(2,1)S(1)}, u32[]{:S(2)}, u32[]{:S(2)}) collective-permute-start(bf16[24,1536]{1,0:T(8,128)(2,1)S(1)} %get-tuple-element.123), channel_id=1, source_target_pairs={{0,12},{4,8},{8,4},{12,0},{1,13},{5,9},{9,5},{13,1},{2,14},{6,10},... | collective-permute-start | bytes 221192 | tf_op jit(solution)/shard_map/ppermute | solution.py:25
  19.2 9.2 %collective-permute-start.12 = (bf16[96,1024]{1,0:T(8,128)(2,1)S(1)}, bf16[96,1024]{1,0:T(8,128)(2,1)S(1)}, u32[]{:S(2)}, u32[]{:S(2)}) collective-permute-start(bf16[96,1024]{1,0:T(8,128)(2,1)S(1)} %shard_map.100.refs_2_), channel_id=1, source_target_pairs={{0,2},{1,3},{2,0},{3,1},{4,6},{5,7},{6,4},{7,5},{8,10},{9,11},{10,... | collective-permute-start | bytes 589832 | tf_op jit(solution)/shard_map/ppermute | solution.py:25
  20.9 6.9 %collective-permute-start.13 = (bf16[48,1024]{1,0:T(8,128)(2,1)S(1)}, bf16[48,1024]{1,0:T(8,128)(2,1)S(1)}, u32[]{:S(2)}, u32[]{:S(2)}) collective-permute-start(bf16[48,1024]{1,0:T(8,128)(2,1)S(1)} %get-tuple-element.77), channel_id=1, source_target_pairs={{0,1},{1,0},{2,3},{3,2},{4,5},{5,4},{6,7},{7,6},{8,9},{9,8},{10,11... | collective-permute-start | bytes 294920 | tf_op jit(solution)/shard_map/ppermute | solution.py:25
  20.9 9.4 %collective-permute-start.11 = (bf16[96,1024]{1,0:T(8,128)(2,1)S(1)}, bf16[96,1024]{1,0:T(8,128)(2,1)S(1)}, u32[]{:S(2)}, u32[]{:S(2)}) collective-permute-start(bf16[96,1024]{1,0:T(8,128)(2,1)S(1)} %shard_map.98.refs_0_), channel_id=1, source_target_pairs={{0,2},{1,3},{2,0},{3,1},{4,6},{5,7},{6,4},{7,5},{8,10},{9,11},{10,... | collective-permute-start | bytes 589832 | tf_op jit(solution)/shard_map/ppermute | solution.py:25
  21.3 6.8 %collective-permute-start.14 = (bf16[48,1024]{1,0:T(8,128)(2,1)S(1)}, bf16[48,1024]{1,0:T(8,128)(2,1)S(1)}, u32[]{:S(2)}, u32[]{:S(2)}) collective-permute-start(bf16[48,1024]{1,0:T(8,128)(2,1)S(1)} %get-tuple-element.78), channel_id=1, source_target_pairs={{0,1},{1,0},{2,3},{3,2},{4,5},{5,4},{6,7},{7,6},{8,9},{9,8},{10,11... | collective-permute-start | bytes 294920 | tf_op jit(solution)/shard_map/ppermute | solution.py:25
  30.7 9.0 %collective-permute-start.20 = (bf16[96,1024]{1,0:T(8,128)(2,1)S(1)}, bf16[96,1024]{1,0:T(8,128)(2,1)S(1)}, u32[]{:S(2)}, u32[]{:S(2)}) collective-permute-start(bf16[96,1024]{1,0:T(8,128)(2,1)S(1)} %shard_map.102.refs_7_), channel_id=1, source_target_pairs={{0,2},{1,3},{2,0},{3,1},{4,6},{5,7},{6,4},{7,5},{8,10},{9,11},{10,... | collective-permute-start | bytes 589832 | tf_op jit(solution)/shard_map/ppermute | solution.py:25
  32.5 13.3 %collective-permute-start.15 = (bf16[96,1024]{1,0:T(8,128)(2,1)S(1)}, bf16[96,1024]{1,0:T(8,128)(2,1)S(1)}, u32[]{:S(2)}, u32[]{:S(2)}) collective-permute-start(bf16[96,1024]{1,0:T(8,128)(2,1)S(1)} %get-tuple-element.79.refs_1_.first_ref), channel_id=1, source_target_pairs={{0,2},{1,3},{2,0},{3,1},{4,6},{5,7},{6,4},{7,5},{8,10},{9,11},{10,... | collective-permute-start | bytes 589832 | tf_op jit(solution)/shard_map/ppermute | solution.py:25
  37.9 9.2 %collective-permute-start.25 = (bf16[96,1024]{1,0:T(8,128)(2,1)S(1)}, bf16[96,1024]{1,0:T(8,128)(2,1)S(1)}, u32[]{:S(2)}, u32[]{:S(2)}) collective-permute-start(bf16[96,1024]{1,0:T(8,128)(2,1)S(1)} %shard_map.106.refs_2_), channel_id=1, source_target_pairs={{0,2},{1,3},{2,0},{3,1},{4,6},{5,7},{6,4},{7,5},{8,10},{9,11},{10,... | collective-permute-start | bytes 589832 | tf_op jit(solution)/shard_map/ppermute | solution.py:25
  47.9 7.0 %collective-permute-start.29 = (bf16[96,1024]{1,0:T(8,128)(2,1)S(1)}, bf16[96,1024]{1,0:T(8,128)(2,1)S(1)}, u32[]{:S(2)}, u32[]{:S(2)}) collective-permute-start(bf16[96,1024]{1,0:T(8,128)(2,1)S(1)} %get-tuple-element.90.rest_1_.first_ref), channel_id=1, source_target_pairs={{0,2},{1,3},{2,0},{3,1},{4,6},{5,7},{6,4},{7,5},{8,10},{9,11},{10,... | collective-permute-start | bytes 589832 | tf_op jit(solution)/shard_map/ppermute | solution.py:25
  55.0 9.6 %collective-permute-start.27 = (bf16[24,1536]{1,0:T(8,128)(2,1)S(1)}, bf16[24,1536]{1,0:T(8,128)(2,1)S(1)}, u32[]{:S(2)}, u32[]{:S(2)}) collective-permute-start(bf16[24,1536]{1,0:T(8,128)(2,1)S(1)} %get-tuple-element.93), channel_id=1, source_target_pairs={{0,8},{4,12},{8,0},{12,4},{1,9},{5,13},{9,1},{13,5},{2,10},{6,14},... | collective-permute-start | bytes 221192 | tf_op jit(solution)/shard_map/ppermute | solution.py:25
  56.9 7.7 %collective-permute-start.28 = (bf16[24,1536]{1,0:T(8,128)(2,1)S(1)}, bf16[24,1536]{1,0:T(8,128)(2,1)S(1)}, u32[]{:S(2)}, u32[]{:S(2)}) collective-permute-start(bf16[24,1536]{1,0:T(8,128)(2,1)S(1)} %get-tuple-element.94), channel_id=1, source_target_pairs={{0,12},{4,8},{8,4},{12,0},{1,13},{5,9},{9,5},{13,1},{2,14},{6,10},... | collective-permute-start | bytes 221192 | tf_op jit(solution)/shard_map/ppermute | solution.py:25
  60.6 12.3 %collective-permute-start.36 = (bf16[24,1536]{1,0:T(8,128)(2,1)S(1)}, bf16[24,1536]{1,0:T(8,128)(2,1)S(1)}, u32[]{:S(2)}, u32[]{:S(2)}) collective-permute-start(bf16[24,1536]{1,0:T(8,128)(2,1)S(1)} %get-tuple-element.99), channel_id=1, source_target_pairs={{0,8},{4,12},{8,0},{12,4},{1,9},{5,13},{9,1},{13,5},{2,10},{6,14},... | collective-permute-start | bytes 221192 | tf_op jit(solution)/shard_map/ppermute | solution.py:25
  62.7 10.2 %collective-permute-start.37 = (bf16[24,1536]{1,0:T(8,128)(2,1)S(1)}, bf16[24,1536]{1,0:T(8,128)(2,1)S(1)}, u32[]{:S(2)}, u32[]{:S(2)}) collective-permute-start(bf16[24,1536]{1,0:T(8,128)(2,1)S(1)} %get-tuple-element.100), channel_id=1, source_target_pairs={{0,12},{4,8},{8,4},{12,0},{1,13},{5,9},{9,5},{13,1},{2,14},{6,10},... | collective-permute-start | bytes 221192 | tf_op jit(solution)/shard_map/ppermute | solution.py:25
  66.5 6.4 %collective-permute-start.33 = (bf16[24,1536]{1,0:T(8,128)(2,1)S(1)}, bf16[24,1536]{1,0:T(8,128)(2,1)S(1)}, u32[]{:S(2)}, u32[]{:S(2)}) collective-permute-start(bf16[24,1536]{1,0:T(8,128)(2,1)S(1)} %get-tuple-element.97.refs_5_.refs_0_), channel_id=1, source_target_pairs={{0,4},{4,0},{8,12},{12,8},{1,5},{5,1},{9,13},{13,9},{2,6},{6,2},{1... | collective-permute-start | bytes 221192 | tf_op jit(solution)/shard_map/ppermute | solution.py:25
  69.5 9.5 %collective-permute-start.34 = (bf16[24,1536]{1,0:T(8,128)(2,1)S(1)}, bf16[24,1536]{1,0:T(8,128)(2,1)S(1)}, u32[]{:S(2)}, u32[]{:S(2)}) collective-permute-start(bf16[24,1536]{1,0:T(8,128)(2,1)S(1)} %get-tuple-element.98), channel_id=1, source_target_pairs={{0,8},{4,12},{8,0},{12,4},{1,9},{5,13},{9,1},{13,5},{2,10},{6,14},... | collective-permute-start | bytes 221192 | tf_op jit(solution)/shard_map/ppermute | solution.py:25
  71.5 7.5 %collective-permute-start.35 = (bf16[24,1536]{1,0:T(8,128)(2,1)S(1)}, bf16[24,1536]{1,0:T(8,128)(2,1)S(1)}, u32[]{:S(2)}, u32[]{:S(2)}) collective-permute-start(bf16[24,1536]{1,0:T(8,128)(2,1)S(1)} %get-tuple-element.98), channel_id=1, source_target_pairs={{0,12},{4,8},{8,4},{12,0},{1,13},{5,9},{9,5},{13,1},{2,14},{6,10},... | collective-permute-start | bytes 221192 | tf_op jit(solution)/shard_map/ppermute | solution.py:25
  74.9 9.8 %collective-permute-start.39 = (bf16[24,1536]{1,0:T(8,128)(2,1)S(1)}, bf16[24,1536]{1,0:T(8,128)(2,1)S(1)}, u32[]{:S(2)}, u32[]{:S(2)}) collective-permute-start(bf16[24,1536]{1,0:T(8,128)(2,1)S(1)} %get-tuple-element.102), channel_id=1, source_target_pairs={{0,8},{4,12},{8,0},{12,4},{1,9},{5,13},{9,1},{13,5},{2,10},{6,14},... | collective-permute-start | bytes 221192 | tf_op jit(solution)/shard_map/ppermute | solution.py:25
  77.7 7.0 %collective-permute-start.40 = (bf16[24,1536]{1,0:T(8,128)(2,1)S(1)}, bf16[24,1536]{1,0:T(8,128)(2,1)S(1)}, u32[]{:S(2)}, u32[]{:S(2)}) collective-permute-start(bf16[24,1536]{1,0:T(8,128)(2,1)S(1)} %get-tuple-element.102), channel_id=1, source_target_pairs={{0,12},{4,8},{8,4},{12,0},{1,13},{5,9},{9,5},{13,1},{2,14},{6,10},... | collective-permute-start | bytes 221192 | tf_op jit(solution)/shard_map/ppermute | solution.py:25
  88.4 7.4 %collective-permute-start.48 = (bf16[2,96,512]{2,1,0:T(8,128)(2,1)S(1)}, bf16[2,96,512]{2,1,0:T(8,128)(2,1)S(1)}, u32[]{:S(2)}, u32[]{:S(2)}) collective-permute-start(bf16[2,96,512]{2,1,0:T(8,128)(2,1)S(1)} %shard_map.117.refs_9_), channel_id=1, source_target_pairs={{0,2},{1,3},{2,0},{3,1},{4,6},{5,7},{6,4},{7,5},{8,10},{9,11},{10,... | collective-permute-start | bytes 589832 | tf_op jit(solution)/shard_map/ppermute | solution.py:25
  91.7 7.9 %collective-permute-start.45 = (bf16[2,96,512]{2,1,0:T(8,128)(2,1)S(1)}, bf16[2,96,512]{2,1,0:T(8,128)(2,1)S(1)}, u32[]{:S(2)}, u32[]{:S(2)}) collective-permute-start(bf16[2,96,512]{2,1,0:T(8,128)(2,1)S(1)} %shard_map.119.refs_8_), channel_id=1, source_target_pairs={{0,2},{1,3},{2,0},{3,1},{4,6},{5,7},{6,4},{7,5},{8,10},{9,11},{10,... | collective-permute-start | bytes 589832 | tf_op jit(solution)/shard_map/ppermute | solution.py:25
  100.4 7.8 %collective-permute-start.52 = (bf16[2,96,512]{2,1,0:T(8,128)(2,1)S(1)}, bf16[2,96,512]{2,1,0:T(8,128)(2,1)S(1)}, u32[]{:S(2)}, u32[]{:S(2)}) collective-permute-start(bf16[2,96,512]{2,1,0:T(8,128)(2,1)S(1)} %shard_map.120.refs_8_.refs_0_), channel_id=1, source_target_pairs={{0,2},{1,3},{2,0},{3,1},{4,6},{5,7},{6,4},{7,5},{8,10},{9,11},{10,... | collective-permute-start | bytes 589832 | tf_op jit(solution)/shard_map/ppermute | solution.py:25
  101.4 10.1 %collective-permute-start.51 = (bf16[2,96,512]{2,1,0:T(8,128)(2,1)S(1)}, bf16[2,96,512]{2,1,0:T(8,128)(2,1)S(1)}, u32[]{:S(2)}, u32[]{:S(2)}) collective-permute-start(bf16[2,96,512]{2,1,0:T(8,128)(2,1)S(1)} %shard_map.121.refs_1_), channel_id=1, source_target_pairs={{0,2},{1,3},{2,0},{3,1},{4,6},{5,7},{6,4},{7,5},{8,10},{9,11},{10,... | collective-permute-start | bytes 589832 | tf_op jit(solution)/shard_map/ppermute | solution.py:25
  (40 other events, 146.8 us)

commit v4 on v3

--- a/solution.py
+++ b/solution.py
@@ -476,7 +476,7 @@
     far, up_across = far_sum(*up_far, [keep])
     send, near = stream_products(me, slot_rows, [gate_weight, up_weight], (1, 0), [far])
     near_got = core(send)
-    far, gate_tangent_across = far_sum(*gate_tangent_far, [near, gate_across, up_across])
+    far, gate_tangent_across = far_sum(*gate_tangent_far, [near, gate_across])
     hidden, gate_value, up_value = by_rows(
         hidden_rows,
         [near, *near_got, gate_across, up_across],
@@ -563,11 +563,11 @@
     across = [swap(term, "dp", 2) for term in terms]
     beside = [swap(term, "dp", 1) for term in terms]
     places = [(offset, i) for offset in (0, 1) for i in range(chunks)]
-    *outputs, last = outer_products(me, slot_rows, terms + beside, places, chunks, None)
-    passed = []
-    for i in range(chunks):
-        last = pass_on(across[i], [last])
-        passed.append((last, swap(last, "dp", 1)))
+    *outputs, last = outer_products(
+        me, slot_rows, terms + beside, places, chunks, None, across[: chunks - 1]
+    )
+    last = pass_on(across[-1], [last])
+    passed = [(part, swap(part, "dp", 1)) for part in across[:-1] + [last]]
     for i in range(chunks):
         outputs = outer_products(
             me, slot_rows, passed[i], [(2, i), (3, i)], chunks, outputs, [last]

time: 119 us -> 116 us (0.975)
  waiting for transfers between devices: 21.9 us -> 20.2 us
    ppermute x57, waiting for transfers between devices: 21.9 us -> 20.2 us  [swap(): return lax.ppermute(value, axis, [(i, i ^ mask) for i in range(size)])]
  transfers between devices with their start and end apart: 57 -> 57, of which waited for: 13 -> 17; matrix products, arithmetic and copies ran while one was open for 0% -> 0% of each run, Pallas kernels for 36% -> 37%
where the time goes in v4:
time: 116 us
  Pallas kernels  49.4 us (43%)
  starting transfers between devices  43.9 us (38%)
  waiting for transfers between devices  20.2 us (17%)
  between operations  1.27 us (1%)
  other arithmetic  1.21 us (1%)
    ppermute x57, starting transfers between devices, swap(): return lax.ppermute(value, axis, [(i, i ^ mask) for i in range(size)])  43.9 us
    ppermute x57, waiting for transfers between devices, swap(): return lax.ppermute(value, axis, [(i, i ^ mask) for i in range(size)])  20.2 us
    pallas_call x3, Pallas kernels, stream_products(): pl.pallas_call(functools.partial(stream_kernel, count, offsets), in_specs...  14.7 us
    pallas_call x3, Pallas kernels, outer_products(): pl.pallas_call(functools.partial(outer_kernel, places, chunks, flags), in...  12 us
    pallas_call x1, Pallas kernels, prefetch(): pl.pallas_call(functools.partial(prefetch_kernel, offsets), in_specs=[IN_...  6.55 us
    pallas_call x4, Pallas kernels, down_products(): pl.pallas_call(functools.partial(down_kernel, offsets, start is not None,...  4.72 us
    pallas_call x3, Pallas kernels, back_products(): pl.pallas_call(functools.partial(back_kernel, count, jobs, width), in_spe...  4.57 us
    pallas_call x3, Pallas kernels, resident_products(): pl.pallas_call(resident_kernel, in_specs=[IN_VMEM] * 2 + [ANYWHERE] * len...  3.61 us
  transfers between devices with their start and end apart: 57, of which 17 were waited for; matrix products, arithmetic and copies ran while one was open for 0% of the time, Pallas kernels for 37%

profile of v4, /device:TPU:0, one launch (start us, length us, event | category | flops | bytes accessed | tf_op | source)
XLA Modules:
  0.0 116.2 jit_solution(9777797405884534925)
XLA Ops:
  1.9 3.1 %collective-permute-start = (bf16[24,1536]{1,0:T(8,128)(2,1)S(1)}, bf16[24,1536]{1,0:T(8,128)(2,1)S(1)}, u32[]{:S(2)}, u32[]{:S(2)}) collective-permute-start(bf16[24,1536]{1,0:T(8,128)(2,1)S(1)} %get-tuple-element.122), channel_id=1, source_target_pairs={{0,4},{4,0},{8,12},{12,8},{1,5},{5,1},{9,13},{13,9},{2,6},{6,2},{1... | collective-permute-start | bytes 221192 | tf_op jit(solution)/shard_map/ppermute | solution.py:25
  5.0 2.5 %collective-permute-start.2 = (bf16[24,1536]{1,0:T(8,128)(2,1)S(1)}, bf16[24,1536]{1,0:T(8,128)(2,1)S(1)}, u32[]{:S(2)}, u32[]{:S(2)}) collective-permute-start(bf16[24,1536]{1,0:T(8,128)(2,1)S(1)} %get-tuple-element.123), channel_id=1, source_target_pairs={{0,12},{4,8},{8,4},{12,0},{1,13},{5,9},{9,5},{13,1},{2,14},{6,10},... | collective-permute-start | bytes 221192 | tf_op jit(solution)/shard_map/ppermute | solution.py:25
  7.6 6.6 %shard_map.95 = (bf16[2,1536,1024]{2,1,0:T(8,128)(2,1)S(1)}, bf16[2,1536,1024]{2,1,0:T(8,128)(2,1)S(1)}, bf16[2,1536,1024]{2,1,0:T(8,128)(2,1)S(1)}) custom-call(s32[1]{0:T(128)} %bitcast.me_ref, bf16[1536,4096]{1,0:T(8,128)(2,1)} %refs_0_.5, bf16[1536,4096]{1,0:T(8,128)(2,1)} %refs_1_.4, bf16[1536,4096]{1,0:T(8,128)(2,1)} %refs_0_.7), custom_call_target="tpu_custom_call" | custom-call | flops 1 | bytes 37748736 | tf_op jit(solution)/shard_map/pallas_call | solution.py:61
  18.2 1.6 %collective-permute-start.11 = (bf16[96,1024]{1,0:T(8,128)(2,1)S(1)}, bf16[96,1024]{1,0:T(8,128)(2,1)S(1)}, u32[]{:S(2)}, u32[]{:S(2)}) collective-permute-start(bf16[96,1024]{1,0:T(8,128)(2,1)S(1)} %shard_map.98.refs_0_), channel_id=1, source_target_pairs={{0,2},{1,3},{2,0},{3,1},{4,6},{5,7},{6,4},{7,5},{8,10},{9,11},{10,... | collective-permute-start | bytes 589832 | tf_op jit(solution)/shard_map/ppermute | solution.py:25
  22.2 6.0 %shard_map.101 = (bf16[48,1024]{1,0:T(8,128)(2,1)S(1)}, bf16[48,1024]{1,0:T(8,128)(2,1)S(1)}, bf16[48,1024]{1,0:T(8,128)(2,1)S(1)}, bf16[48,1024]{1,0:T(8,128)(2,1)S(1)}, bf16[2,96,1024]{2,1,0:T(8,128)(2,1)S(1)}) custom-call(s32[1]{0:T(128)} %bitcast.me_ref, bf16[96,1536]{1,0:T(8,128)(2,1)S(1)} %pad_maximum_fusion.rows_ref.tokens_ref, ...), custom_call_target="tpu_custom_call" | custom-call | flops 1 | bytes 1 | tf_op jit(solution)/shard_map/pallas_call | solution.py:148
  32.9 3.3 %shard_map.104 = (bf16[48,1024]{1,0:T(8,128)(2,1)S(1)}, bf16[48,1024]{1,0:T(8,128)(2,1)S(1)}, bf16[1,96,1024]{2,1,0:T(8,128)(2,1)S(1)}) custom-call(s32[1]{0:T(128)} %bitcast.me_ref, bf16[96,1536]{1,0:T(8,128)(2,1)S(1)} %pad_maximum_fusion.rows_ref.tokens_ref, bf16[1536,4096]{1,0:T(8,128)(2,1)} %refs_1_.5, ...), custom_call_target="tpu_custom_call" | custom-call | flops 1 | bytes 1 | tf_op jit(solution)/shard_map/pallas_call | solution.py:148
  38.0 1.6 %collective-permute-start.25 = (bf16[96,1024]{1,0:T(8,128)(2,1)S(1)}, bf16[96,1024]{1,0:T(8,128)(2,1)S(1)}, u32[]{:S(2)}, u32[]{:S(2)}) collective-permute-start(bf16[96,1024]{1,0:T(8,128)(2,1)S(1)} %shard_map.106.refs_2_), channel_id=1, source_target_pairs={{0,2},{1,3},{2,0},{3,1},{4,6},{5,7},{6,4},{7,5},{8,10},{9,11},{10,... | collective-permute-start | bytes 589832 | tf_op jit(solution)/shard_map/ppermute | solution.py:25
  39.6 5.4 %shard_map.107 = (bf16[48,1024]{1,0:T(8,128)(2,1)S(1)}, bf16[48,1024]{1,0:T(8,128)(2,1)S(1)}, bf16[48,1024]{1,0:T(8,128)(2,1)S(1)}, bf16[48,1024]{1,0:T(8,128)(2,1)S(1)}, bf16[2,96,1024]{2,1,0:T(8,128)(2,1)S(1)}) custom-call(s32[1]{0:T(128)} %bitcast.me_ref, bf16[96,1536]{1,0:T(8,128)(2,1)S(1)} %pad_maximum_fusion.rows_ref.tokens_ref, ...), custom_call_target="tpu_custom_call" | custom-call | flops 1 | bytes 1 | tf_op jit(solution)/shard_map/pallas_call | solution.py:148
  49.4 1.6 %collective-permute-start.26 = (bf16[24,1536]{1,0:T(8,128)(2,1)S(1)}, bf16[24,1536]{1,0:T(8,128)(2,1)S(1)}, u32[]{:S(2)}, u32[]{:S(2)}) collective-permute-start(bf16[24,1536]{1,0:T(8,128)(2,1)S(1)} %get-tuple-element.92), channel_id=1, source_target_pairs={{0,4},{4,0},{8,12},{12,8},{1,5},{5,1},{9,13},{13,9},{2,6},{6,2},{1... | collective-permute-start | bytes 221192 | tf_op jit(solution)/shard_map/ppermute | solution.py:25
  52.1 1.7 %collective-permute-done.26.refs_1_ = bf16[24,1536]{1,0:T(8,128)(2,1)S(1)} collective-permute-done((bf16[24,1536]{1,0:T(8,128)(2,1)S(1)}, bf16[24,1536]{1,0:T(8,128)(2,1)S(1)}, u32[]{:S(2)}, u32[]{:S(2)}) %collective-permute-start.26) | collective-permute-done | bytes 73760 | tf_op jit(solution)/shard_map/ppermute | solution.py:25
  54.9 2.5 %collective-permute-start.27 = (bf16[24,1536]{1,0:T(8,128)(2,1)S(1)}, bf16[24,1536]{1,0:T(8,128)(2,1)S(1)}, u32[]{:S(2)}, u32[]{:S(2)}) collective-permute-start(bf16[24,1536]{1,0:T(8,128)(2,1)S(1)} %get-tuple-element.93), channel_id=1, source_target_pairs={{0,8},{4,12},{8,0},{12,4},{1,9},{5,13},{9,1},{13,5},{2,10},{6,14},... | collective-permute-start | bytes 221192 | tf_op jit(solution)/shard_map/ppermute | solution.py:25
  60.2 3.0 %collective-permute-start.36 = (bf16[24,1536]{1,0:T(8,128)(2,1)S(1)}, bf16[24,1536]{1,0:T(8,128)(2,1)S(1)}, u32[]{:S(2)}, u32[]{:S(2)}) collective-permute-start(bf16[24,1536]{1,0:T(8,128)(2,1)S(1)} %get-tuple-element.99), channel_id=1, source_target_pairs={{0,8},{4,12},{8,0},{12,4},{1,9},{5,13},{9,1},{13,5},{2,10},{6,14},... | collective-permute-start | bytes 221192 | tf_op jit(solution)/shard_map/ppermute | solution.py:25
  66.6 3.0 %collective-permute-start.33 = (bf16[24,1536]{1,0:T(8,128)(2,1)S(1)}, bf16[24,1536]{1,0:T(8,128)(2,1)S(1)}, u32[]{:S(2)}, u32[]{:S(2)}) collective-permute-start(bf16[24,1536]{1,0:T(8,128)(2,1)S(1)} %get-tuple-element.97.refs_5_.refs_0_), channel_id=1, source_target_pairs={{0,4},{4,0},{8,12},{12,8},{1,5},{5,1},{9,13},{13,9},{2,6},{6,2},{1... | collective-permute-start | bytes 221192 | tf_op jit(solution)/shard_map/ppermute | solution.py:25
  69.6 3.4 %collective-permute-start.35 = (bf16[24,1536]{1,0:T(8,128)(2,1)S(1)}, bf16[24,1536]{1,0:T(8,128)(2,1)S(1)}, u32[]{:S(2)}, u32[]{:S(2)}) collective-permute-start(bf16[24,1536]{1,0:T(8,128)(2,1)S(1)} %get-tuple-element.98), channel_id=1, source_target_pairs={{0,12},{4,8},{8,4},{12,0},{1,13},{5,9},{9,5},{13,1},{2,14},{6,10},... | collective-permute-start | bytes 221192 | tf_op jit(solution)/shard_map/ppermute | solution.py:25
  74.0 2.7 %collective-permute-start.40 = (bf16[24,1536]{1,0:T(8,128)(2,1)S(1)}, bf16[24,1536]{1,0:T(8,128)(2,1)S(1)}, u32[]{:S(2)}, u32[]{:S(2)}) collective-permute-start(bf16[24,1536]{1,0:T(8,128)(2,1)S(1)} %get-tuple-element.102), channel_id=1, source_target_pairs={{0,12},{4,8},{8,4},{12,0},{1,13},{5,9},{9,5},{13,1},{2,14},{6,10},... | collective-permute-start | bytes 221192 | tf_op jit(solution)/shard_map/ppermute | solution.py:25
  78.4 2.6 %collective-permute-done.34.refs_2_ = bf16[24,1536]{1,0:T(8,128)(2,1)S(1)} collective-permute-done((bf16[24,1536]{1,0:T(8,128)(2,1)S(1)}, bf16[24,1536]{1,0:T(8,128)(2,1)S(1)}, u32[]{:S(2)}, u32[]{:S(2)}) %collective-permute-start.34) | collective-permute-done | bytes 73760 | tf_op jit(solution)/shard_map/ppermute | solution.py:25
  81.0 3.2 %collective-permute-done.39.refs_6_ = bf16[24,1536]{1,0:T(8,128)(2,1)S(1)} collective-permute-done((bf16[24,1536]{1,0:T(8,128)(2,1)S(1)}, bf16[24,1536]{1,0:T(8,128)(2,1)S(1)}, u32[]{:S(2)}, u32[]{:S(2)}) %collective-permute-start.39) | collective-permute-done | bytes 73760 | tf_op jit(solution)/shard_map/ppermute | solution.py:25
  88.7 2.1 %shard_map.118 = (bf16[96,512]{1,0:T(8,128)(2,1)S(1)}, bf16[96,512]{1,0:T(8,128)(2,1)S(1)}, bf16[2,96,512]{2,1,0:T(8,128)(2,1)S(1)}, bf16[96,512]{1,0:T(8,128)(2...) custom-call(s32[1]{0:T(128)} %bitcast.me_ref, ...), custom_call_target="tpu_custom_call" | custom-call | flops 1 | bytes 1 | tf_op jit(solution)/shard_map/pallas_call | solution.py:192
  93.6 2.0 %collective-permute-done.48.refs_1_ = bf16[2,96,512]{2,1,0:T(8,128)(2,1)S(1)} collective-permute-done((bf16[2,96,512]{2,1,0:T(8,128)(2,1)S(1)}, bf16[2,96,512]{2,1,0:T(8,128)(2,1)S(1)}, u32[]{:S(2)}, u32[]{:S(2)}) %collective-permute-start.48) | collective-permute-done | bytes 196640 | tf_op jit(solution)/shard_map/ppermute | solution.py:25
  96.1 3.7 %collective-permute-done.45.refs_1_ = bf16[2,96,512]{2,1,0:T(8,128)(2,1)S(1)} collective-permute-done((bf16[2,96,512]{2,1,0:T(8,128)(2,1)S(1)}, bf16[2,96,512]{2,1,0:T(8,128)(2,1)S(1)}, u32[]{:S(2)}, u32[]{:S(2)}) %collective-permute-start.45) | collective-permute-done | bytes 196640 | tf_op jit(solution)/shard_map/ppermute | solution.py:25
  100.9 2.4 %collective-permute-done.54.refs_4_.refs_0_ = bf16[2,96,512]{2,1,0:T(8,128)(2,1)S(1)} collective-permute-done((bf16[2,96,512]{2,1,0:T(8,128)(2,1)S(1)}, bf16[2,96,512]{2,1,0:T(8,128)(2,1)S(1)}, u32[]{:S(2)}, u32[]{:S(2)}) %collective-permute-start.54) | collective-permute-done | bytes 196640 | tf_op jit(solution)/shard_map/ppermute | solution.py:25
  103.3 5.3 %shard_map.122 = (bf16[1536,4096]{1,0:T(8,128)(2,1)}, bf16[1536,4096]{1,0:T(8,128)(2,1)}, f32[8,128]{1,0:T(8,128)S(1)}) custom-call(s32[1]{0:T(128)} %bitcast.me_ref, bf16[96,1536]{1,0:T(8,128)(2,1)S(1)} %pad_maximum_fusion.rows_ref.tokens_ref, bf16[2,96,512]{2,1,0:T(8,128)(2,1)S(1)} %shard_map.120.refs_8_.refs_0_, ...), custom_call_target="tpu_custom_call" | custom-call | flops 1 | bytes 1 | tf_op jit(solution)/shard_map/pallas_call | solution.py:310
  109.2 3.4 %shard_map.124 = (bf16[1536,4096]{1,0:T(8,128)(2,1)}, bf16[1536,4096]{1,0:T(8,128)(2,1)}) custom-call(s32[1]{0:T(128)} %bitcast.me_ref, bf16[96,1536]{1,0:T(8,128)(2,1)S(1)} %pad_maximum_fusion.rows_ref.tokens_ref, bf16[2,96,512]{2,1,0:T(8,128)(2,1)S(1)} %collective-permute-done.54.refs_4_.refs_0_, ...), custom_call_target="tpu_custom_call", output_to_operand_aliasing={{0}: (4, {}), {1}: (5, {})} | custom-call | flops 1 | bytes 1 | tf_op jit(solution)/shard_map/pallas_call | solution.py:310
  112.6 3.4 %shard_map.125 = (bf16[1536,4096]{1,0:T(8,128)(2,1)}, bf16[1536,4096]{1,0:T(8,128)(2,1)}) custom-call(s32[1]{0:T(128)} %bitcast.me_ref, bf16[96,1536]{1,0:T(8,128)(2,1)S(1)} %pad_maximum_fusion.rows_ref.tokens_ref, bf16[2,96,512]{2,1,0:T(8,128)(2,1)S(1)} %shard_map.123.refs_4_.refs_0_, ...), custom_call_target="tpu_custom_call", output_to_operand_aliasing={{0}: (4, {}), {1}: (5, {})} | custom-call | flops 1 | bytes 1 | tf_op jit(solution)/shard_map/pallas_call | solution.py:310
  (146 shorter events, 39.2 us)
Async XLA Ops:
  1.9 12.2 %collective-permute-start = (bf16[24,1536]{1,0:T(8,128)(2,1)S(1)}, bf16[24,1536]{1,0:T(8,128)(2,1)S(1)}, u32[]{:S(2)}, u32[]{:S(2)}) collective-permute-start(bf16[24,1536]{1,0:T(8,128)(2,1)S(1)} %get-tuple-element.122), channel_id=1, source_target_pairs={{0,4},{4,0},{8,12},{12,8},{1,5},{5,1},{9,13},{13,9},{2,6},{6,2},{1... | collective-permute-start | bytes 221192 | tf_op jit(solution)/shard_map/ppermute | solution.py:25
  5.0 9.2 %collective-permute-start.2 = (bf16[24,1536]{1,0:T(8,128)(2,1)S(1)}, bf16[24,1536]{1,0:T(8,128)(2,1)S(1)}, u32[]{:S(2)}, u32[]{:S(2)}) collective-permute-start(bf16[24,1536]{1,0:T(8,128)(2,1)S(1)} %get-tuple-element.123), channel_id=1, source_target_pairs={{0,12},{4,8},{8,4},{12,0},{1,13},{5,9},{9,5},{13,1},{2,14},{6,10},... | collective-permute-start | bytes 221192 | tf_op jit(solution)/shard_map/ppermute | solution.py:25
  7.5 7.1 %collective-permute-start.1 = (bf16[24,1536]{1,0:T(8,128)(2,1)S(1)}, bf16[24,1536]{1,0:T(8,128)(2,1)S(1)}, u32[]{:S(2)}, u32[]{:S(2)}) collective-permute-start(bf16[24,1536]{1,0:T(8,128)(2,1)S(1)} %get-tuple-element.123), channel_id=1, source_target_pairs={{0,8},{4,12},{8,0},{12,4},{1,9},{5,13},{9,1},{13,5},{2,10},{6,14},... | collective-permute-start | bytes 221192 | tf_op jit(solution)/shard_map/ppermute | solution.py:25
  18.2 10.7 %collective-permute-start.11 = (bf16[96,1024]{1,0:T(8,128)(2,1)S(1)}, bf16[96,1024]{1,0:T(8,128)(2,1)S(1)}, u32[]{:S(2)}, u32[]{:S(2)}) collective-permute-start(bf16[96,1024]{1,0:T(8,128)(2,1)S(1)} %shard_map.98.refs_0_), channel_id=1, source_target_pairs={{0,2},{1,3},{2,0},{3,1},{4,6},{5,7},{6,4},{7,5},{8,10},{9,11},{10,... | collective-permute-start | bytes 589832 | tf_op jit(solution)/shard_map/ppermute | solution.py:25
  21.0 7.3 %collective-permute-start.13 = (bf16[48,1024]{1,0:T(8,128)(2,1)S(1)}, bf16[48,1024]{1,0:T(8,128)(2,1)S(1)}, u32[]{:S(2)}, u32[]{:S(2)}) collective-permute-start(bf16[48,1024]{1,0:T(8,128)(2,1)S(1)} %get-tuple-element.77), channel_id=1, source_target_pairs={{0,1},{1,0},{2,3},{3,2},{4,5},{5,4},{6,7},{7,6},{8,9},{9,8},{10,11... | collective-permute-start | bytes 294920 | tf_op jit(solution)/shard_map/ppermute | solution.py:25
  21.1 7.7 %collective-permute-start.14 = (bf16[48,1024]{1,0:T(8,128)(2,1)S(1)}, bf16[48,1024]{1,0:T(8,128)(2,1)S(1)}, u32[]{:S(2)}, u32[]{:S(2)}) collective-permute-start(bf16[48,1024]{1,0:T(8,128)(2,1)S(1)} %get-tuple-element.78), channel_id=1, source_target_pairs={{0,1},{1,0},{2,3},{3,2},{4,5},{5,4},{6,7},{7,6},{8,9},{9,8},{10,11... | collective-permute-start | bytes 294920 | tf_op jit(solution)/shard_map/ppermute | solution.py:25
  21.6 8.6 %collective-permute-start.12 = (bf16[96,1024]{1,0:T(8,128)(2,1)S(1)}, bf16[96,1024]{1,0:T(8,128)(2,1)S(1)}, u32[]{:S(2)}, u32[]{:S(2)}) collective-permute-start(bf16[96,1024]{1,0:T(8,128)(2,1)S(1)} %shard_map.100.refs_2_), channel_id=1, source_target_pairs={{0,2},{1,3},{2,0},{3,1},{4,6},{5,7},{6,4},{7,5},{8,10},{9,11},{10,... | collective-permute-start | bytes 589832 | tf_op jit(solution)/shard_map/ppermute | solution.py:25
  30.9 8.7 %collective-permute-start.20 = (bf16[96,1024]{1,0:T(8,128)(2,1)S(1)}, bf16[96,1024]{1,0:T(8,128)(2,1)S(1)}, u32[]{:S(2)}, u32[]{:S(2)}) collective-permute-start(bf16[96,1024]{1,0:T(8,128)(2,1)S(1)} %shard_map.102.refs_7_), channel_id=1, source_target_pairs={{0,2},{1,3},{2,0},{3,1},{4,6},{5,7},{6,4},{7,5},{8,10},{9,11},{10,... | collective-permute-start | bytes 589832 | tf_op jit(solution)/shard_map/ppermute | solution.py:25
  32.4 13.3 %collective-permute-start.15 = (bf16[96,1024]{1,0:T(8,128)(2,1)S(1)}, bf16[96,1024]{1,0:T(8,128)(2,1)S(1)}, u32[]{:S(2)}, u32[]{:S(2)}) collective-permute-start(bf16[96,1024]{1,0:T(8,128)(2,1)S(1)} %get-tuple-element.79.refs_1_.first_ref), channel_id=1, source_target_pairs={{0,2},{1,3},{2,0},{3,1},{4,6},{5,7},{6,4},{7,5},{8,10},{9,11},{10,... | collective-permute-start | bytes 589832 | tf_op jit(solution)/shard_map/ppermute | solution.py:25
  38.0 9.0 %collective-permute-start.25 = (bf16[96,1024]{1,0:T(8,128)(2,1)S(1)}, bf16[96,1024]{1,0:T(8,128)(2,1)S(1)}, u32[]{:S(2)}, u32[]{:S(2)}) collective-permute-start(bf16[96,1024]{1,0:T(8,128)(2,1)S(1)} %shard_map.106.refs_2_), channel_id=1, source_target_pairs={{0,2},{1,3},{2,0},{3,1},{4,6},{5,7},{6,4},{7,5},{8,10},{9,11},{10,... | collective-permute-start | bytes 589832 | tf_op jit(solution)/shard_map/ppermute | solution.py:25
  47.7 7.0 %collective-permute-start.29 = (bf16[96,1024]{1,0:T(8,128)(2,1)S(1)}, bf16[96,1024]{1,0:T(8,128)(2,1)S(1)}, u32[]{:S(2)}, u32[]{:S(2)}) collective-permute-start(bf16[96,1024]{1,0:T(8,128)(2,1)S(1)} %get-tuple-element.90.rest_1_.first_ref), channel_id=1, source_target_pairs={{0,2},{1,3},{2,0},{3,1},{4,6},{5,7},{6,4},{7,5},{8,10},{9,11},{10,... | collective-permute-start | bytes 589832 | tf_op jit(solution)/shard_map/ppermute | solution.py:25
  54.9 9.8 %collective-permute-start.27 = (bf16[24,1536]{1,0:T(8,128)(2,1)S(1)}, bf16[24,1536]{1,0:T(8,128)(2,1)S(1)}, u32[]{:S(2)}, u32[]{:S(2)}) collective-permute-start(bf16[24,1536]{1,0:T(8,128)(2,1)S(1)} %get-tuple-element.93), channel_id=1, source_target_pairs={{0,8},{4,12},{8,0},{12,4},{1,9},{5,13},{9,1},{13,5},{2,10},{6,14},... | collective-permute-start | bytes 221192 | tf_op jit(solution)/shard_map/ppermute | solution.py:25
  57.4 7.2 %collective-permute-start.28 = (bf16[24,1536]{1,0:T(8,128)(2,1)S(1)}, bf16[24,1536]{1,0:T(8,128)(2,1)S(1)}, u32[]{:S(2)}, u32[]{:S(2)}) collective-permute-start(bf16[24,1536]{1,0:T(8,128)(2,1)S(1)} %get-tuple-element.94), channel_id=1, source_target_pairs={{0,12},{4,8},{8,4},{12,0},{1,13},{5,9},{9,5},{13,1},{2,14},{6,10},... | collective-permute-start | bytes 221192 | tf_op jit(solution)/shard_map/ppermute | solution.py:25
  60.2 12.8 %collective-permute-start.36 = (bf16[24,1536]{1,0:T(8,128)(2,1)S(1)}, bf16[24,1536]{1,0:T(8,128)(2,1)S(1)}, u32[]{:S(2)}, u32[]{:S(2)}) collective-permute-start(bf16[24,1536]{1,0:T(8,128)(2,1)S(1)} %get-tuple-element.99), channel_id=1, source_target_pairs={{0,8},{4,12},{8,0},{12,4},{1,9},{5,13},{9,1},{13,5},{2,10},{6,14},... | collective-permute-start | bytes 221192 | tf_op jit(solution)/shard_map/ppermute | solution.py:25
  63.3 9.7 %collective-permute-start.37 = (bf16[24,1536]{1,0:T(8,128)(2,1)S(1)}, bf16[24,1536]{1,0:T(8,128)(2,1)S(1)}, u32[]{:S(2)}, u32[]{:S(2)}) collective-permute-start(bf16[24,1536]{1,0:T(8,128)(2,1)S(1)} %get-tuple-element.100), channel_id=1, source_target_pairs={{0,12},{4,8},{8,4},{12,0},{1,13},{5,9},{9,5},{13,1},{2,14},{6,10},... | collective-permute-start | bytes 221192 | tf_op jit(solution)/shard_map/ppermute | solution.py:25
  69.6 8.8 %collective-permute-start.35 = (bf16[24,1536]{1,0:T(8,128)(2,1)S(1)}, bf16[24,1536]{1,0:T(8,128)(2,1)S(1)}, u32[]{:S(2)}, u32[]{:S(2)}) collective-permute-start(bf16[24,1536]{1,0:T(8,128)(2,1)S(1)} %get-tuple-element.98), channel_id=1, source_target_pairs={{0,12},{4,8},{8,4},{12,0},{1,13},{5,9},{9,5},{13,1},{2,14},{6,10},... | collective-permute-start | bytes 221192 | tf_op jit(solution)/shard_map/ppermute | solution.py:25
  73.0 8.0 %collective-permute-start.34 = (bf16[24,1536]{1,0:T(8,128)(2,1)S(1)}, bf16[24,1536]{1,0:T(8,128)(2,1)S(1)}, u32[]{:S(2)}, u32[]{:S(2)}) collective-permute-start(bf16[24,1536]{1,0:T(8,128)(2,1)S(1)} %get-tuple-element.98), channel_id=1, source_target_pairs={{0,8},{4,12},{8,0},{12,4},{1,9},{5,13},{9,1},{13,5},{2,10},{6,14},... | collective-permute-start | bytes 221192 | tf_op jit(solution)/shard_map/ppermute | solution.py:25
  74.0 7.0 %collective-permute-start.40 = (bf16[24,1536]{1,0:T(8,128)(2,1)S(1)}, bf16[24,1536]{1,0:T(8,128)(2,1)S(1)}, u32[]{:S(2)}, u32[]{:S(2)}) collective-permute-start(bf16[24,1536]{1,0:T(8,128)(2,1)S(1)} %get-tuple-element.102), channel_id=1, source_target_pairs={{0,12},{4,8},{8,4},{12,0},{1,13},{5,9},{9,5},{13,1},{2,14},{6,10},... | collective-permute-start | bytes 221192 | tf_op jit(solution)/shard_map/ppermute | solution.py:25
  76.7 7.5 %collective-permute-start.39 = (bf16[24,1536]{1,0:T(8,128)(2,1)S(1)}, bf16[24,1536]{1,0:T(8,128)(2,1)S(1)}, u32[]{:S(2)}, u32[]{:S(2)}) collective-permute-start(bf16[24,1536]{1,0:T(8,128)(2,1)S(1)} %get-tuple-element.102), channel_id=1, source_target_pairs={{0,8},{4,12},{8,0},{12,4},{1,9},{5,13},{9,1},{13,5},{2,10},{6,14},... | collective-permute-start | bytes 221192 | tf_op jit(solution)/shard_map/ppermute | solution.py:25
  77.1 7.1 %collective-permute-start.38 = (bf16[24,1536]{1,0:T(8,128)(2,1)S(1)}, bf16[24,1536]{1,0:T(8,128)(2,1)S(1)}, u32[]{:S(2)}, u32[]{:S(2)}) collective-permute-start(bf16[24,1536]{1,0:T(8,128)(2,1)S(1)} %get-tuple-element.101.refs_4_.refs_9_), channel_id=1, source_target_pairs={{0,4},{4,0},{8,12},{12,8},{1,5},{5,1},{9,13},{13,9},{2,6},{6,2},{1... | collective-permute-start | bytes 221192 | tf_op jit(solution)/shard_map/ppermute | solution.py:25
  87.9 7.7 %collective-permute-start.48 = (bf16[2,96,512]{2,1,0:T(8,128)(2,1)S(1)}, bf16[2,96,512]{2,1,0:T(8,128)(2,1)S(1)}, u32[]{:S(2)}, u32[]{:S(2)}) collective-permute-start(bf16[2,96,512]{2,1,0:T(8,128)(2,1)S(1)} %shard_map.117.refs_9_), channel_id=1, source_target_pairs={{0,2},{1,3},{2,0},{3,1},{4,6},{5,7},{6,4},{7,5},{8,10},{9,11},{10,... | collective-permute-start | bytes 589832 | tf_op jit(solution)/shard_map/ppermute | solution.py:25
  91.0 8.9 %collective-permute-start.45 = (bf16[2,96,512]{2,1,0:T(8,128)(2,1)S(1)}, bf16[2,96,512]{2,1,0:T(8,128)(2,1)S(1)}, u32[]{:S(2)}, u32[]{:S(2)}) collective-permute-start(bf16[2,96,512]{2,1,0:T(8,128)(2,1)S(1)} %shard_map.119.refs_8_), channel_id=1, source_target_pairs={{0,2},{1,3},{2,0},{3,1},{4,6},{5,7},{6,4},{7,5},{8,10},{9,11},{10,... | collective-permute-start | bytes 589832 | tf_op jit(solution)/shard_map/ppermute | solution.py:25
  95.9 7.5 %collective-permute-start.54 = (bf16[2,96,512]{2,1,0:T(8,128)(2,1)S(1)}, bf16[2,96,512]{2,1,0:T(8,128)(2,1)S(1)}, u32[]{:S(2)}, u32[]{:S(2)}) collective-permute-start(bf16[2,96,512]{2,1,0:T(8,128)(2,1)S(1)} %shard_map.120.refs_8_.refs_0_), channel_id=1, source_target_pairs={{0,2},{1,3},{2,0},{3,1},{4,6},{5,7},{6,4},{7,5},{8,10},{9,11},{10,... | collective-permute-start | bytes 589832 | tf_op jit(solution)/shard_map/ppermute | solution.py:25
  100.7 8.0 %collective-permute-start.51 = (bf16[2,96,512]{2,1,0:T(8,128)(2,1)S(1)}, bf16[2,96,512]{2,1,0:T(8,128)(2,1)S(1)}, u32[]{:S(2)}, u32[]{:S(2)}) collective-permute-start(bf16[2,96,512]{2,1,0:T(8,128)(2,1)S(1)} %shard_map.121.refs_1_), channel_id=1, source_target_pairs={{0,2},{1,3},{2,0},{3,1},{4,6},{5,7},{6,4},{7,5},{8,10},{9,11},{10,... | collective-permute-start | bytes 589832 | tf_op jit(solution)/shard_map/ppermute | solution.py:25
  (40 other events, 153.5 us)

commit v5 on v4

--- a/solution.py
+++ b/solution.py
@@ -143,7 +143,7 @@
     count, (height, depth) = len(weights), rows.shape
     quarter = weights[0].shape[1] // 4
     sub = sub_width(quarter)
-    slots = min(4, 2 * count * (quarter // sub))
+    slots = min(8, 2 * count * (quarter // sub))
     shapes = result_shapes(count, height, quarter)
     *send, keep = pl.pallas_call(
         functools.partial(stream_kernel, count, offsets),

time: 116 us -> 116 us (level)
  starting transfers between devices: 43.9 us -> 45.3 us
  waiting for transfers between devices: 20.2 us -> 19 us
    ppermute x57, starting transfers between devices: 43.9 us -> 45.3 us  [swap(): return lax.ppermute(value, axis, [(i, i ^ mask) for i in range(size)])]
    ppermute x57, waiting for transfers between devices: 20.2 us -> 19 us  [swap(): return lax.ppermute(value, axis, [(i, i ^ mask) for i in range(size)])]
where the time goes in v5:
time: 116 us; the launch traced here: 115 us
  Pallas kernels  48.5 us (42%)
  starting transfers between devices  45.3 us (39%)
  waiting for transfers between devices  19 us (16%)
  between operations  1.27 us (1%)
  other arithmetic  1.21 us (1%)
    ppermute x57, starting transfers between devices, swap(): return lax.ppermute(value, axis, [(i, i ^ mask) for i in range(size)])  45.3 us
    ppermute x57, waiting for transfers between devices, swap(): return lax.ppermute(value, axis, [(i, i ^ mask) for i in range(size)])  19 us
    pallas_call x3, Pallas kernels, stream_products(): pl.pallas_call(functools.partial(stream_kernel, count, offsets), in_specs...  13.8 us
    pallas_call x3, Pallas kernels, outer_products(): pl.pallas_call(functools.partial(outer_kernel, places, chunks, flags), in...  12 us
    pallas_call x1, Pallas kernels, prefetch(): pl.pallas_call(functools.partial(prefetch_kernel, offsets), in_specs=[IN_...  6.55 us
    pallas_call x4, Pallas kernels, down_products(): pl.pallas_call(functools.partial(down_kernel, offsets, start is not None,...  4.71 us
    pallas_call x3, Pallas kernels, back_products(): pl.pallas_call(functools.partial(back_kernel, count, jobs, width), in_spe...  4.59 us
    pallas_call x3, Pallas kernels, resident_products(): pl.pallas_call(resident_kernel, in_specs=[IN_VMEM] * 2 + [ANYWHERE] * len...  3.61 us
  transfers between devices with their start and end apart: 57, of which 17 were waited for; matrix products, arithmetic and copies ran while one was open for 0% of the time, Pallas kernels for 37%

profile of v5, /device:TPU:0, one launch (start us, length us, event | category | flops | bytes accessed | tf_op | source)
XLA Modules:
  0.0 115.5 jit_solution(16403572594230911455)
XLA Ops:
  1.9 3.1 %collective-permute-start = (bf16[24,1536]{1,0:T(8,128)(2,1)S(1)}, bf16[24,1536]{1,0:T(8,128)(2,1)S(1)}, u32[]{:S(2)}, u32[]{:S(2)}) collective-permute-start(bf16[24,1536]{1,0:T(8,128)(2,1)S(1)} %get-tuple-element.122), channel_id=1, source_target_pairs={{0,4},{4,0},{8,12},{12,8},{1,5},{5,1},{9,13},{13,9},{2,6},{6,2},{1... | collective-permute-start | bytes 221192 | tf_op jit(solution)/shard_map/ppermute | solution.py:25
  5.0 2.5 %collective-permute-start.2 = (bf16[24,1536]{1,0:T(8,128)(2,1)S(1)}, bf16[24,1536]{1,0:T(8,128)(2,1)S(1)}, u32[]{:S(2)}, u32[]{:S(2)}) collective-permute-start(bf16[24,1536]{1,0:T(8,128)(2,1)S(1)} %get-tuple-element.123), channel_id=1, source_target_pairs={{0,12},{4,8},{8,4},{12,0},{1,13},{5,9},{9,5},{13,1},{2,14},{6,10},... | collective-permute-start | bytes 221192 | tf_op jit(solution)/shard_map/ppermute | solution.py:25
  7.6 6.6 %shard_map.95 = (bf16[2,1536,1024]{2,1,0:T(8,128)(2,1)S(1)}, bf16[2,1536,1024]{2,1,0:T(8,128)(2,1)S(1)}, bf16[2,1536,1024]{2,1,0:T(8,128)(2,1)S(1)}) custom-call(s32[1]{0:T(128)} %bitcast.me_ref, bf16[1536,4096]{1,0:T(8,128)(2,1)} %refs_0_.5, bf16[1536,4096]{1,0:T(8,128)(2,1)} %refs_1_.4, bf16[1536,4096]{1,0:T(8,128)(2,1)} %refs_0_.7), custom_call_target="tpu_custom_call" | custom-call | flops 1 | bytes 37748736 | tf_op jit(solution)/shard_map/pallas_call | solution.py:61
  18.2 1.6 %collective-permute-start.11 = (bf16[96,1024]{1,0:T(8,128)(2,1)S(1)}, bf16[96,1024]{1,0:T(8,128)(2,1)S(1)}, u32[]{:S(2)}, u32[]{:S(2)}) collective-permute-start(bf16[96,1024]{1,0:T(8,128)(2,1)S(1)} %shard_map.98.refs_0_), channel_id=1, source_target_pairs={{0,2},{1,3},{2,0},{3,1},{4,6},{5,7},{6,4},{7,5},{8,10},{9,11},{10,... | collective-permute-start | bytes 589832 | tf_op jit(solution)/shard_map/ppermute | solution.py:25
  22.2 5.3 %shard_map.101 = (bf16[48,1024]{1,0:T(8,128)(2,1)S(1)}, bf16[48,1024]{1,0:T(8,128)(2,1)S(1)}, bf16[48,1024]{1,0:T(8,128)(2,1)S(1)}, bf16[48,1024]{1,0:T(8,128)(2,1)S(1)}, bf16[2,96,1024]{2,1,0:T(8,128)(2,1)S(1)}) custom-call(s32[1]{0:T(128)} %bitcast.me_ref, bf16[96,1536]{1,0:T(8,128)(2,1)S(1)} %pad_maximum_fusion.rows_ref.tokens_ref, ...), custom_call_target="tpu_custom_call" | custom-call | flops 1 | bytes 1 | tf_op jit(solution)/shard_map/pallas_call | solution.py:148
  32.2 3.3 %shard_map.104 = (bf16[48,1024]{1,0:T(8,128)(2,1)S(1)}, bf16[48,1024]{1,0:T(8,128)(2,1)S(1)}, bf16[1,96,1024]{2,1,0:T(8,128)(2,1)S(1)}) custom-call(s32[1]{0:T(128)} %bitcast.me_ref, bf16[96,1536]{1,0:T(8,128)(2,1)S(1)} %pad_maximum_fusion.rows_ref.tokens_ref, bf16[1536,4096]{1,0:T(8,128)(2,1)} %refs_1_.5, ...), custom_call_target="tpu_custom_call" | custom-call | flops 1 | bytes 1 | tf_op jit(solution)/shard_map/pallas_call | solution.py:148
  37.3 1.6 %collective-permute-start.25 = (bf16[96,1024]{1,0:T(8,128)(2,1)S(1)}, bf16[96,1024]{1,0:T(8,128)(2,1)S(1)}, u32[]{:S(2)}, u32[]{:S(2)}) collective-permute-start(bf16[96,1024]{1,0:T(8,128)(2,1)S(1)} %shard_map.106.refs_2_), channel_id=1, source_target_pairs={{0,2},{1,3},{2,0},{3,1},{4,6},{5,7},{6,4},{7,5},{8,10},{9,11},{10,... | collective-permute-start | bytes 589832 | tf_op jit(solution)/shard_map/ppermute | solution.py:25
  38.9 5.2 %shard_map.107 = (bf16[48,1024]{1,0:T(8,128)(2,1)S(1)}, bf16[48,1024]{1,0:T(8,128)(2,1)S(1)}, bf16[48,1024]{1,0:T(8,128)(2,1)S(1)}, bf16[48,1024]{1,0:T(8,128)(2,1)S(1)}, bf16[2,96,1024]{2,1,0:T(8,128)(2,1)S(1)}) custom-call(s32[1]{0:T(128)} %bitcast.me_ref, bf16[96,1536]{1,0:T(8,128)(2,1)S(1)} %pad_maximum_fusion.rows_ref.tokens_ref, ...), custom_call_target="tpu_custom_call" | custom-call | flops 1 | bytes 1 | tf_op jit(solution)/shard_map/pallas_call | solution.py:148
  48.7 1.5 %collective-permute-start.26 = (bf16[24,1536]{1,0:T(8,128)(2,1)S(1)}, bf16[24,1536]{1,0:T(8,128)(2,1)S(1)}, u32[]{:S(2)}, u32[]{:S(2)}) collective-permute-start(bf16[24,1536]{1,0:T(8,128)(2,1)S(1)} %get-tuple-element.92), channel_id=1, source_target_pairs={{0,4},{4,0},{8,12},{12,8},{1,5},{5,1},{9,13},{13,9},{2,6},{6,2},{1... | collective-permute-start | bytes 221192 | tf_op jit(solution)/shard_map/ppermute | solution.py:25
  51.4 1.7 %collective-permute-done.26.refs_1_ = bf16[24,1536]{1,0:T(8,128)(2,1)S(1)} collective-permute-done((bf16[24,1536]{1,0:T(8,128)(2,1)S(1)}, bf16[24,1536]{1,0:T(8,128)(2,1)S(1)}, u32[]{:S(2)}, u32[]{:S(2)}) %collective-permute-start.26) | collective-permute-done | bytes 73760 | tf_op jit(solution)/shard_map/ppermute | solution.py:25
  54.0 2.5 %collective-permute-start.27 = (bf16[24,1536]{1,0:T(8,128)(2,1)S(1)}, bf16[24,1536]{1,0:T(8,128)(2,1)S(1)}, u32[]{:S(2)}, u32[]{:S(2)}) collective-permute-start(bf16[24,1536]{1,0:T(8,128)(2,1)S(1)} %get-tuple-element.93), channel_id=1, source_target_pairs={{0,8},{4,12},{8,0},{12,4},{1,9},{5,13},{9,1},{13,5},{2,10},{6,14},... | collective-permute-start | bytes 221192 | tf_op jit(solution)/shard_map/ppermute | solution.py:25
  59.3 3.0 %collective-permute-start.36 = (bf16[24,1536]{1,0:T(8,128)(2,1)S(1)}, bf16[24,1536]{1,0:T(8,128)(2,1)S(1)}, u32[]{:S(2)}, u32[]{:S(2)}) collective-permute-start(bf16[24,1536]{1,0:T(8,128)(2,1)S(1)} %get-tuple-element.99), channel_id=1, source_target_pairs={{0,8},{4,12},{8,0},{12,4},{1,9},{5,13},{9,1},{13,5},{2,10},{6,14},... | collective-permute-start | bytes 221192 | tf_op jit(solution)/shard_map/ppermute | solution.py:25
  65.8 3.0 %collective-permute-start.33 = (bf16[24,1536]{1,0:T(8,128)(2,1)S(1)}, bf16[24,1536]{1,0:T(8,128)(2,1)S(1)}, u32[]{:S(2)}, u32[]{:S(2)}) collective-permute-start(bf16[24,1536]{1,0:T(8,128)(2,1)S(1)} %get-tuple-element.97.refs_5_.refs_0_), channel_id=1, source_target_pairs={{0,4},{4,0},{8,12},{12,8},{1,5},{5,1},{9,13},{13,9},{2,6},{6,2},{1... | collective-permute-start | bytes 221192 | tf_op jit(solution)/shard_map/ppermute | solution.py:25
  68.7 3.4 %collective-permute-start.35 = (bf16[24,1536]{1,0:T(8,128)(2,1)S(1)}, bf16[24,1536]{1,0:T(8,128)(2,1)S(1)}, u32[]{:S(2)}, u32[]{:S(2)}) collective-permute-start(bf16[24,1536]{1,0:T(8,128)(2,1)S(1)} %get-tuple-element.98), channel_id=1, source_target_pairs={{0,12},{4,8},{8,4},{12,0},{1,13},{5,9},{9,5},{13,1},{2,14},{6,10},... | collective-permute-start | bytes 221192 | tf_op jit(solution)/shard_map/ppermute | solution.py:25
  73.1 2.7 %collective-permute-start.40 = (bf16[24,1536]{1,0:T(8,128)(2,1)S(1)}, bf16[24,1536]{1,0:T(8,128)(2,1)S(1)}, u32[]{:S(2)}, u32[]{:S(2)}) collective-permute-start(bf16[24,1536]{1,0:T(8,128)(2,1)S(1)} %get-tuple-element.102), channel_id=1, source_target_pairs={{0,12},{4,8},{8,4},{12,0},{1,13},{5,9},{9,5},{13,1},{2,14},{6,10},... | collective-permute-start | bytes 221192 | tf_op jit(solution)/shard_map/ppermute | solution.py:25
  77.6 2.6 %collective-permute-done.34.refs_2_ = bf16[24,1536]{1,0:T(8,128)(2,1)S(1)} collective-permute-done((bf16[24,1536]{1,0:T(8,128)(2,1)S(1)}, bf16[24,1536]{1,0:T(8,128)(2,1)S(1)}, u32[]{:S(2)}, u32[]{:S(2)}) %collective-permute-start.34) | collective-permute-done | bytes 73760 | tf_op jit(solution)/shard_map/ppermute | solution.py:25
  80.1 3.2 %collective-permute-done.39.refs_6_ = bf16[24,1536]{1,0:T(8,128)(2,1)S(1)} collective-permute-done((bf16[24,1536]{1,0:T(8,128)(2,1)S(1)}, bf16[24,1536]{1,0:T(8,128)(2,1)S(1)}, u32[]{:S(2)}, u32[]{:S(2)}) %collective-permute-start.39) | collective-permute-done | bytes 73760 | tf_op jit(solution)/shard_map/ppermute | solution.py:25
  88.1 2.1 %shard_map.118 = (bf16[96,512]{1,0:T(8,128)(2,1)S(1)}, bf16[96,512]{1,0:T(8,128)(2,1)S(1)}, bf16[2,96,512]{2,1,0:T(8,128)(2,1)S(1)}, bf16[96,512]{1,0:T(8,128)(2...) custom-call(s32[1]{0:T(128)} %bitcast.me_ref, ...), custom_call_target="tpu_custom_call" | custom-call | flops 1 | bytes 1 | tf_op jit(solution)/shard_map/pallas_call | solution.py:192
  92.8 1.7 %collective-permute-done.48.refs_1_ = bf16[2,96,512]{2,1,0:T(8,128)(2,1)S(1)} collective-permute-done((bf16[2,96,512]{2,1,0:T(8,128)(2,1)S(1)}, bf16[2,96,512]{2,1,0:T(8,128)(2,1)S(1)}, u32[]{:S(2)}, u32[]{:S(2)}) %collective-permute-start.48) | collective-permute-done | bytes 196640 | tf_op jit(solution)/shard_map/ppermute | solution.py:25
  95.7 3.0 %collective-permute-done.45.refs_1_ = bf16[2,96,512]{2,1,0:T(8,128)(2,1)S(1)} collective-permute-done((bf16[2,96,512]{2,1,0:T(8,128)(2,1)S(1)}, bf16[2,96,512]{2,1,0:T(8,128)(2,1)S(1)}, u32[]{:S(2)}, u32[]{:S(2)}) %collective-permute-start.45) | collective-permute-done | bytes 196640 | tf_op jit(solution)/shard_map/ppermute | solution.py:25
  100.4 2.2 %collective-permute-done.54.refs_4_.refs_0_ = bf16[2,96,512]{2,1,0:T(8,128)(2,1)S(1)} collective-permute-done((bf16[2,96,512]{2,1,0:T(8,128)(2,1)S(1)}, bf16[2,96,512]{2,1,0:T(8,128)(2,1)S(1)}, u32[]{:S(2)}, u32[]{:S(2)}) %collective-permute-start.54) | collective-permute-done | bytes 196640 | tf_op jit(solution)/shard_map/ppermute | solution.py:25
  102.6 5.3 %shard_map.122 = (bf16[1536,4096]{1,0:T(8,128)(2,1)}, bf16[1536,4096]{1,0:T(8,128)(2,1)}, f32[8,128]{1,0:T(8,128)S(1)}) custom-call(s32[1]{0:T(128)} %bitcast.me_ref, bf16[96,1536]{1,0:T(8,128)(2,1)S(1)} %pad_maximum_fusion.rows_ref.tokens_ref, bf16[2,96,512]{2,1,0:T(8,128)(2,1)S(1)} %shard_map.120.refs_8_.refs_0_, ...), custom_call_target="tpu_custom_call" | custom-call | flops 1 | bytes 1 | tf_op jit(solution)/shard_map/pallas_call | solution.py:310
  108.5 3.4 %shard_map.124 = (bf16[1536,4096]{1,0:T(8,128)(2,1)}, bf16[1536,4096]{1,0:T(8,128)(2,1)}) custom-call(s32[1]{0:T(128)} %bitcast.me_ref, bf16[96,1536]{1,0:T(8,128)(2,1)S(1)} %pad_maximum_fusion.rows_ref.tokens_ref, bf16[2,96,512]{2,1,0:T(8,128)(2,1)S(1)} %collective-permute-done.54.refs_4_.refs_0_, ...), custom_call_target="tpu_custom_call", output_to_operand_aliasing={{0}: (4, {}), {1}: (5, {})} | custom-call | flops 1 | bytes 1 | tf_op jit(solution)/shard_map/pallas_call | solution.py:310
  111.9 3.4 %shard_map.125 = (bf16[1536,4096]{1,0:T(8,128)(2,1)}, bf16[1536,4096]{1,0:T(8,128)(2,1)}) custom-call(s32[1]{0:T(128)} %bitcast.me_ref, bf16[96,1536]{1,0:T(8,128)(2,1)S(1)} %pad_maximum_fusion.rows_ref.tokens_ref, bf16[2,96,512]{2,1,0:T(8,128)(2,1)S(1)} %shard_map.123.refs_4_.refs_0_, ...), custom_call_target="tpu_custom_call", output_to_operand_aliasing={{0}: (4, {}), {1}: (5, {})} | custom-call | flops 1 | bytes 1 | tf_op jit(solution)/shard_map/pallas_call | solution.py:310
  (146 shorter events, 40.4 us)
Async XLA Ops:
  1.9 12.2 %collective-permute-start = (bf16[24,1536]{1,0:T(8,128)(2,1)S(1)}, bf16[24,1536]{1,0:T(8,128)(2,1)S(1)}, u32[]{:S(2)}, u32[]{:S(2)}) collective-permute-start(bf16[24,1536]{1,0:T(8,128)(2,1)S(1)} %get-tuple-element.122), channel_id=1, source_target_pairs={{0,4},{4,0},{8,12},{12,8},{1,5},{5,1},{9,13},{13,9},{2,6},{6,2},{1... | collective-permute-start | bytes 221192 | tf_op jit(solution)/shard_map/ppermute | solution.py:25
  5.0 9.2 %collective-permute-start.2 = (bf16[24,1536]{1,0:T(8,128)(2,1)S(1)}, bf16[24,1536]{1,0:T(8,128)(2,1)S(1)}, u32[]{:S(2)}, u32[]{:S(2)}) collective-permute-start(bf16[24,1536]{1,0:T(8,128)(2,1)S(1)} %get-tuple-element.123), channel_id=1, source_target_pairs={{0,12},{4,8},{8,4},{12,0},{1,13},{5,9},{9,5},{13,1},{2,14},{6,10},... | collective-permute-start | bytes 221192 | tf_op jit(solution)/shard_map/ppermute | solution.py:25
  7.5 7.1 %collective-permute-start.1 = (bf16[24,1536]{1,0:T(8,128)(2,1)S(1)}, bf16[24,1536]{1,0:T(8,128)(2,1)S(1)}, u32[]{:S(2)}, u32[]{:S(2)}) collective-permute-start(bf16[24,1536]{1,0:T(8,128)(2,1)S(1)} %get-tuple-element.123), channel_id=1, source_target_pairs={{0,8},{4,12},{8,0},{12,4},{1,9},{5,13},{9,1},{13,5},{2,10},{6,14},... | collective-permute-start | bytes 221192 | tf_op jit(solution)/shard_map/ppermute | solution.py:25
  18.2 10.0 %collective-permute-start.11 = (bf16[96,1024]{1,0:T(8,128)(2,1)S(1)}, bf16[96,1024]{1,0:T(8,128)(2,1)S(1)}, u32[]{:S(2)}, u32[]{:S(2)}) collective-permute-start(bf16[96,1024]{1,0:T(8,128)(2,1)S(1)} %shard_map.98.refs_0_), channel_id=1, source_target_pairs={{0,2},{1,3},{2,0},{3,1},{4,6},{5,7},{6,4},{7,5},{8,10},{9,11},{10,... | collective-permute-start | bytes 589832 | tf_op jit(solution)/shard_map/ppermute | solution.py:25
  21.0 6.6 %collective-permute-start.13 = (bf16[48,1024]{1,0:T(8,128)(2,1)S(1)}, bf16[48,1024]{1,0:T(8,128)(2,1)S(1)}, u32[]{:S(2)}, u32[]{:S(2)}) collective-permute-start(bf16[48,1024]{1,0:T(8,128)(2,1)S(1)} %get-tuple-element.77), channel_id=1, source_target_pairs={{0,1},{1,0},{2,3},{3,2},{4,5},{5,4},{6,7},{7,6},{8,9},{9,8},{10,11... | collective-permute-start | bytes 294920 | tf_op jit(solution)/shard_map/ppermute | solution.py:25
  21.1 7.1 %collective-permute-start.14 = (bf16[48,1024]{1,0:T(8,128)(2,1)S(1)}, bf16[48,1024]{1,0:T(8,128)(2,1)S(1)}, u32[]{:S(2)}, u32[]{:S(2)}) collective-permute-start(bf16[48,1024]{1,0:T(8,128)(2,1)S(1)} %get-tuple-element.78), channel_id=1, source_target_pairs={{0,1},{1,0},{2,3},{3,2},{4,5},{5,4},{6,7},{7,6},{8,9},{9,8},{10,11... | collective-permute-start | bytes 294920 | tf_op jit(solution)/shard_map/ppermute | solution.py:25
  21.6 8.0 %collective-permute-start.12 = (bf16[96,1024]{1,0:T(8,128)(2,1)S(1)}, bf16[96,1024]{1,0:T(8,128)(2,1)S(1)}, u32[]{:S(2)}, u32[]{:S(2)}) collective-permute-start(bf16[96,1024]{1,0:T(8,128)(2,1)S(1)} %shard_map.100.refs_2_), channel_id=1, source_target_pairs={{0,2},{1,3},{2,0},{3,1},{4,6},{5,7},{6,4},{7,5},{8,10},{9,11},{10,... | collective-permute-start | bytes 589832 | tf_op jit(solution)/shard_map/ppermute | solution.py:25
  30.2 8.7 %collective-permute-start.20 = (bf16[96,1024]{1,0:T(8,128)(2,1)S(1)}, bf16[96,1024]{1,0:T(8,128)(2,1)S(1)}, u32[]{:S(2)}, u32[]{:S(2)}) collective-permute-start(bf16[96,1024]{1,0:T(8,128)(2,1)S(1)} %shard_map.102.refs_7_), channel_id=1, source_target_pairs={{0,2},{1,3},{2,0},{3,1},{4,6},{5,7},{6,4},{7,5},{8,10},{9,11},{10,... | collective-permute-start | bytes 589832 | tf_op jit(solution)/shard_map/ppermute | solution.py:25
  31.7 13.0 %collective-permute-start.15 = (bf16[96,1024]{1,0:T(8,128)(2,1)S(1)}, bf16[96,1024]{1,0:T(8,128)(2,1)S(1)}, u32[]{:S(2)}, u32[]{:S(2)}) collective-permute-start(bf16[96,1024]{1,0:T(8,128)(2,1)S(1)} %get-tuple-element.79.refs_1_.first_ref), channel_id=1, source_target_pairs={{0,2},{1,3},{2,0},{3,1},{4,6},{5,7},{6,4},{7,5},{8,10},{9,11},{10,... | collective-permute-start | bytes 589832 | tf_op jit(solution)/shard_map/ppermute | solution.py:25
  37.3 8.8 %collective-permute-start.25 = (bf16[96,1024]{1,0:T(8,128)(2,1)S(1)}, bf16[96,1024]{1,0:T(8,128)(2,1)S(1)}, u32[]{:S(2)}, u32[]{:S(2)}) collective-permute-start(bf16[96,1024]{1,0:T(8,128)(2,1)S(1)} %shard_map.106.refs_2_), channel_id=1, source_target_pairs={{0,2},{1,3},{2,0},{3,1},{4,6},{5,7},{6,4},{7,5},{8,10},{9,11},{10,... | collective-permute-start | bytes 589832 | tf_op jit(solution)/shard_map/ppermute | solution.py:25
  46.9 7.0 %collective-permute-start.29 = (bf16[96,1024]{1,0:T(8,128)(2,1)S(1)}, bf16[96,1024]{1,0:T(8,128)(2,1)S(1)}, u32[]{:S(2)}, u32[]{:S(2)}) collective-permute-start(bf16[96,1024]{1,0:T(8,128)(2,1)S(1)} %get-tuple-element.90.rest_1_.first_ref), channel_id=1, source_target_pairs={{0,2},{1,3},{2,0},{3,1},{4,6},{5,7},{6,4},{7,5},{8,10},{9,11},{10,... | collective-permute-start | bytes 589832 | tf_op jit(solution)/shard_map/ppermute | solution.py:25
  54.0 9.7 %collective-permute-start.27 = (bf16[24,1536]{1,0:T(8,128)(2,1)S(1)}, bf16[24,1536]{1,0:T(8,128)(2,1)S(1)}, u32[]{:S(2)}, u32[]{:S(2)}) collective-permute-start(bf16[24,1536]{1,0:T(8,128)(2,1)S(1)} %get-tuple-element.93), channel_id=1, source_target_pairs={{0,8},{4,12},{8,0},{12,4},{1,9},{5,13},{9,1},{13,5},{2,10},{6,14},... | collective-permute-start | bytes 221192 | tf_op jit(solution)/shard_map/ppermute | solution.py:25
  56.5 7.2 %collective-permute-start.28 = (bf16[24,1536]{1,0:T(8,128)(2,1)S(1)}, bf16[24,1536]{1,0:T(8,128)(2,1)S(1)}, u32[]{:S(2)}, u32[]{:S(2)}) collective-permute-start(bf16[24,1536]{1,0:T(8,128)(2,1)S(1)} %get-tuple-element.94), channel_id=1, source_target_pairs={{0,12},{4,8},{8,4},{12,0},{1,13},{5,9},{9,5},{13,1},{2,14},{6,10},... | collective-permute-start | bytes 221192 | tf_op jit(solution)/shard_map/ppermute | solution.py:25
  59.3 12.8 %collective-permute-start.36 = (bf16[24,1536]{1,0:T(8,128)(2,1)S(1)}, bf16[24,1536]{1,0:T(8,128)(2,1)S(1)}, u32[]{:S(2)}, u32[]{:S(2)}) collective-permute-start(bf16[24,1536]{1,0:T(8,128)(2,1)S(1)} %get-tuple-element.99), channel_id=1, source_target_pairs={{0,8},{4,12},{8,0},{12,4},{1,9},{5,13},{9,1},{13,5},{2,10},{6,14},... | collective-permute-start | bytes 221192 | tf_op jit(solution)/shard_map/ppermute | solution.py:25
  62.4 9.7 %collective-permute-start.37 = (bf16[24,1536]{1,0:T(8,128)(2,1)S(1)}, bf16[24,1536]{1,0:T(8,128)(2,1)S(1)}, u32[]{:S(2)}, u32[]{:S(2)}) collective-permute-start(bf16[24,1536]{1,0:T(8,128)(2,1)S(1)} %get-tuple-element.100), channel_id=1, source_target_pairs={{0,12},{4,8},{8,4},{12,0},{1,13},{5,9},{9,5},{13,1},{2,14},{6,10},... | collective-permute-start | bytes 221192 | tf_op jit(solution)/shard_map/ppermute | solution.py:25
  68.7 8.8 %collective-permute-start.35 = (bf16[24,1536]{1,0:T(8,128)(2,1)S(1)}, bf16[24,1536]{1,0:T(8,128)(2,1)S(1)}, u32[]{:S(2)}, u32[]{:S(2)}) collective-permute-start(bf16[24,1536]{1,0:T(8,128)(2,1)S(1)} %get-tuple-element.98), channel_id=1, source_target_pairs={{0,12},{4,8},{8,4},{12,0},{1,13},{5,9},{9,5},{13,1},{2,14},{6,10},... | collective-permute-start | bytes 221192 | tf_op jit(solution)/shard_map/ppermute | solution.py:25
  72.1 8.0 %collective-permute-start.34 = (bf16[24,1536]{1,0:T(8,128)(2,1)S(1)}, bf16[24,1536]{1,0:T(8,128)(2,1)S(1)}, u32[]{:S(2)}, u32[]{:S(2)}) collective-permute-start(bf16[24,1536]{1,0:T(8,128)(2,1)S(1)} %get-tuple-element.98), channel_id=1, source_target_pairs={{0,8},{4,12},{8,0},{12,4},{1,9},{5,13},{9,1},{13,5},{2,10},{6,14},... | collective-permute-start | bytes 221192 | tf_op jit(solution)/shard_map/ppermute | solution.py:25
  73.1 7.0 %collective-permute-start.40 = (bf16[24,1536]{1,0:T(8,128)(2,1)S(1)}, bf16[24,1536]{1,0:T(8,128)(2,1)S(1)}, u32[]{:S(2)}, u32[]{:S(2)}) collective-permute-start(bf16[24,1536]{1,0:T(8,128)(2,1)S(1)} %get-tuple-element.102), channel_id=1, source_target_pairs={{0,12},{4,8},{8,4},{12,0},{1,13},{5,9},{9,5},{13,1},{2,14},{6,10},... | collective-permute-start | bytes 221192 | tf_op jit(solution)/shard_map/ppermute | solution.py:25
  75.8 7.5 %collective-permute-start.39 = (bf16[24,1536]{1,0:T(8,128)(2,1)S(1)}, bf16[24,1536]{1,0:T(8,128)(2,1)S(1)}, u32[]{:S(2)}, u32[]{:S(2)}) collective-permute-start(bf16[24,1536]{1,0:T(8,128)(2,1)S(1)} %get-tuple-element.102), channel_id=1, source_target_pairs={{0,8},{4,12},{8,0},{12,4},{1,9},{5,13},{9,1},{13,5},{2,10},{6,14},... | collective-permute-start | bytes 221192 | tf_op jit(solution)/shard_map/ppermute | solution.py:25
  76.2 7.1 %collective-permute-start.38 = (bf16[24,1536]{1,0:T(8,128)(2,1)S(1)}, bf16[24,1536]{1,0:T(8,128)(2,1)S(1)}, u32[]{:S(2)}, u32[]{:S(2)}) collective-permute-start(bf16[24,1536]{1,0:T(8,128)(2,1)S(1)} %get-tuple-element.101.refs_4_.refs_9_), channel_id=1, source_target_pairs={{0,4},{4,0},{8,12},{12,8},{1,5},{5,1},{9,13},{13,9},{2,6},{6,2},{1... | collective-permute-start | bytes 221192 | tf_op jit(solution)/shard_map/ppermute | solution.py:25
  87.1 7.4 %collective-permute-start.48 = (bf16[2,96,512]{2,1,0:T(8,128)(2,1)S(1)}, bf16[2,96,512]{2,1,0:T(8,128)(2,1)S(1)}, u32[]{:S(2)}, u32[]{:S(2)}) collective-permute-start(bf16[2,96,512]{2,1,0:T(8,128)(2,1)S(1)} %shard_map.117.refs_9_), channel_id=1, source_target_pairs={{0,2},{1,3},{2,0},{3,1},{4,6},{5,7},{6,4},{7,5},{8,10},{9,11},{10,... | collective-permute-start | bytes 589832 | tf_op jit(solution)/shard_map/ppermute | solution.py:25
  90.3 8.4 %collective-permute-start.45 = (bf16[2,96,512]{2,1,0:T(8,128)(2,1)S(1)}, bf16[2,96,512]{2,1,0:T(8,128)(2,1)S(1)}, u32[]{:S(2)}, u32[]{:S(2)}) collective-permute-start(bf16[2,96,512]{2,1,0:T(8,128)(2,1)S(1)} %shard_map.119.refs_8_), channel_id=1, source_target_pairs={{0,2},{1,3},{2,0},{3,1},{4,6},{5,7},{6,4},{7,5},{8,10},{9,11},{10,... | collective-permute-start | bytes 589832 | tf_op jit(solution)/shard_map/ppermute | solution.py:25
  94.8 7.9 %collective-permute-start.54 = (bf16[2,96,512]{2,1,0:T(8,128)(2,1)S(1)}, bf16[2,96,512]{2,1,0:T(8,128)(2,1)S(1)}, u32[]{:S(2)}, u32[]{:S(2)}) collective-permute-start(bf16[2,96,512]{2,1,0:T(8,128)(2,1)S(1)} %shard_map.120.refs_8_.refs_0_), channel_id=1, source_target_pairs={{0,2},{1,3},{2,0},{3,1},{4,6},{5,7},{6,4},{7,5},{8,10},{9,11},{10,... | collective-permute-start | bytes 589832 | tf_op jit(solution)/shard_map/ppermute | solution.py:25
  99.5 8.4 %collective-permute-start.51 = (bf16[2,96,512]{2,1,0:T(8,128)(2,1)S(1)}, bf16[2,96,512]{2,1,0:T(8,128)(2,1)S(1)}, u32[]{:S(2)}, u32[]{:S(2)}) collective-permute-start(bf16[2,96,512]{2,1,0:T(8,128)(2,1)S(1)} %shard_map.121.refs_1_), channel_id=1, source_target_pairs={{0,2},{1,3},{2,0},{3,1},{4,6},{5,7},{6,4},{7,5},{8,10},{9,11},{10,... | collective-permute-start | bytes 589832 | tf_op jit(solution)/shard_map/ppermute | solution.py:25
  (40 other events, 154.4 us)
